TPU v7x, 32 devices: a whole 2x2x4 slice. The times are simulated.
32 devices in a mesh: dp: 8 (over z, y), fsdp: 4 (over x, core).
Axes of the slice: x: 2, y: 2, z: 4, core: 2. Of those that a mesh axis runs over, the one named last changes fastest.
Arguments:
- tokens: bfloat16 [32768, 512], P(('dp', 'fsdp')), may hold values from -6 to 6
- cotangent: bfloat16 [32768, 512], P(('dp', 'fsdp')), may hold values from -6 to 6
- row_length: int32 [8], P('dp'), may hold values from 1024 to 4096, as said below
- first_gain: bfloat16 [512], P(('dp', 'fsdp')), may hold values from 0.099609375 to 1.8984375
- first_shift: bfloat16 [512], P(('dp', 'fsdp')), may hold values from -1.75 to 1.75
- query_weight: bfloat16 [512, 512], P(('dp', 'fsdp')), may hold values from -0.375 to 0.375
- key_weight: bfloat16 [512, 512], P(('dp', 'fsdp')), may hold values from -0.375 to 0.375
- value_weight: bfloat16 [512, 512], P(('dp', 'fsdp')), may hold values from -0.25 to 0.25
- mixer_weight: bfloat16 [512, 512], P(('dp', 'fsdp')), may hold values from -6 to 6
- mixer_bias: bfloat16 [512], P(('dp', 'fsdp')), may hold values from -1.75 to 1.75
- second_gain: bfloat16 [512], P(('dp', 'fsdp')), may hold values from 0.099609375 to 1.8984375
- second_shift: bfloat16 [512], P(('dp', 'fsdp')), may hold values from -1.75 to 1.75
- inner_weight: bfloat16 [512, 2048], P(('dp', 'fsdp')), may hold values from -0.25 to 0.25
- inner_bias: bfloat16 [2048], P(('dp', 'fsdp')), may hold values from -3 to 3
- outer_weight: bfloat16 [2048, 512], P(('dp', 'fsdp')), may hold values from -0.125 to 0.125
- outer_bias: bfloat16 [512], P(('dp', 'fsdp')), may hold values from -1.75 to 1.75
Outputs:
- output: bfloat16 [32768, 512], P(('dp', 'fsdp'))
- grad_tokens: bfloat16 [32768, 512], P(('dp', 'fsdp'))
- grad_first_gain: float32 [512], P(('dp', 'fsdp'))
- grad_first_shift: float32 [512], P(('dp', 'fsdp'))
- grad_query_weight: float32 [512, 512], P(('dp', 'fsdp'))
- grad_key_weight: float32 [512, 512], P(('dp', 'fsdp'))
- grad_value_weight: float32 [512, 512], P(('dp', 'fsdp'))
- grad_mixer_weight: float32 [512, 512], P(('dp', 'fsdp'))
- grad_mixer_bias: float32 [512], P(('dp', 'fsdp'))
- grad_second_gain: float32 [512], P(('dp', 'fsdp'))
- grad_second_shift: float32 [512], P(('dp', 'fsdp'))
- grad_inner_weight: float32 [512, 2048], P(('dp', 'fsdp'))
- grad_inner_bias: float32 [2048], P(('dp', 'fsdp'))
- grad_outer_weight: float32 [2048, 512], P(('dp', 'fsdp'))
- grad_outer_bias: float32 [512], P(('dp', 'fsdp'))
Inputs may be any that keep to these rules, and one draw needn't show every extreme that they name: `row_length`: each entry is 1024 or 4096; both values occur.
All inputs are finite; a program needn't handle non-finite values.
Results may differ from a plain program's by a relative error of at most 0.018.
Values may be sent and summed in bfloat16 or wider, within the bound.
A program may use at most 192 MiB of HBM per device.

v0:
```python
import jax
import jax.numpy as jnp
from jax import lax
from jax.sharding import PartitionSpec as P

D = 512
HEADS = 8
HEAD = 64
BLOCK = 16
SHORT = 1024
LEVELS_SHORT = 6
FAR_LEVELS = 2


norm_eps = 1e-05
far_off = -1e30


def exact_gelu(values):
    return jax.nn.gelu(values, approximate=False)


def normalize(values):
    center = values - jnp.mean(values, axis=-1, keepdims=True)
    inverse = lax.rsqrt(jnp.mean(center * center, axis=-1, keepdims=True) + norm_eps)
    return (center * inverse, inverse)


def normalize_back(grad_normed, normed, inverse):
    return inverse * (
        grad_normed
        - jnp.mean(grad_normed, axis=-1, keepdims=True)
        - normed * jnp.mean(grad_normed * normed, axis=-1, keepdims=True)
    )


def spread(values, stride):
    extent = values.shape
    widened = jnp.broadcast_to(values[:, :, None], extent[:2] + (stride,) + extent[2:])
    return widened.reshape((extent[0], extent[1] * stride) + extent[2:])


def pooled(values, stride):
    extent = values.shape
    return jnp.sum(values.reshape((extent[0], extent[1] // stride, stride) + extent[2:]), axis=2)


def coarse_sets(query_rows, key_rows, value_rows):
    result_sets = [(query_rows, key_rows, value_rows)]
    sum_query = query_rows.astype(jnp.float32)
    sum_key = key_rows.astype(jnp.float32)
    sum_value = value_rows.astype(jnp.float32)
    for degree in range(1, LEVELS_SHORT + FAR_LEVELS):
        sum_query, sum_key, sum_value = (
            pooled(sum_query, 2),
            pooled(sum_key, 2),
            pooled(sum_value, 2),
        )
        stride = 2**degree
        result_sets.append(
            (
                (sum_query / stride).astype(jnp.bfloat16),
                (sum_key / stride).astype(jnp.bfloat16),
                sum_value.astype(jnp.bfloat16),
            )
        )
    return result_sets


def local_read(coarse_query, coarse_key, coarse_value, degree):
    blocks = coarse_query.shape[0] * coarse_query.shape[1] // BLOCK
    blocked = (blocks, BLOCK, HEADS, HEAD)
    paired = (blocks // 2, 2, BLOCK, HEADS, HEAD)
    partner_keys = coarse_key.reshape(paired)[:, ::-1].reshape(blocked)
    partner_values = coarse_value.reshape(paired)[:, ::-1].reshape(blocked)
    if degree == 0:
        read_keys = jnp.concatenate((coarse_key.reshape(blocked), partner_keys), axis=1)
        read_values = jnp.concatenate((coarse_value.reshape(blocked), partner_values), axis=1)
    else:
        read_keys, read_values = (partner_keys, partner_values)
    return (coarse_query.reshape(blocked), read_keys, read_values)


def local_return(grad_read, degree, pieces, amount):
    blocks = pieces * amount // BLOCK
    paired = (blocks // 2, 2, BLOCK, HEADS, HEAD)
    partner_part = grad_read[:, BLOCK:] if degree == 0 else grad_read
    returned = partner_part.reshape(paired)[:, ::-1].reshape(blocks, BLOCK, HEADS, HEAD)
    if degree == 0:
        returned = returned + grad_read[:, :BLOCK]
    return returned.reshape(pieces, amount, HEADS, HEAD)


def far_piece(gathered, step_far, fsdp_index, part_count):
    pieces = gathered.shape[0]
    offset = sum((BLOCK >> earlier for earlier in range(step_far)))
    amount = BLOCK >> step_far
    whole_set = gathered.reshape(pieces, part_count, -1, HEADS, HEAD)[
        :, :, offset : offset + amount
    ]
    first_dev = (fsdp_index >> step_far ^ 1) << step_far
    chosen = lax.dynamic_slice_in_dim(whole_set, first_dev, 2**step_far, axis=1)
    return chosen.reshape(pieces, BLOCK, HEADS, HEAD)


def far_return(grad_read, step_far, fsdp_index, part_count):
    pieces = grad_read.shape[0]
    amount = BLOCK >> step_far
    placed = jnp.zeros((pieces, part_count, amount, HEADS * HEAD), jnp.float32)
    first_dev = (fsdp_index >> step_far ^ 1) << step_far
    return lax.dynamic_update_slice_in_dim(
        placed, grad_read.reshape(pieces, 2**step_far, amount, HEADS * HEAD), first_dev, axis=1
    )


def level_scores(block_query, read_keys):
    scores = jnp.einsum(
        "bqhe,bkhe->bhqk", block_query, read_keys, preferred_element_type=jnp.float32
    ) * HEAD ** (-0.5)
    maxima = jnp.max(scores, axis=-1)
    return (jnp.exp(scores - maxima[..., None]), maxima)


def level_forward(block_query, read_keys, read_values, stride, pieces):
    expscore, maxima = level_scores(block_query, read_keys)
    totals = stride * jnp.sum(expscore, axis=-1)
    numerator = jnp.einsum(
        "bhqk,bkhe->bqhe",
        expscore.astype(jnp.bfloat16),
        read_values,
        preferred_element_type=jnp.float32,
    )
    maxima = jnp.swapaxes(maxima, 1, 2).reshape(pieces, -1, HEADS)
    totals = jnp.swapaxes(totals, 1, 2).reshape(pieces, -1, HEADS)
    numerator = numerator.reshape(pieces, -1, HEADS, HEAD)
    return (maxima, totals, numerator)


def merge_level(running, triple, active):
    peak_val, denominator, num_sum = running
    maxima, totals, numerator = triple
    maxima = jnp.where(active, maxima, far_off)
    newest = jnp.maximum(peak_val, maxima)
    old_factor = jnp.exp(peak_val - newest)
    new_factor = jnp.exp(maxima - newest)
    return (
        newest,
        old_factor * denominator + new_factor * totals,
        old_factor[..., None] * num_sum + new_factor[..., None] * numerator,
    )


def level_backward(
    block_query, read_keys, read_values, stride, pieces, active, pyr_grad, pyr_inner
):
    expscore, maxima = level_scores(block_query, read_keys)
    peak_val = jnp.swapaxes(maxima, 1, 2).reshape(pieces, -1, HEADS)
    scale = jnp.exp(jnp.where(active, peak_val, far_off))
    blocks = block_query.shape[0]
    grad_numer = (scale[..., None] * pyr_grad).astype(jnp.bfloat16).reshape(blocks, -1, HEADS, HEAD)
    grad_total = jnp.swapaxes((scale * pyr_inner).reshape(blocks, -1, HEADS), 1, 2)
    grad_exp = jnp.einsum(
        "bqhe,bkhe->bhqk", grad_numer, read_values, preferred_element_type=jnp.float32
    )
    grad_score = (expscore * (grad_exp - stride * grad_total[..., None])).astype(jnp.bfloat16)
    grad_query = jnp.einsum(
        "bhqk,bkhe->bqhe", grad_score, read_keys, preferred_element_type=jnp.float32
    ) * HEAD ** (-0.5)
    grad_key = jnp.einsum(
        "bhqk,bqhe->bkhe", grad_score, block_query, preferred_element_type=jnp.float32
    ) * HEAD ** (-0.5)
    grad_value = jnp.einsum(
        "bhqk,bqhe->bkhe",
        expscore.astype(jnp.bfloat16),
        grad_numer,
        preferred_element_type=jnp.float32,
    )
    return (grad_query.reshape(pieces, -1, HEADS, HEAD), grad_key, grad_value)


def attention_forward(query_rows, key_rows, value_rows, active, fsdp_index, part_count):
    pieces = query_rows.shape[0]
    result_sets = coarse_sets(query_rows, key_rows, value_rows)
    far_keys = jnp.concatenate(
        [result_sets[LEVELS_SHORT + step_far][1] for step_far in range(FAR_LEVELS)], axis=1
    )
    far_values = jnp.concatenate(
        [result_sets[LEVELS_SHORT + step_far][2] for step_far in range(FAR_LEVELS)], axis=1
    )
    all_keys, all_values = (
        lax.all_gather(far_keys, "fsdp", axis=1, tiled=True),
        lax.all_gather(far_values, "fsdp", axis=1, tiled=True),
    )
    running = None
    for degree in reversed(range(LEVELS_SHORT + FAR_LEVELS)):
        stride = 2**degree
        if degree >= LEVELS_SHORT:
            step_far = degree - LEVELS_SHORT
            block_query = result_sets[degree][0]
            read_keys = far_piece(all_keys, step_far, fsdp_index, part_count)
            read_values = far_piece(all_values, step_far, fsdp_index, part_count)
            triple = level_forward(block_query, read_keys, read_values, stride, pieces)
            flag = active
        else:
            triple = level_forward(*local_read(*result_sets[degree], degree), stride, pieces)
            flag = True
        if running is None:
            running = (jnp.where(flag, triple[0], far_off), triple[1], triple[2])
        else:
            running = merge_level(tuple((spread(member, 2) for member in running)), triple, flag)
    peak_val, denominator, num_sum = running
    mixed = num_sum / denominator[..., None]
    return (mixed, peak_val + jnp.log(denominator), all_keys, all_values)


def attention_backward(
    query_rows,
    key_rows,
    value_rows,
    all_keys,
    all_values,
    active,
    fsdp_index,
    part_count,
    grad_mixed,
    mixed,
    log_total,
):
    pieces = query_rows.shape[0]
    inner_dot = jnp.sum(grad_mixed * mixed, axis=-1)
    result_sets = coarse_sets(query_rows, key_rows, value_rows)
    token_weight = jnp.exp(-log_total)
    pyr_grad = [token_weight[..., None] * grad_mixed.astype(jnp.float32)]
    pyr_inner = [token_weight * inner_dot]
    for degree in range(1, LEVELS_SHORT + FAR_LEVELS):
        pyr_grad.append(pooled(pyr_grad[-1], 2))
        pyr_inner.append(pooled(pyr_inner[-1], 2))
    far_queries = []
    far_grad_keys = []
    far_grad_values = []
    for step_far in range(FAR_LEVELS):
        degree = LEVELS_SHORT + step_far
        stride = 2**degree
        block_query = result_sets[degree][0]
        read_keys = far_piece(all_keys, step_far, fsdp_index, part_count)
        read_values = far_piece(all_values, step_far, fsdp_index, part_count)
        grad_query, grad_key, grad_value = level_backward(
            block_query,
            read_keys,
            read_values,
            stride,
            pieces,
            active,
            pyr_grad[degree],
            pyr_inner[degree],
        )
        far_queries.append(grad_query)
        far_grad_keys.append(far_return(grad_key, step_far, fsdp_index, part_count))
        far_grad_values.append(far_return(grad_value, step_far, fsdp_index, part_count))
    send_keys = jnp.concatenate(far_grad_keys, axis=2).reshape(pieces, -1, HEADS * HEAD)
    send_values = jnp.concatenate(far_grad_values, axis=2).reshape(pieces, -1, HEADS * HEAD)
    own_keys, own_values = (
        lax.psum_scatter(
            send_keys.astype(jnp.bfloat16), "fsdp", scatter_dimension=1, tiled=True
        ).astype(jnp.float32),
        lax.psum_scatter(
            send_values.astype(jnp.bfloat16), "fsdp", scatter_dimension=1, tiled=True
        ).astype(jnp.float32),
    )
    far_key_parts = []
    far_value_parts = []
    offset = 0
    for step_far in range(FAR_LEVELS):
        amount = BLOCK >> step_far
        far_key_parts.append(
            own_keys[:, offset : offset + amount].reshape(pieces, amount, HEADS, HEAD)
        )
        far_value_parts.append(
            own_values[:, offset : offset + amount].reshape(pieces, amount, HEADS, HEAD)
        )
        offset = offset + amount
    running = None
    for degree in reversed(range(LEVELS_SHORT + FAR_LEVELS)):
        stride = 2**degree
        if degree >= LEVELS_SHORT:
            step_far = degree - LEVELS_SHORT
            part_query = far_queries[step_far]
            part_key = far_key_parts[step_far]
            part_value = far_value_parts[step_far]
        else:
            amount = SHORT // stride
            block_query, read_keys, read_values = local_read(*result_sets[degree], degree)
            part_query, grad_key, grad_value = level_backward(
                block_query,
                read_keys,
                read_values,
                stride,
                pieces,
                True,
                pyr_grad[degree],
                pyr_inner[degree],
            )
            part_key = local_return(grad_key, degree, pieces, amount)
            part_value = local_return(grad_value, degree, pieces, amount)
        fresh = (part_query / stride, part_key / stride, part_value)
        if running is None:
            running = fresh
        else:
            running = tuple((spread(member, 2) + addend for member, addend in zip(running, fresh)))
    return running


def gather_mixer(
    first_gain, first_shift, query_weight, key_weight, value_weight, mixer_weight, mixer_bias
):
    return (
        lax.all_gather(first_gain, ("dp", "fsdp"), axis=0, tiled=True),
        lax.all_gather(first_shift, ("dp", "fsdp"), axis=0, tiled=True),
        lax.all_gather(query_weight, ("dp", "fsdp"), axis=0, tiled=True),
        lax.all_gather(key_weight, ("dp", "fsdp"), axis=0, tiled=True),
        lax.all_gather(value_weight, ("dp", "fsdp"), axis=0, tiled=True),
        lax.all_gather(mixer_weight, ("dp", "fsdp"), axis=0, tiled=True),
        lax.all_gather(mixer_bias, ("dp", "fsdp"), axis=0, tiled=True),
    )


def gather_feed(second_gain, second_shift, inner_weight, inner_bias, outer_weight, outer_bias):
    return (
        lax.all_gather(second_gain, ("dp", "fsdp"), axis=0, tiled=True),
        lax.all_gather(second_shift, ("dp", "fsdp"), axis=0, tiled=True),
        lax.all_gather(inner_weight, ("dp", "fsdp"), axis=0, tiled=True),
        lax.all_gather(inner_bias, ("dp", "fsdp"), axis=0, tiled=True),
        lax.all_gather(outer_weight, ("dp", "fsdp"), axis=0, tiled=True),
        lax.all_gather(outer_bias, ("dp", "fsdp"), axis=0, tiled=True),
    )


def on_device(
    tokens,
    cotangent,
    row_length,
    first_gain,
    first_shift,
    query_weight,
    key_weight,
    value_weight,
    mixer_weight,
    mixer_bias,
    second_gain,
    second_shift,
    inner_weight,
    inner_bias,
    outer_weight,
    outer_bias,
):
    active = row_length[0] > SHORT
    fsdp_index = lax.axis_index("fsdp")
    part_count = lax.axis_size("fsdp")
    pieces = tokens.shape[0] // SHORT
    mixer_params = gather_mixer(
        first_gain, first_shift, query_weight, key_weight, value_weight, mixer_weight, mixer_bias
    )
    gain_one, shift_one, weight_query, weight_key, weight_value, weight_mix, bias_mix = mixer_params
    resid_in = tokens.astype(jnp.float32)
    normed_one, inverse_one = normalize(resid_in)
    normal_one = (normed_one * gain_one.astype(jnp.float32) + shift_one.astype(jnp.float32)).astype(
        jnp.bfloat16
    )
    weight_qkv = jnp.concatenate((weight_query, weight_key, weight_value), axis=1)
    projected = jnp.dot(normal_one, weight_qkv, preferred_element_type=jnp.float32).astype(
        jnp.bfloat16
    )
    query_rows = projected[:, :D].reshape(pieces, SHORT, HEADS, HEAD)
    key_rows = projected[:, D : 2 * D].reshape(pieces, SHORT, HEADS, HEAD)
    value_rows = projected[:, 2 * D :].reshape(pieces, SHORT, HEADS, HEAD)
    mixed, log_total, all_keys, all_values = attention_forward(
        query_rows, key_rows, value_rows, active, fsdp_index, part_count
    )
    mixed_low = mixed.reshape(-1, D).astype(jnp.bfloat16)
    resid_mid = (
        resid_in
        + jnp.dot(mixed_low, weight_mix, preferred_element_type=jnp.float32)
        + bias_mix.astype(jnp.float32)
    )
    feed_params = gather_feed(
        second_gain, second_shift, inner_weight, inner_bias, outer_weight, outer_bias
    )
    gain_two, shift_two, weight_in, bias_in, weight_out, bias_out = feed_params
    normed_two, inverse_two = normalize(resid_mid)
    normal_two = (normed_two * gain_two.astype(jnp.float32) + shift_two.astype(jnp.float32)).astype(
        jnp.bfloat16
    )
    pre_act = jnp.dot(normal_two, weight_in, preferred_element_type=jnp.float32) + bias_in.astype(
        jnp.float32
    )
    activated, gelu_pull = jax.vjp(exact_gelu, pre_act)
    hidden = activated.astype(jnp.bfloat16)
    output = (
        resid_mid
        + jnp.dot(hidden, weight_out, preferred_element_type=jnp.float32)
        + bias_out.astype(jnp.float32)
    ).astype(jnp.bfloat16)
    back_feed = gather_feed(
        second_gain, second_shift, inner_weight, inner_bias, outer_weight, outer_bias
    )
    gain_two, shift_two, weight_in, bias_in, weight_out, bias_out = back_feed
    grad_out = cotangent.astype(jnp.float32)
    grad_bias_out = jnp.sum(grad_out, axis=0)
    grad_weight_out = jnp.einsum("tf,td->fd", hidden, cotangent, preferred_element_type=jnp.float32)
    grad_hidden = jnp.einsum("td,fd->tf", cotangent, weight_out, preferred_element_type=jnp.float32)
    grad_pre = gelu_pull(grad_hidden)[0].astype(jnp.bfloat16)
    grad_bias_in = jnp.sum(grad_pre.astype(jnp.float32), axis=0)
    grad_weight_in = jnp.einsum(
        "td,tf->df", normal_two, grad_pre, preferred_element_type=jnp.float32
    )
    grad_normal_two = jnp.einsum(
        "tf,df->td", grad_pre, weight_in, preferred_element_type=jnp.float32
    )
    grad_gain_two = jnp.sum(grad_normal_two * normed_two, axis=0)
    grad_shift_two = jnp.sum(grad_normal_two, axis=0)
    grad_mid = grad_out + normalize_back(
        grad_normal_two * gain_two.astype(jnp.float32), normed_two, inverse_two
    )
    feed_sums = (
        lax.psum_scatter(grad_gain_two, ("dp", "fsdp"), scatter_dimension=0, tiled=True),
        lax.psum_scatter(grad_shift_two, ("dp", "fsdp"), scatter_dimension=0, tiled=True),
        lax.psum_scatter(grad_weight_in, ("dp", "fsdp"), scatter_dimension=0, tiled=True),
        lax.psum_scatter(grad_bias_in, ("dp", "fsdp"), scatter_dimension=0, tiled=True),
        lax.psum_scatter(grad_weight_out, ("dp", "fsdp"), scatter_dimension=0, tiled=True),
        lax.psum_scatter(grad_bias_out, ("dp", "fsdp"), scatter_dimension=0, tiled=True),
    )
    back_mixer = gather_mixer(
        first_gain, first_shift, query_weight, key_weight, value_weight, mixer_weight, mixer_bias
    )
    gain_one, shift_one, weight_query, weight_key, weight_value, weight_mix, bias_mix = back_mixer
    grad_mix = grad_mid.astype(jnp.bfloat16)
    grad_bias_mix = jnp.sum(grad_mix.astype(jnp.float32), axis=0)
    grad_weight_mix = jnp.einsum(
        "td,te->de", mixed_low, grad_mix, preferred_element_type=jnp.float32
    )
    grad_mixed = jnp.einsum(
        "te,de->td", grad_mix, weight_mix, preferred_element_type=jnp.float32
    ).astype(jnp.bfloat16)
    grad_queries, grad_keys, grad_values = attention_backward(
        query_rows,
        key_rows,
        value_rows,
        all_keys,
        all_values,
        active,
        fsdp_index,
        part_count,
        grad_mixed.reshape(pieces, SHORT, HEADS, HEAD),
        mixed,
        log_total,
    )
    grad_proj = jnp.concatenate(
        (grad_queries.reshape(-1, D), grad_keys.reshape(-1, D), grad_values.reshape(-1, D)), axis=1
    ).astype(jnp.bfloat16)
    back_qkv = jnp.concatenate((weight_query, weight_key, weight_value), axis=1)
    grad_weight_qkv = jnp.einsum(
        "td,tf->df", normal_one, grad_proj, preferred_element_type=jnp.float32
    )
    grad_normal_one = jnp.einsum(
        "tf,df->td", grad_proj, back_qkv, preferred_element_type=jnp.float32
    )
    grad_gain_one = jnp.sum(grad_normal_one * normed_one, axis=0)
    grad_shift_one = jnp.sum(grad_normal_one, axis=0)
    grad_input = grad_mid + normalize_back(
        grad_normal_one * gain_one.astype(jnp.float32), normed_one, inverse_one
    )
    grad_weight_query = grad_weight_qkv[:, :D]
    grad_weight_key = grad_weight_qkv[:, D : 2 * D]
    grad_weight_value = grad_weight_qkv[:, 2 * D :]
    mixer_sums = (
        lax.psum_scatter(grad_gain_one, ("dp", "fsdp"), scatter_dimension=0, tiled=True),
        lax.psum_scatter(grad_shift_one, ("dp", "fsdp"), scatter_dimension=0, tiled=True),
        lax.psum_scatter(grad_weight_query, ("dp", "fsdp"), scatter_dimension=0, tiled=True),
        lax.psum_scatter(grad_weight_key, ("dp", "fsdp"), scatter_dimension=0, tiled=True),
        lax.psum_scatter(grad_weight_value, ("dp", "fsdp"), scatter_dimension=0, tiled=True),
        lax.psum_scatter(grad_weight_mix, ("dp", "fsdp"), scatter_dimension=0, tiled=True),
        lax.psum_scatter(grad_bias_mix, ("dp", "fsdp"), scatter_dimension=0, tiled=True),
    )
    totals_out = tuple(mixer_sums) + tuple(feed_sums)
    return (output, grad_input.astype(jnp.bfloat16)) + totals_out


def solution(mesh):
    in_specs = (
        P(("dp", "fsdp"), None),
        P(("dp", "fsdp"), None),
        P("dp"),
        P(("dp", "fsdp")),
        P(("dp", "fsdp")),
        P(("dp", "fsdp"), None),
        P(("dp", "fsdp"), None),
        P(("dp", "fsdp"), None),
        P(("dp", "fsdp"), None),
        P(("dp", "fsdp")),
        P(("dp", "fsdp")),
        P(("dp", "fsdp")),
        P(("dp", "fsdp"), None),
        P(("dp", "fsdp")),
        P(("dp", "fsdp"), None),
        P(("dp", "fsdp")),
    )
    out_specs = (
        P(("dp", "fsdp"), None),
        P(("dp", "fsdp"), None),
        P(("dp", "fsdp")),
        P(("dp", "fsdp")),
        P(("dp", "fsdp"), None),
        P(("dp", "fsdp"), None),
        P(("dp", "fsdp"), None),
        P(("dp", "fsdp"), None),
        P(("dp", "fsdp")),
        P(("dp", "fsdp")),
        P(("dp", "fsdp")),
        P(("dp", "fsdp"), None),
        P(("dp", "fsdp")),
        P(("dp", "fsdp"), None),
        P(("dp", "fsdp")),
    )
    return jax.shard_map(
        on_device, mesh=mesh, in_specs=in_specs, out_specs=out_specs, check_vma=False
    )
```

profile of v0, /device:TPU:0, one launch (start us, length us, event | category | flops | bytes accessed | tf_op | source)
XLA Modules:
  0.0 1580.7 jit_solution(6896361434456298406)
XLA Ops:
  14.7 42.2 %all-reduce.15 = (bf16[512]{0:T(512)(128)(2,1)S(1)}, bf16[512]{0:T(512)(128)(2,1)S(1)}, bf16[512]{0:T(512)(128)(2,1)}, bf16[512]{0:T(512)(128)(2,1)}, bf16[512]{...) all-reduce(bf16[512]{0:T(512)(128)(2,1)S(1)} %dynamic-update-slice., ...), channel_id=1, replica_groups=mesh['dp'=8,'fsdp'=4] {'dp','fsdp'}, use_global_device_ids=true, to_apply=%add.1 | all-reduce | flops 5120 | bytes 20480
  59.0 42.5 %all_gather.55 = bf16[512,512]{1,0:T(8,128)(2,1)S(1)} all-gather(bf16[16,512]{1,0:T(8,128)(2,1)S(1)} %copy-done.178), channel_id=1, replica_groups=mesh['dp'=8,'fsdp'=4] {'dp','fsdp'}, dimensions={0}, use_global_device_ids=true | all-gather | bytes 540672 | tf_op jit(solution)/shard_map/all_gather | solution.py:319
  101.5 38.4 %all_gather.56 = bf16[512,512]{1,0:T(8,128)(2,1)S(1)} all-gather(bf16[16,512]{1,0:T(8,128)(2,1)S(1)} %copy-done.179), channel_id=1, replica_groups=mesh['dp'=8,'fsdp'=4] {'dp','fsdp'}, dimensions={0}, use_global_device_ids=true | all-gather | bytes 540672 | tf_op jit(solution)/shard_map/all_gather | solution.py:320
  139.9 39.4 %all_gather.57 = bf16[512,512]{1,0:T(8,128)(2,1)S(1)} all-gather(bf16[16,512]{1,0:T(8,128)(2,1)S(1)} %copy-done.180), channel_id=1, replica_groups=mesh['dp'=8,'fsdp'=4] {'dp','fsdp'}, dimensions={0}, use_global_device_ids=true | all-gather | bytes 540672 | tf_op jit(solution)/shard_map/all_gather | solution.py:321
  203.7 5.6 all_gather.58
  210.6 5.8 all_gather.59
  269.5 6.5 multiply_reduce_fusion.1
  393.7 4.8 reshape.2700
  402.8 41.0 %all_gather.60 = bf16[512,512]{1,0:T(8,128)(2,1)} all-gather(bf16[16,512]{1,0:T(8,128)(2,1)} %param.24), channel_id=1, replica_groups=mesh['dp'=8,'fsdp'=4] {'dp','fsdp'}, dimensions={0}, use_global_device_ids=true | all-gather | bytes 540672 | tf_op jit(solution)/shard_map/all_gather | solution.py:322
  471.8 24.7 %multiply_convert_fusion = (bf16[1024,2048]{1,0:T(8,128)(2,1)}, f32[1024,2048]{1,0:T(8,128)}, f32[1024,2048]{1,0:T(8,128)}) fusion(f32[2048]{0:T(1024)} %convert_element_type.587, bf16[512,2048]{1,0:T(8,128)(2,1)} %all-gather.3.cloned.1.call-done, f32[1024,512]{0,1:T(8,128)} %copy-done.13, f32[512]{0:T(512)} %convert_element_type.585, ...), kind=kOutput, calls=%fused_computation.5 | convolution fusion | flops 2288517120 | bytes 25186304 | tf_op jit(solution)/shard_map/dot_general | solution.py:393
  496.5 9.8 convert_reduce_fusion
  538.6 9.6 fusion.9
  554.8 5.1 multiply_convert_fusion.2
  629.7 5.8 convolution_bitcast_fusion
  644.0 6.1 copy.1408
  670.2 4.8 broadcast_in_dim.524
  684.4 6.5 slice_add_fusion.1
  703.8 6.6 slice_add_fusion
  714.5 6.2 copy.1424
  733.9 4.8 reshape.2743
  774.5 4.9 broadcast_in_dim.540
  788.8 4.8 broadcast_in_dim.555
  803.7 6.6 fusion.214
  810.4 6.9 fusion.232
  817.9 6.2 add_convert_fusion.4
  835.3 37.3 %all-reduce.14 = (f32[512]{0:T(512)S(1)}, f32[512]{0:T(512)S(1)}, f32[512]{0:T(512)S(1)}, f32[512]{0:T(512)S(1)}, f32[512]{0:T(512)S(1)}, /*index=5*/f32[2048]{0:T(1024)S(1)}, f32[512]{0:T(512)S(1)}) all-reduce(f32[512]{0:T(512)S(1)} %get-tuple-element.137, ...), channel_id=4, replica_groups=mesh['dp'=8,'fsdp'=4] {'dp','fsdp'}, use_global_device_ids=true, to_apply=%region_63.64.clone | all-reduce | flops 5120 | bytes 40960
  882.2 11.3 reduce-scatter.19.cloned.1.call-done
  893.5 133.6 %reduce-scatter.13.cloned.1.call-done = f32[16,512]{1,0:T(8,128)} async-done(((f32[512,512]{1,0:T(8,128)}), f32[16,512]{1,0:T(8,128)}) %reduce-scatter.13.cloned.1.call-update) | async-done | bytes 32784 | tf_op jit(solution)/shard_map/reduce_scatter | solution.py:478
  1027.0 133.6 %reduce-scatter.15.cloned.1.call-done = f32[16,512]{1,0:T(8,128)} async-done(((f32[512,512]{1,0:T(8,128)}), f32[16,512]{1,0:T(8,128)}) %reduce-scatter.15.cloned.1.call-update) | async-done | bytes 32784 | tf_op jit(solution)/shard_map/reduce_scatter | solution.py:479
  1160.6 133.7 %reduce-scatter.17.cloned.1.call-done = f32[16,512]{1,0:T(8,128)} async-done(((f32[512,512]{1,0:T(8,128)}), f32[16,512]{1,0:T(8,128)}) %reduce-scatter.17.cloned.1.call-update) | async-done | bytes 32784 | tf_op jit(solution)/shard_map/reduce_scatter | solution.py:480
  1294.3 139.7 %reduce-scatter.21.cloned.1.call-done = f32[16,2048]{1,0:T(8,128)} async-done(((f32[512,2048]{1,0:T(8,128)}), f32[16,2048]{1,0:T(8,128)}) %reduce-scatter.21.cloned.1.call-update) | async-done | bytes 131088 | tf_op jit(solution)/shard_map/reduce_scatter | solution.py:427
  1434.0 139.6 %reduce-scatter.23.cloned.1.call-done = f32[64,512]{1,0:T(8,128)} async-done(((f32[2048,512]{1,0:T(8,128)}), f32[64,512]{1,0:T(8,128)}) %reduce-scatter.23.cloned.1.call-update) | async-done | bytes 131088 | tf_op jit(solution)/shard_map/reduce_scatter | solution.py:429
  (866 shorter events, 488.5 us)
Async XLA Ops:
  7.2 464.6 %all-gather.3.cloned.1.call-start = ((), (), s32[]{:S(2)}) async-start(), calls=%async_computation.8 | async-start | bytes 2162688 | tf_op jit(solution)/shard_map/all_gather | solution.py:331
  7.9 488.5 %all-gather.5.cloned.1.call-start = ((), (), s32[]{:S(2)}) async-start(), calls=%async_computation.9 | async-start | bytes 2162688 | tf_op jit(solution)/shard_map/all_gather | solution.py:333
  8.7 754.0 %reduce-scatter.9.cloned.1.call-start = ((), (), s32[]{:S(2)}) async-start(), calls=%async_computation.10 | async-start | bytes 122880 | tf_op jit(solution)/shard_map/reduce_scatter | solution.py:263
  56.9 122.6 %copy-start.174 = (f32[512]{0:T(512)}, f32[512]{0:T(512)S(1)}, u32[]{:S(2)}) copy-start(f32[512]{0:T(512)S(1)} %convert_element_type.524) | copy-start | bytes 6148
  56.9 122.6 %copy-start.191 = (f32[512]{0:T(512)}, f32[512]{0:T(512)S(1)}, u32[]{:S(2)}) copy-start(f32[512]{0:T(512)S(1)} %convert_element_type.525) | copy-start | bytes 6148
  58.4 395.0 %copy-start.6 = (bf16[1024,512]{0,1:T(8,128)(2,1)}, bf16[1024,512]{0,1:T(8,128)(2,1)S(1)}, u32[]{:S(2)}) copy-start(bf16[1024,512]{0,1:T(8,128)(2,1)S(1)} %copy.1219) | copy-start | bytes 3145732
  58.4 43.1 %copy-start.179 = (bf16[16,512]{1,0:T(8,128)(2,1)S(1)}, bf16[16,512]{1,0:T(8,128)(2,1)}, u32[]{:S(2)}) copy-start(bf16[16,512]{1,0:T(8,128)(2,1)} %param.22) | copy-start | bytes 49156
  58.4 81.5 %copy-start.180 = (bf16[16,512]{1,0:T(8,128)(2,1)S(1)}, bf16[16,512]{1,0:T(8,128)(2,1)}, u32[]{:S(2)}) copy-start(bf16[16,512]{1,0:T(8,128)(2,1)} %param.23) | copy-start | bytes 49156
  58.6 120.8 %copy-start.167 = (f32[1024]{0:T(1024)}, f32[1024]{0:T(1024)S(1)}, u32[]{:S(2)}) copy-start(f32[1024]{0:T(1024)S(1)} %broadcast_multiply_fusion.5) | copy-start | bytes 12292
  59.0 120.5 %copy-start.171 = (f32[1024]{0:T(1024)}, f32[1024]{0:T(1024)S(1)}, u32[]{:S(2)}) copy-start(f32[1024]{0:T(1024)S(1)} %add_rsqrt_fusion.1) | copy-start | bytes 12292
  202.8 13.6 copy-start.23
  203.0 13.4 copy-start.48
  282.0 10.5 copy-start.120
  282.8 9.8 copy-start.99
  284.6 10.2 copy-start.106
  456.1 9.4 copy-start.54
  471.8 24.7 %copy-start.109 = (bf16[1024,512]{1,0:T(8,128)(2,1)S(1)}, bf16[1024,512]{1,0:T(8,128)(2,1)}, u32[]{:S(2)}) copy-start(bf16[1024,512]{1,0:T(8,128)(2,1)} %param.17) | copy-start | bytes 3145732
  496.4 9.8 copy-start.198
  581.5 18.9 %copy-start.20 = (f32[8,8,16,16]{2,3,1,0:T(8,128)S(1)}, f32[8,8,16,16]{2,3,1,0:T(8,128)}, u32[]{:S(2)}) copy-start(f32[8,8,16,16]{2,3,1,0:T(8,128)} %copy-done.19) | copy-start | bytes 196612
  581.7 17.6 %copy-start.52 = (f32[128,8,64]{2,1,0:T(8,128)S(1)}, f32[128,8,64]{2,1,0:T(8,128)}, u32[]{:S(2)}) copy-start(f32[128,8,64]{2,1,0:T(8,128)} %copy-done.51) | copy-start | bytes 786436
  650.1 10.4 copy-start.127
  650.1 11.1 copy-start.95
  650.1 11.9 copy-start.70
  653.8 12.6 copy-start.63
  691.9 87.6 %reduce-scatter.11.cloned.1.call-start = ((), (), s32[]{:S(2)}) async-start(), calls=%async_computation.11 | async-start | bytes 122880 | tf_op jit(solution)/shard_map/reduce_scatter | solution.py:266
  714.5 179.0 %reduce-scatter.19.cloned.1.call-start = ((), (), s32[]{:S(2)}) async-start(), calls=%async_computation.15 | async-start | bytes 1081344 | tf_op jit(solution)/shard_map/reduce_scatter | solution.py:481
  761.0 266.1 %reduce-scatter.13.cloned.1.call-start = ((), (), s32[]{:S(2)}) async-start(), calls=%async_computation.12 | async-start | bytes 1081344 | tf_op jit(solution)/shard_map/reduce_scatter | solution.py:478
  802.1 358.5 %reduce-scatter.15.cloned.1.call-start = ((), (), s32[]{:S(2)}) async-start(), calls=%async_computation.13 | async-start | bytes 1081344 | tf_op jit(solution)/shard_map/reduce_scatter | solution.py:479
  802.8 491.5 %reduce-scatter.17.cloned.1.call-start = ((), (), s32[]{:S(2)}) async-start(), calls=%async_computation.14 | async-start | bytes 1081344 | tf_op jit(solution)/shard_map/reduce_scatter | solution.py:480
  803.6 630.4 %reduce-scatter.21.cloned.1.call-start = ((), (), s32[]{:S(2)}) async-start(), calls=%async_computation.16 | async-start | bytes 4325376 | tf_op jit(solution)/shard_map/reduce_scatter | solution.py:427
  810.3 763.3 %reduce-scatter.23.cloned.1.call-start = ((), (), s32[]{:S(2)}) async-start(), calls=%async_computation.17 | async-start | bytes 4325376 | tf_op jit(solution)/shard_map/reduce_scatter | solution.py:429
  832.7 43.4 %copy-start.5 = (f32[1024,512]{0,1:T(8,128)S(1)}, f32[1024,512]{0,1:T(8,128)}, u32[]{:S(2)}) copy-start(f32[1024,512]{0,1:T(8,128)} %copy-done.3) | copy-start | bytes 6291460
  (178 other events, 563.7 us)
Sparse Core Ops, SparseCore 0:
  10.9 59.3 all-gather.2
  73.1 55.7 all-gather.4
  692.0 16.9 reduce-scatter.8
  714.6 16.9 reduce-scatter.10
  761.1 132.3 reduce-scatter.18
  896.2 130.7 reduce-scatter.12
  1029.9 130.7 reduce-scatter.14
  1163.5 130.7 reduce-scatter.16
  1297.1 136.8 reduce-scatter.20
  1436.7 136.8 reduce-scatter.22
where the time goes:
time: 1600 us; the launch traced here: 1580 us
  waiting for transfers between devices  694 us (43%)
  local copies, waits for them, and re-layouts  332 us (21%)
  blocking collectives  252 us (16%)
  matrix products  144 us (9%)
  other arithmetic  140 us (9%)
  between operations  17.9 us (1%)
    reduce_scatter x1, waiting for transfers between devices, on_device(): lax.psum_scatter(grad_weight_in, ('dp', 'fsdp'), scatter_dimension=0, til...  140 us
    reduce_scatter x1, waiting for transfers between devices, on_device(): lax.psum_scatter(grad_weight_out, ('dp', 'fsdp'), scatter_dimension=0, ti...  140 us
    reduce_scatter x1, waiting for transfers between devices, on_device(): lax.psum_scatter(grad_weight_value, ('dp', 'fsdp'), scatter_dimension=0,...  134 us
    reduce_scatter x1, waiting for transfers between devices, on_device(): lax.psum_scatter(grad_weight_query, ('dp', 'fsdp'), scatter_dimension=0,...  134 us
    reduce_scatter x1, waiting for transfers between devices, on_device(): lax.psum_scatter(grad_weight_key, ('dp', 'fsdp'), scatter_dimension=0, ti...  134 us
    unnamed x2, blocking collectives  79.5 us
    broadcast_in_dim x44, local copies, waits for them, and re-layouts, spread(): jnp.broadcast_to(values[:, :, None], extent[:2] + (stride,) + extent[2:])  48.2 us
    unnamed x430, local copies, waits for them, and re-layouts  45.5 us
  transfers between devices with their start and end apart: 10, of which 6 were waited for; matrix products, arithmetic and copies ran while one was open for 26% of the time, Pallas kernels for 0%

commit v1 on v0

v1 whole, which is shorter than its diff:
```python
import functools
import math
import types

import jax
import jax.numpy as jnp
import numpy as np
from jax import lax
from jax.experimental import pallas as pl
from jax.experimental.pallas import tpu as pltpu
from jax.sharding import PartitionSpec as P

D = 512
HEADS = 8
HEAD = 64
BLOCK = 16
SHORT = 1024
LEVELS = 8
TILE = 128
CHUNK = 256
STACK = 2 * SHORT
WIDTH = 3 * D
SMALL = 128
FEED_STEPS = 2
AXES = ("dp", "fsdp")
MESH = pl.DeviceIdType.MESH
SLOTS = (4, 2, 2, 2)

norm_eps = 1e-05
far_off = -1e30
f32 = jnp.float32
bf16 = jnp.bfloat16

FIRST = [STACK - (STACK >> level) for level in range(LEVELS + 1)]
LOW_TOP = 4


def member_matrix():
    token = np.arange(SHORT)
    rows = []
    for level, span in ((1, 256), (2, 512), (3, 1024)):
        rows.append((token[None] % span) >> level == np.arange(TILE)[:, None])
    for level in range(LOW_TOP, LEVELS):
        rows.append(token[None] >> level == np.arange(SHORT >> level)[:, None])
    rows.append(np.zeros((8, SHORT), bool))
    return np.concatenate(rows).astype(np.float32)


def block_bias():
    key = np.arange(32)[:, None]
    query = np.arange(2 * TILE)[None]
    across = (key < BLOCK) != (query % 32 < BLOCK)
    last = np.where(query % TILE >= 96, ~across, across)
    kinds = [np.ones_like(across), across, last]
    return np.stack([np.where(kind, 0.0, far_off) for kind in kinds]).astype(np.float32)


def head_mask():
    lane = np.arange(TILE)[None]
    side = np.arange(2 * TILE)[:, None] // TILE
    return (lane // HEAD == side).astype(np.float32)


def group_mask():
    key = np.arange(TILE)[:, None]
    query = np.arange(2 * TILE)[None]
    return (key // 32 == query % TILE // 32).astype(np.float32)


def top_level_of():
    index = np.arange(TILE)
    return np.minimum(LOW_TOP + (index >= 64) * 1 + (index >= 96) * 1 + (index >= 112) * 1, 7)


def nn(a, b):
    return lax.dot_general(a, b, (((1,), (0,)), ((), ())), preferred_element_type=f32)


def nt(a, b):
    return lax.dot_general(a, b, (((1,), (1,)), ((), ())), preferred_element_type=f32)


def tn(a, b):
    return lax.dot_general(a, b, (((0,), (0,)), ((), ())), preferred_element_type=f32)


def normalize(values):
    center = values - jnp.mean(values, axis=-1, keepdims=True)
    inverse = lax.rsqrt(jnp.mean(center * center, axis=-1, keepdims=True) + norm_eps)
    return center * inverse, inverse


def normalize_back(grad_normed, normed, inverse):
    return inverse * (
        grad_normed
        - jnp.mean(grad_normed, axis=-1, keepdims=True)
        - normed * jnp.mean(grad_normed * normed, axis=-1, keepdims=True)
    )


def gelu_both(v):
    mag = jnp.abs(v) * (0.5**0.5)
    t = 1.0 / (1.0 + 0.3275911 * mag)
    gauss = jnp.exp(-0.5 * v * v)
    poly = t * (
        0.254829592
        + t * (-0.284496736 + t * (1.421413741 + t * (-1.453152027 + t * 1.061405429)))
    )
    tail = 0.5 * poly * gauss
    cdf = jnp.where(v < 0, tail, 1.0 - tail)
    return v * cdf, cdf + v * gauss * ((2 * math.pi) ** -0.5)


def split3(values):
    one = values.astype(bf16)
    rest = values - one.astype(f32)
    two = rest.astype(bf16)
    return one, two, (rest - two.astype(f32)).astype(bf16)


def split2(values):
    one = values.astype(bf16)
    return one, (values - one.astype(f32)).astype(bf16)


class Place:
    def __init__(self):
        self.dp = lax.axis_index("dp")
        self.fs = lax.axis_index("fsdp")
        self.z, self.y = self.dp // 2, self.dp % 2
        self.x, self.c = self.fs // 2, self.fs % 2
        self.oy, self.ox, self.oc = 1 - self.y, 1 - self.x, 1 - self.c
        self.zs = [lax.rem(self.z + step, 4) for step in (1, 2, 3)]
        self.by_core = (self.dp, self.x * 2 + self.oc)
        self.by_x = (self.dp, self.ox * 2 + self.c)
        self.by_y = (self.z * 2 + self.oy, self.fs)
        self.by_z = [(z * 2 + self.y, self.fs) for z in self.zs]


def remote(src, dst, send, recv, device):
    return pltpu.make_async_remote_copy(
        src_ref=src, dst_ref=dst, send_sem=send, recv_sem=recv, device_id=device, device_id_type=MESH
    )


class Gather:
    def __init__(self, ref, p, send, recv, half):
        g = ref
        a, b = pl.ds(0, half), pl.ds(half, g.shape[-1] - half)
        count = iter(range(12))

        def copy(at, device):
            slot = next(count)
            return remote(at, at, send.at[slot], recv.at[slot], device)

        mine = g.at[p.z, p.y, p.x, p.c]
        self.zs = [copy(mine, device) for device in p.by_z]
        self.one = [copy(g.at[:, p.y, p.x, p.c, :, a], p.by_x), copy(g.at[:, p.y, p.x, p.c, :, b], p.by_y)]
        self.core_one = [copy(g.at[:, p.y, p.x, p.c], p.by_core)]
        self.two = [copy(g.at[:, p.y, :, p.c, :, a], p.by_y), copy(g.at[:, :, p.x, p.c, :, b], p.by_x)]
        self.core_two = [
            copy(g.at[:, p.y, p.ox, p.c, :, a], p.by_core),
            copy(g.at[:, p.oy, p.x, p.c, :, b], p.by_core),
        ]
        self.core_three = [
            copy(g.at[:, p.oy, :, p.c, :, a], p.by_core),
            copy(g.at[:, :, p.ox, p.c, :, b], p.by_core),
        ]
        self.every = self.zs + self.one + self.core_one + self.two + self.core_two + self.core_three

    def begin(self):
        for copy in self.zs:
            copy.start()

    def second(self):
        for copy in self.zs:
            copy.wait_recv()
        for copy in self.one + self.core_one:
            copy.start()

    def third(self):
        for copy in self.one:
            copy.wait_recv()
        for copy in self.two + self.core_two:
            copy.start()

    def fourth(self):
        for copy in self.two:
            copy.wait_recv()
        for copy in self.core_three:
            copy.start()

    def finish(self):
        for copy in self.core_one + self.core_two + self.core_three:
            copy.wait_recv()
        for copy in self.every:
            copy.wait_send()


class Scatter:
    def __init__(self, ref, p, send, recv, half, cores, from_core, one_a, one_b, two_a, two_b, far):
        s = ref
        self.s, self.p = ref, p
        self.a, self.b = a, b = pl.ds(0, half), pl.ds(half, s.shape[-1] - half)
        self.from_core, self.one_a, self.one_b = from_core, one_a, one_b
        self.two_a, self.two_b, self.far = two_a, two_b, far
        count = iter(range(7))

        def copy(at, dst, device):
            slot = next(count)
            return remote(at, dst, send.at[slot], recv.at[slot], device)

        self.cores = cores
        self.one = [
            copy(s.at[:, p.oy, :, p.c, :, a], one_a, p.by_y),
            copy(s.at[:, :, p.ox, p.c, :, b], one_b, p.by_x),
        ]
        self.two = [
            copy(s.at[:, p.y, p.ox, p.c, :, a], two_a, p.by_x),
            copy(s.at[:, p.oy, p.x, p.c, :, b], two_b, p.by_y),
        ]
        self.zs = [
            copy(s.at[z, p.y, p.x, p.c], far.at[step], device)
            for step, (z, device) in enumerate(zip(p.zs, p.by_z))
        ]

    def second(self):
        p, s = self.p, self.s
        for copy in self.cores:
            copy.wait_recv()

        def add(z, carry):
            s[z, :, :, p.c] = (s[z, :, :, p.c].astype(f32) + self.from_core[z].astype(f32)).astype(bf16)
            return carry

        lax.fori_loop(0, 4, add, 0)
        for copy in self.one:
            copy.start()

    def third(self):
        p, s, a, b = self.p, self.s, self.a, self.b
        for copy in self.one:
            copy.wait_recv()

        def add(z, carry):
            s[z, p.y, :, p.c, :, a] = (s[z, p.y, :, p.c, :, a].astype(f32) + self.one_a[z].astype(f32)).astype(bf16)
            s[z, :, p.x, p.c, :, b] = (s[z, :, p.x, p.c, :, b].astype(f32) + self.one_b[z].astype(f32)).astype(bf16)
            return carry

        lax.fori_loop(0, 4, add, 0)
        for copy in self.two:
            copy.start()

    def fourth(self):
        p, s, a, b = self.p, self.s, self.a, self.b
        for copy in self.two:
            copy.wait_recv()

        def add(z, carry):
            s[z, p.y, p.x, p.c, :, a] = (s[z, p.y, p.x, p.c, :, a].astype(f32) + self.two_a[z].astype(f32)).astype(bf16)
            s[z, p.y, p.x, p.c, :, b] = (s[z, p.y, p.x, p.c, :, b].astype(f32) + self.two_b[z].astype(f32)).astype(bf16)
            return carry

        lax.fori_loop(0, 4, add, 0)
        for copy in self.zs:
            copy.start()

    def finish(self, out):
        p = self.p
        total = self.s[p.z, p.y, p.x, p.c].astype(f32)
        for step, copy in enumerate(self.zs):
            copy.wait_recv()
            total = total + self.far[step].astype(f32)
        out[...] = total
        for copy in self.cores + self.one + self.two + self.zs:
            copy.wait_send()


def layer_kernel(fast, kinds, *refs):
    shapes = dict(kinds, **scratch_list(fast))
    r, left = types.SimpleNamespace(), list(refs)
    for name, kind in shapes.items():
        amount = len(kind) if isinstance(kind, list) else 1
        taken, left = left[:amount], left[amount:]
        setattr(r, name, taken if isinstance(kind, list) else taken[0])
    assert not left
    p = Place()
    tok, cot = r.tok, r.cot
    member, spread = r.member, r.spread
    stack, probs, out_t, mix_t = r.stack, r.probs, r.out_t, r.mix_t
    lse_s, share, inner_s, total_h = r.lse_s, r.share, r.inner_s, r.total_h
    resid, n_one, n_two = r.resid, r.n_one, r.n_two
    acc_out, acc_two = r.acc_out, r.acc_two
    pair_ff = r.pair_ff
    g_att, g_num = r.g_att, r.g_num
    g_mix, weight = g_num.at[0:SHORT], r.weight
    grad_v = r.grad_v
    vec = r.vec
    wa, wi, wo = r.wa, r.wi, r.wo
    da, di, do = (r.da, r.di, r.do) if fast else (r.o_a, r.o_i, r.o_o)
    grad_k = pair_ff
    grad_qt = out_t

    local = []

    def fetch(src, dst):
        copy = pltpu.make_async_copy(src, dst, r.in_sem.at[len(local)])
        copy.start()
        local.append(copy)

    if fast:
        own = wa.at[p.z, p.y, p.x, p.c]
        for slot, ref in enumerate((r.wq_s, r.wk_s, r.wv_s)):
            fetch(ref, own.at[:, pl.ds(slot * D, D)])
        own = wi.at[p.z, p.y, p.x, p.c]
        fetch(r.wi_s, own.at[:, pl.ds(0, 4 * D)])
        fetch(r.wm_s, own.at[:, pl.ds(4 * D, D)])
        fetch(r.wo_s, wo.at[p.z, p.y, p.x, p.c])
    shards = len(local)
    fetch(r.tok_h, tok)
    fetch(r.member_h, member)
    fetch(r.cot_h, cot)
    fetch(r.spread_h, spread)

    other = p.fs // 2 * 2 + 1 - p.fs % 2
    pair = (1 - p.fs // 2) * 2
    side = p.fs % 2
    barrier = pltpu.get_barrier_semaphore()
    reach = [(p.dp, other), (p.dp, pair), (p.dp, pair + 1)]
    if fast:
        reach += [p.by_y] + p.by_z
    for device in reach:
        pl.semaphore_signal(barrier, inc=1, device_id=device, device_id_type=MESH)
    if fast:
        whose = p.dp * 4 + p.fs
        at = lax.broadcasted_iota(jnp.int32, (HEAD, SMALL), 0)
        lane = lax.broadcasted_iota(jnp.int32, (HEAD, SMALL), 1)
        rows = [ref[...].astype(f32).reshape(1, 16) for ref in r.vectors[:6]]
        rows = jnp.concatenate(rows + [jnp.zeros((10, 16), f32)], axis=0).astype(bf16)
        spot = (lane[0:16] == at[0:16] + 16 * (whose % 8)).astype(f32).astype(bf16)
        own = nn(rows, spot)
        bias = jnp.concatenate([r.vectors[6][...].astype(f32).reshape(1, HEAD), jnp.zeros((15, HEAD), f32)], axis=0)
        spot = (lane == at + HEAD * (whose % 2)).astype(f32).astype(bf16)
        own_bias = nn(bias.astype(bf16), spot)
        own = jnp.concatenate([own[0:6], own_bias[0:1], jnp.zeros((9, SMALL), f32)], axis=0)
        wa[p.z, p.y, p.x, p.c, :, WIDTH : WIDTH + SMALL] = own.astype(bf16)
    for copy in local[:shards]:
        copy.wait()
    pl.semaphore_wait(barrier, len(reach))


    def first_norm(step, carry):
        at = pl.ds(pl.multiple_of(step * CHUNK, CHUNK), CHUNK)
        acc_two[at, :] = normalize(tok[at, :].astype(f32))[0]
        return carry

    if fast:
        gat_a = Gather(wa, p, *r.ga, 768)
        gat_i = Gather(wi, p, *r.gi, 1280)
        gat_o = Gather(wo, p, *r.go, 256)
        gat_a.begin()
    for copy in local[shards:]:
        copy.wait()
    lax.fori_loop(0, SHORT // CHUNK, first_norm, 0)
    if fast:
        gat_a.second()
        gat_i.begin()
        gat_a.third()
        gat_a.fourth()
        gat_i.second()
        gat_o.begin()
        gat_a.finish()

    def rows_of(ref, lo, width):
        return ref[:, :, :, :, :, lo : lo + width].reshape(512, width)

    small = wa[:, :, :, :, :, WIDTH : WIDTH + SMALL].astype(f32)
    by_z = jnp.sum(small, axis=(1, 2, 3))
    param = jnp.concatenate([by_z[z] for z in range(4)], axis=1)
    r.param[...] = param
    by_pair = jnp.sum(small, axis=3)
    r.bias_in[...] = jnp.concatenate(
        [by_pair[z, y, x, 6:7, :] for z in range(4) for y in range(2) for x in range(2)], axis=1
    )
    vec[...] = jnp.zeros_like(vec)
    r.lanes_in[...] = jnp.zeros_like(r.lanes_in)

    gain_one, shift_one = r.param[0:1, :], r.param[1:2, :]

    def scale_shift(step, carry):
        at = pl.ds(pl.multiple_of(step * CHUNK, CHUNK), CHUNK)
        n_one[at, :] = (acc_two[at, :] * gain_one + shift_one).astype(bf16)
        return carry

    lax.fori_loop(0, SHORT // CHUNK, scale_shift, 0)

    def project(third, carry):
        lanes = pl.ds(pl.multiple_of(third * D, D), D)
        made = nn(n_one[...], wa[:, :, :, :, :, lanes].reshape(D, D))
        stack[0:SHORT, lanes] = (made * jnp.where(third == 0, 0.125, 1.0)).astype(bf16)
        return carry

    lax.fori_loop(0, 3, project, 0)
    if fast:
        gat_i.third()

    index = lax.broadcasted_iota(jnp.int32, (TILE, 1), 0)
    steps_down = jnp.where(
        index < 64, 1 / 16, jnp.where(index < 96, 1 / 32, jnp.where(index < 112, 1 / 64, 1 / 128))
    ).astype(f32)

    def chunk_rows(step):
        one = pl.ds(pl.multiple_of(FIRST[1] + step * 128, 128), 128)
        two = pl.ds(pl.multiple_of(FIRST[2] + step * 64, 64), 64)
        return one, two, pl.ds(pl.multiple_of(FIRST[3] + step * 32, 32), 32)

    def chunk_members(chunk):
        near = [member[lo:hi, 0:CHUNK] for lo, hi in ((0, 128), (128, 192), (256, 288))]
        return near + [member[lo:hi, chunk] for lo, hi in ((384, 448), (448, 480), (480, 496), (496, 512))]

    tops_acc = acc_out
    tops_acc[0:384, :] = jnp.zeros((384, D), f32)

    def pool(step, carry):
        chunk = pl.ds(pl.multiple_of(step * CHUNK, CHUNK), CHUNK)
        rows = jnp.concatenate(chunk_members(chunk), axis=0)
        to = chunk_rows(step)
        for third in range(3):
            lanes = pl.ds(third * D, D)
            made = nn(rows, stack[chunk, lanes])
            for level, (lo, hi) in enumerate(((0, 128), (128, 192), (192, 224))):
                scale = 1.0 if third == 2 else 0.5 ** (level + 1)
                stack[to[level], lanes] = (made[lo:hi] * scale).astype(bf16)
            tops_acc[third * TILE : (third + 1) * TILE, :] += made[224:352]
        return carry

    lax.fori_loop(0, SHORT // CHUNK, pool, 0)
    for third in range(3):
        made = tops_acc[third * TILE : (third + 1) * TILE, :]
        stack[FIRST[4] : STACK, third * D : (third + 1) * D] = (
            made if third == 2 else made * steps_down
        ).astype(bf16)

    far_s, far_r = r.far_s, r.far_r
    far_s[0] = stack[2016:2032, D:]
    far_s[1] = stack[2032:2048, D:]
    send, recv = r.far_send, r.far_recv
    far_out = [
        remote(far_s.at[0], far_r.at[0], send.at[0], recv.at[0], (p.dp, other)),
        remote(far_s.at[1], far_r.at[1 + side], send.at[1], recv.at[1 + side], (p.dp, pair)),
        remote(far_s.at[1], far_r.at[1 + side], send.at[2], recv.at[1 + side], (p.dp, pair + 1)),
    ]
    for copy in far_out:
        copy.start()

    lane_group = lax.broadcasted_iota(jnp.int32, (32, 2 * TILE), 1) % TILE // 32

    def squeeze(tall):
        parts = [tall[32 * part : 32 * part + 32, :] for part in range(4)]
        return jnp.where(
            lane_group < 2,
            jnp.where(lane_group == 0, parts[0], parts[1]),
            jnp.where(lane_group == 2, parts[2], parts[3]),
        )

    def widen(low):
        return jnp.concatenate([low, low, low, low], axis=0) * r.group_m[...]

    def two_heads(low):
        return jnp.concatenate([low, low], axis=0) * r.head_m[...]

    def tile_forward(tile, kind, scale_t):
        rows = pl.ds(pl.multiple_of(tile * TILE, TILE), TILE)
        bias = r.bias[kind]
        tops = []
        for pair_at in range(HEADS // 2):
            lo = pair_at * TILE
            query = two_heads(stack[rows, lo : lo + TILE])
            score = squeeze(nt(stack[rows, D + lo : D + lo + TILE], query)) + bias
            peak = jnp.max(score, axis=0, keepdims=True)
            prob = jnp.exp(score - peak)
            total = jnp.sum(prob, axis=0, keepdims=True)
            low = (prob * (1.0 / total)).astype(bf16)
            probs[tile, :, pair_at * 2 * TILE : (pair_at + 1) * 2 * TILE] = low
            log_total = peak + jnp.log(total)
            tops += [log_total[:, :TILE], log_total[:, TILE:]]
            wide = widen(low)
            made = nn(stack[rows, 2 * D + lo : 2 * D + lo + TILE].T, wide)
            out_t[lo : lo + HEAD, rows] = (made[:HEAD, :TILE] * scale_t).astype(bf16)
            out_t[lo + HEAD : lo + TILE, rows] = (made[HEAD:, TILE:] * scale_t).astype(bf16)
        lse_s[:, rows] = jnp.concatenate(tops, axis=0)

    top_lane = lax.broadcasted_iota(jnp.int32, (HEADS, TILE), 1)
    top_scale_t = jnp.where(
        top_lane < 64, 1 / 16, jnp.where(top_lane < 96, 1 / 32, jnp.where(top_lane < 112, 1 / 64, 1 / 128))
    ).astype(f32)

    def tile_scale(tile):
        return jnp.where(
            tile < 8, 1.0, jnp.where(tile < 12, 0.5, jnp.where(tile < 14, 0.25, 0.125))
        ).astype(f32)

    def near_tiles(tile, carry):
        if fast:
            pl.when(tile == 3)(gat_i.fourth)
            pl.when(tile == 4)(gat_o.second)
            pl.when(tile == 8)(gat_o.third)
            pl.when(tile == 13)(gat_o.fourth)
        tile_forward(tile, jnp.where(tile < 8, 0, 1), tile_scale(tile))
        return carry

    lax.fori_loop(0, 15, near_tiles, 0)
    for slot in range(3):
        remote(far_s.at[0], far_r.at[slot], send.at[slot], recv.at[slot], (p.dp, other)).wait_recv()
    for copy in far_out:
        copy.wait_send()
    stack[2016:2032, D:] = far_r[0]
    stack[2032:2048, D:] = jnp.concatenate(
        [far_r[1].astype(f32)[:8], far_r[2].astype(f32)[:8]], axis=0
    ).astype(bf16)
    tile_forward(15, 2, top_scale_t[0:1, :])
    idle = jnp.where(r.row_length[0] > SHORT, 0.0, far_off)
    lse_s[:, 1920:2048] = lse_s[:, 1920:2048] + jnp.where(top_lane >= 96, idle, 0.0)

    edges = (0, 64, 96, 112, 128)

    def windows(step):
        one = pl.ds(pl.multiple_of(FIRST[1] + step * TILE, TILE), TILE)
        two = pl.ds(pl.multiple_of(FIRST[2] + step // 2 * TILE, TILE), TILE)
        return one, two, pl.ds(FIRST[3], TILE), pl.ds(FIRST[4], TILE)

    def per_level(step, chunk):
        one = member[0:512, chunk]

        def for_head(head):
            rows = []
            spans = [(0, 128), (128, 256), (256, 384), (384, 448), (448, 480), (480, 496), (496, 512)]
            for level, (lo, hi) in enumerate(spans, 1):
                rows.append(one[lo:hi] * share[level, head : head + 1, chunk].astype(bf16))
            return jnp.concatenate(rows, axis=0)

        return for_head

    def combine(step, carry):
        chunk = pl.ds(pl.multiple_of(step * CHUNK, CHUNK), CHUNK)
        wins = windows(step)
        logs = [lse_s[:, chunk]]
        for slot in range(3):
            parts = jnp.concatenate(split3(lse_s[:, wins[slot]]), axis=0)
            made = nn(parts, member[slot * TILE : (slot + 1) * TILE, chunk])
            logs.append(made[0:8] + made[8:16] + made[16:24] + (slot + 1) * math.log(2.0))
        top = lse_s[:, wins[3]]
        parts = []
        for slot in range(4):
            inside = (top_lane >= edges[slot]) & (top_lane < edges[slot + 1])
            parts += list(split3(jnp.where(inside, top, 0.0)))
        made = nn(jnp.concatenate(parts, axis=0), member[384:512, chunk])
        for slot in range(4):
            b = slot * 24
            logs.append(made[b : b + 8] + made[b + 8 : b + 16] + made[b + 16 : b + 24] + (slot + 4) * math.log(2.0))
        peak = functools.reduce(jnp.maximum, logs)
        den = functools.reduce(jnp.add, [jnp.exp(one - peak) for one in logs])
        lse = peak + jnp.log(den)
        for level in range(LEVELS):
            share[level, :, chunk] = jnp.exp(logs[level] - lse)
        for_head = per_level(step, chunk)
        for head in range(HEADS):
            at = slice(head * HEAD, (head + 1) * HEAD)
            coarse = jnp.concatenate([out_t[at, win] for win in wins], axis=1)
            made = nn(coarse, for_head(head))
            made = made + share[0, head : head + 1, chunk] * out_t[at, chunk].astype(f32)
            mix_t[at, chunk] = made.astype(bf16)
        return carry

    lax.fori_loop(0, SHORT // CHUNK, combine, 0)

    if fast:
        gat_i.finish()
    bias_mix, gain_two = r.param[2:3, :], r.param[3:4, :]
    shift_two, bias_out = r.param[4:5, :], r.param[5:6, :]
    w_mix = rows_of(wi, 4 * D, D)
    resid[...] = tn(mix_t[...], w_mix)

    def second_norm(step, carry):
        at = pl.ds(pl.multiple_of(step * CHUNK, CHUNK), CHUNK)
        mid = tok[at, :].astype(f32) + resid[at, :] + bias_mix
        resid[at, :] = mid
        normed, _ = normalize(mid)
        n_two[at, :] = (normed * gain_two + shift_two).astype(bf16)
        return carry

    lax.fori_loop(0, SHORT // CHUNK, second_norm, 0)
    if fast:
        gat_o.finish()

    hid, g_pre = pair_ff.at[0:SHORT], pair_ff.at[SHORT:STACK]
    acc_out[...] = jnp.zeros_like(acc_out)
    acc_two[...] = jnp.zeros_like(acc_two)

    if fast:
        ways = (r.si[2], r.so[2], r.core_send, r.core_recv)

        def core_i(part):
            lanes = pl.ds(pl.multiple_of(part * 512, 512), 512)
            return remote(
                di.at[:, :, :, p.oc, :, lanes], ways[0].at[:, :, :, :, lanes], ways[2].at[part], ways[3].at[part], p.by_core
            )

        def core_o(part):
            return remote(do.at[part, :, :, p.oc], ways[1].at[part], ways[2].at[part + 5], ways[3].at[part + 5], p.by_core)

    def feed(part, carry):
        lanes = pl.ds(pl.multiple_of(part * 512, 512), 512)
        w_in = wi[:, :, :, :, :, lanes].reshape(512, 512)
        w_out = wo[part].reshape(512, 512)
        b_in = r.bias_in[:, lanes]
        sums = jnp.zeros((1, 512), f32)
        for step in range(FEED_STEPS):
            at = pl.ds(step * (SHORT // FEED_STEPS), SHORT // FEED_STEPS)
            act, slope = gelu_both(nn(n_two[at, :], w_in) + b_in)
            act = act.astype(bf16)
            hid[at, :] = act
            back = (nt(cot[at, :], w_out) * slope).astype(bf16)
            g_pre[at, :] = back
            acc_out[at, :] += nn(act, w_out)
            acc_two[at, :] += nt(back, w_in)
            sums = sums + jnp.sum(back.astype(f32), axis=0, keepdims=True)
        r.lanes_in[0:1, lanes] = sums
        di[:, :, :, :, :, lanes] = tn(n_two[...], g_pre[...]).astype(bf16).reshape(4, 2, 2, 2, 16, 512)
        do[part] = tn(hid[...], cot[...]).astype(bf16).reshape(2, 2, 2, 64, 512)
        if fast:
            core_i(part).start()
            core_o(part).start()
        return carry

    lax.fori_loop(0, 4, feed, 0)

    if fast:
        sc_i = Scatter(
            di, p, *r.si[:2], 1280, [core_i(k) for k in range(5)], *r.si[2:]
        )
        sc_o = Scatter(
            do, p, *r.so[:2], 256, [core_o(k) for k in range(4)], *r.so[2:]
        )
        sc_o.second()

    def middle(step, carry):
        at = pl.ds(pl.multiple_of(step * CHUNK, CHUNK), CHUNK)
        mid = resid[at, :]
        r.out[at, :] = (mid + acc_out[at, :] + bias_out).astype(bf16)
        normed, inverse = normalize(mid)
        g_two = acc_two[at, :]
        c = cot[at, :].astype(f32)
        g_mid = c + normalize_back(g_two * gain_two, normed, inverse)
        resid[at, :] = g_mid
        low = g_mid.astype(bf16)
        g_att[at, :] = low
        vec[2:3, :] += jnp.sum(low.astype(f32), axis=0, keepdims=True)
        vec[3:4, :] += jnp.sum(g_two * normed, axis=0, keepdims=True)
        vec[4:5, :] += jnp.sum(g_two, axis=0, keepdims=True)
        vec[5:6, :] += jnp.sum(c, axis=0, keepdims=True)
        return carry

    lax.fori_loop(0, SHORT // CHUNK, middle, 0)
    g_mix[...] = nt(g_att[...], w_mix).astype(bf16)

    def inner_sums(step, carry):
        at = pl.ds(pl.multiple_of(step * 512, 512), 512)
        turned = nt(w_mix, g_att[at, :]).astype(bf16).astype(f32) * mix_t[:, at].astype(f32)
        inner_s[:, at] = jnp.concatenate(
            [jnp.sum(turned[h * HEAD : (h + 1) * HEAD], axis=0, keepdims=True) for h in range(HEADS)], axis=0
        )
        return carry

    lax.fori_loop(0, SHORT // 512, inner_sums, 0)

    made = nn(mix_t[...], g_att[...])
    di[:, :, :, :, :, 4 * D :] = made.astype(bf16).reshape(4, 2, 2, 2, 16, D)
    if fast:
        core_i(4).start()
        sc_o.third()


    def sums_of(level, source, members):
        both = jnp.concatenate(split2(share[level, :, source] * inner_s[:, source]), axis=0)
        made = nt(both, members)
        return made[0:8] + made[8:16]

    tops_acc[0:TILE, :] = jnp.zeros((TILE, D), f32)

    def lift(step, carry):
        chunk = pl.ds(pl.multiple_of(step * CHUNK, CHUNK), CHUNK)
        to = chunk_rows(step)
        members = chunk_members(chunk)
        for pair_at in range(HEADS // 2):
            lo = pair_at * TILE
            left = [
                jnp.concatenate(
                    [one * share[1 + k, head : head + 1, chunk].astype(bf16) for k, one in enumerate(members)], axis=0
                )
                for head in (2 * pair_at, 2 * pair_at + 1)
            ]
            tokens = g_num[chunk, lo : lo + TILE]
            right = [tokens * r.head_m[0:1, :], tokens * r.head_m[TILE : TILE + 1, :]]
            made = nn(jnp.concatenate(left, axis=1), jnp.concatenate(right, axis=0))
            for level, (low, high) in enumerate(((0, 128), (128, 192), (192, 224))):
                g_num[to[level], lo : lo + TILE] = (made[low:high] * 0.5 ** (level + 1)).astype(bf16)
            tops_acc[0:TILE, lo : lo + TILE] += made[224:352]
        total_h[:, chunk] = share[0, :, chunk] * inner_s[:, chunk]
        total_h[:, to[0]] = sums_of(1, chunk, member[0:128, chunk])
        return carry

    lax.fori_loop(0, SHORT // CHUNK, lift, 0)
    g_num[FIRST[4] : STACK, :] = (tops_acc[0:TILE, :] * steps_down).astype(bf16)

    def lift_two(step, carry):
        source = pl.ds(pl.multiple_of(step * 512, 512), 512)
        rows = pl.ds(pl.multiple_of(FIRST[2] + step * TILE, TILE), TILE)
        total_h[:, rows] = sums_of(2, source, member[128:256, source])
        return carry

    lax.fori_loop(0, 2, lift_two, 0)
    every = pl.ds(0, SHORT)
    total_h[:, FIRST[3] : FIRST[4]] = sums_of(3, every, member[256:384, :])
    tops = [sums_of(4 + slot, every, member[384:512, :]) for slot in range(4)]
    total_h[:, FIRST[4] : STACK] = jnp.where(
        top_lane < 64, tops[0], jnp.where(top_lane < 96, tops[1], jnp.where(top_lane < 112, tops[2], tops[3]))
    )
    if fast:
        sc_i.second()
        sc_o.fourth()
    weight[:, 0:SHORT] = share[0]
    weight[:, SHORT:STACK] = jnp.ones((HEADS, SHORT), f32)

    def tile_backward(tile, scale, scale_t):
        rows = pl.ds(pl.multiple_of(tile * TILE, TILE), TILE)
        for pair_at in range(HEADS // 2):
            lo = pair_at * TILE
            both = lambda ref: jnp.concatenate(
                [ref[2 * pair_at : 2 * pair_at + 1, rows], ref[2 * pair_at + 1 : 2 * pair_at + 2, rows]], axis=1
            )
            low = probs[tile, :, pair_at * 2 * TILE : (pair_at + 1) * 2 * TILE].astype(f32)
            times = both(weight)
            num = two_heads(g_num[rows, lo : lo + TILE])
            got = squeeze(nt(stack[rows, 2 * D + lo : 2 * D + lo + TILE], num))
            wide_s = widen((low * (got * times - both(total_h))).astype(bf16))
            wide_p = widen((low * times).astype(bf16))
            query = two_heads(stack[rows, lo : lo + TILE])
            grad_k[rows, lo : lo + TILE] = (nn(wide_s, query) * scale).astype(bf16)
            grad_v[rows, lo : lo + TILE] = nn(wide_p, num).astype(bf16)
            made = nn(stack[rows, D + lo : D + lo + TILE].T, wide_s)
            grad_qt[lo : lo + HEAD, rows] = (made[:HEAD, :TILE] * scale_t).astype(bf16)
            grad_qt[lo + HEAD : lo + TILE, rows] = (made[HEAD:, TILE:] * scale_t).astype(bf16)

    tile_backward(15, steps_down, top_scale_t[0:1, :] * 0.125)
    back_s, back_r = r.back_s, r.back_r
    top_k, top_v = grad_k[2016:2048, :].astype(f32), grad_v[2016:2048, :].astype(f32)
    tall = jnp.concatenate([top_k, top_v], axis=1)
    nothing = jnp.zeros((8, 2 * D), f32)
    back_s[0] = tall[0:16].astype(bf16)
    back_s[1] = jnp.concatenate([tall[16:24], nothing], axis=0).astype(bf16)
    back_s[2] = jnp.concatenate([tall[24:32], nothing], axis=0).astype(bf16)
    send, recv = r.back_send, r.back_recv
    back_out = [
        remote(back_s.at[0], back_r.at[0], send.at[0], recv.at[0], (p.dp, other)),
        remote(back_s.at[1], back_r.at[1 + side], send.at[1], recv.at[1 + side], (p.dp, pair)),
        remote(back_s.at[2], back_r.at[1 + side], send.at[2], recv.at[1 + side], (p.dp, pair + 1)),
    ]
    for copy in back_out:
        copy.start()

    def near_back(tile, carry):
        if fast:
            pl.when(tile == 2)(sc_i.third)
            pl.when(tile == 8)(sc_i.fourth)
        scale = tile_scale(tile)
        tile_backward(tile, scale, scale * 0.125)
        return carry

    lax.fori_loop(0, 15, near_back, 0)
    for slot in range(3):
        remote(back_s.at[slot], back_r.at[slot], send.at[slot], recv.at[slot], (p.dp, other)).wait_recv()
    for copy in back_out:
        copy.wait_send()
    two = back_r[1].astype(f32) + back_r[2].astype(f32)
    grad_k[2016:2032, :] = back_r[0, :, 0:D]
    grad_v[2016:2032, :] = back_r[0, :, D:]
    grad_k[2032:2048, :] = two[:, 0:D].astype(bf16)
    grad_v[2032:2048, :] = two[:, D:].astype(bf16)

    def level_sums(step, carry):
        chunk = pl.ds(pl.multiple_of(step * CHUNK, CHUNK), CHUNK)
        wins = windows(step)
        turned = nn(jnp.concatenate([grad_qt[:, win] for win in wins], axis=1), member[:, chunk])
        turned = (turned + grad_qt[:, chunk].astype(f32)).astype(bf16)
        stack[chunk, 0:D] = turned.T
        for slot, ref in ((1, grad_k), (2, grad_v)):
            made = nn(spread[chunk, :], jnp.concatenate([ref[win, :] for win in wins], axis=0))
            stack[chunk, slot * D : (slot + 1) * D] = (made + ref[chunk, :].astype(f32)).astype(bf16)
        return carry

    lax.fori_loop(0, SHORT // CHUNK, level_sums, 0)

    def project_grad(part, carry):
        lanes = pl.ds(pl.multiple_of(part * D, D), D)
        made = tn(n_one[...], stack[0:SHORT, lanes])
        da[:, :, :, :, :, lanes] = made.astype(bf16).reshape(4, 2, 2, 2, 16, D)
        return carry

    lax.fori_loop(0, 3, project_grad, 0)
    if fast:
        core_a = remote(da.at[:, :, :, p.oc], r.sa[2], r.core_send.at[9], r.core_recv.at[9], p.by_core)
        core_a.start()
        sc_a = Scatter(da, p, *r.sa[:2], 768, [core_a], *r.sa[2:])
        sc_o.finish(r.o_o)
        sc_i.finish(r.o_i)

    acc_two[...] = nt(stack[0:SHORT, :], wa[:, :, :, :, :, 0:WIDTH].reshape(D, WIDTH))
    if fast:
        sc_a.second()

    def first_back(step, carry):
        if fast:
            pl.when(step == 3)(sc_a.third)
        chunk = pl.ds(pl.multiple_of(step * CHUNK, CHUNK), CHUNK)
        g_one = acc_two[chunk, :]
        normed, inverse = normalize(tok[chunk, :].astype(f32))
        vec[0:1, :] += jnp.sum(g_one * normed, axis=0, keepdims=True)
        vec[1:2, :] += jnp.sum(g_one, axis=0, keepdims=True)
        r.g_tok[chunk, :] = (resid[chunk, :] + normalize_back(g_one * gain_one, normed, inverse)).astype(bf16)
        return carry

    lax.fori_loop(0, SHORT // CHUNK, first_back, 0)
    for part in range(4):
        vec[8 + part : 9 + part, :] = r.lanes_in[0:1, part * 512 : (part + 1) * 512]
    if fast:
        vec_r, vec_n = r.vec_r, r.vec_n
        send, recv = r.v_send, r.v_recv
        hops = [
            remote(src, vec_r.at[k], send.at[k], recv.at[k], device)
            for k, (src, device) in enumerate(((vec, p.by_core), (vec_n.at[0], p.by_y), (vec_n.at[1], p.by_x)))
        ]
        hops += [
            remote(vec_n.at[2], vec_r.at[3 + k], send.at[3 + k], recv.at[3 + k], p.by_z[k]) for k in range(3)
        ]
        hops[0].start()
        hops[0].wait_recv()
        vec_n[0] = vec[...] + vec_r[0]
        hops[1].start()
        sc_a.fourth()
        hops[1].wait_recv()
        vec_n[1] = vec_n[0] + vec_r[1]
        hops[2].start()
        hops[2].wait_recv()
        vec_n[2] = vec_n[1] + vec_r[2]
        for hop in hops[3:]:
            hop.start()
        sc_a.finish(r.o_a)
        for hop in hops[3:]:
            hop.wait_recv()
        for hop in hops:
            hop.wait_send()
        total = vec_n[2] + vec_r[3] + vec_r[4] + vec_r[5]
        short = pltpu.roll(total[0:8], 512 - 16 * whose, axis=1)[:, 0:SMALL]
        long = jnp.concatenate([total[8 + k : 9 + k] for k in range(4)], axis=1)
        long = pltpu.roll(jnp.concatenate([long] * 8, axis=0), 2048 - HEAD * whose, axis=1)[:, 0:SMALL]
        r.o_v[0:8] = short
        r.o_v[8:16] = long
    else:
        r.o_v[...] = vec[...]


def final_kernel(out, g_tok, o_a, o_i, o_o, o_v, *rest):
    outs, (kept, sem) = rest[:-2], rest[-2:]
    halves = [pl.ds(k * 512, 512) for k in range(2)]
    into = [
        pltpu.make_async_copy(ref.at[half], kept.at[slot, half], sem.at[0, slot, k])
        for slot, ref in enumerate((out, g_tok)) for k, half in enumerate(halves)
    ]
    onto = [
        pltpu.make_async_copy(kept.at[slot, half], outs[slot].at[half], sem.at[1, slot, k])
        for slot in range(2) for k, half in enumerate(halves)
    ]
    for copy in into:
        copy.start()
    for slot, at in ((2, 0), (3, 1), (8, 2), (9, 3), (10, 4), (14, 5)):
        outs[slot][...] = o_v[at : at + 1, 0:16].reshape(16)
    outs[12][...] = o_v[8:9, 0:HEAD].reshape(HEAD)
    for k in range(3):
        outs[4 + k][...] = o_a[:, k * D : (k + 1) * D]
    outs[7][...] = o_i[:, 4 * D :]
    outs[11][...] = o_i[:, : 4 * D]
    outs[13][...] = o_o[...]
    for copy, then in zip(into, onto):
        copy.wait()
        then.start()
    for copy in onto:
        copy.wait()


def scratch_list(fast):
    V, S = pltpu.VMEM, pltpu.SemaphoreType.DMA
    made = dict(
        tok=V((SHORT, D), bf16),
        cot=V((SHORT, D), bf16),
        member=V((D, SHORT), bf16),
        spread=V((SHORT, D), bf16),
        in_sem=S((10,)),
        stack=V((STACK, WIDTH), bf16),
        probs=V((16, 32, HEADS * TILE), bf16),
        out_t=V((D, STACK), bf16),
        mix_t=V((D, SHORT), bf16),
        lse_s=V((HEADS, STACK), f32),
        share=V((LEVELS, HEADS, SHORT), f32),
        inner_s=V((HEADS, SHORT), f32),
        total_h=V((HEADS, STACK), f32),
        resid=V((SHORT, D), f32),
        n_one=V((SHORT, D), bf16),
        n_two=V((SHORT, D), bf16),
        acc_out=V((SHORT, D), f32),
        acc_two=V((SHORT, D), f32),
        pair_ff=V((STACK, D), bf16),
        g_att=V((SHORT, D), bf16),
        weight=V((HEADS, STACK), f32),
        g_num=V((STACK, D), bf16),
        grad_v=V((STACK, D), bf16),
        vec=V((16, D), f32),
        param=V((16, D), f32),
        bias_in=V((1, 4 * D), f32),
        lanes_in=V((8, 4 * D), f32),
        far_s=V((2, 16, 2 * D), bf16),
        far_r=V((3, 16, 2 * D), bf16),
        far_send=S((3,)),
        far_recv=S((3,)),
        back_s=V((3, 16, 2 * D), bf16),
        back_r=V((3, 16, 2 * D), bf16),
        back_send=S((3,)),
        back_recv=S((3,)),
    )
    if fast:
        pairs = lambda count: [S((count,)), S((count,))]

        def sums(rows, wide):
            half = wide // 2
            return pairs(7) + [
                V((4, 2, 2, rows, wide), bf16),
                V((4, 2, rows, half), bf16),
                V((4, 2, rows, half), bf16),
                V((4, rows, half), bf16),
                V((4, rows, half), bf16),
                V((3, rows, wide), bf16),
            ]

        made.update(
            wa=V(SLOTS + (16, WIDTH + SMALL), bf16),
            wi=V(SLOTS + (16, 5 * D), bf16),
            wo=V(SLOTS + (64, D), bf16),
            da=V(SLOTS + (16, WIDTH), bf16),
            di=V(SLOTS + (16, 5 * D), bf16),
            do=V(SLOTS + (64, D), bf16),
            ga=pairs(12),
            gi=pairs(12),
            go=pairs(12),
            si=sums(16, 5 * D),
            so=sums(64, D),
            sa=sums(16, WIDTH),
            core_send=S((10,)),
            core_recv=S((10,)),
            vec_r=V((6, 16, D), f32),
            vec_n=V((3, 16, D), f32),
            v_send=S((6,)),
            v_recv=S((6,)),
        )
    return made


def constants():
    member = member_matrix()
    as_low = lambda values: jnp.asarray(values.astype(np.float32), bf16)
    return dict(
        member_h=as_low(member),
        spread_h=as_low(np.ascontiguousarray(member.T)),
        head_m=as_low(head_mask()),
        group_m=as_low(group_mask()),
        bias=jnp.asarray(block_bias()),
    )


def run_layer(fast, hbm, vmem):
    sd = jax.ShapeDtypeStruct
    const = constants()
    hbm = dict(hbm, member_h=const.pop("member_h"), spread_h=const.pop("spread_h"))
    vmem = dict(vmem, **const)
    here, there = pl.BlockSpec(memory_space=pltpu.VMEM), pl.BlockSpec(memory_space=pl.ANY)
    slots = () if fast else SLOTS
    kind = f32 if fast else bf16
    outs = dict(
        out=sd((SHORT, D), bf16),
        g_tok=sd((SHORT, D), bf16),
        o_a=sd(slots + (16, WIDTH), kind),
        o_i=sd(slots + (16, 5 * D), kind),
        o_o=sd(slots + (64, D), kind),
        o_v=sd((16, SMALL if fast else D), f32),
    )
    row_length = hbm.pop("row_length")
    operands = dict(hbm, row_length=row_length, **vmem)
    specs = [there] * len(hbm) + [pl.BlockSpec(memory_space=pltpu.SMEM)]
    for operand in vmem.values():
        specs += [here] * (len(operand) if isinstance(operand, list) else 1)
    flat = lambda parts: [one for part in parts.values() for one in (part if isinstance(part, list) else [part])]
    return pl.pallas_call(
        functools.partial(layer_kernel, fast, dict(operands, **outs)),
        out_shape=list(outs.values()),
        in_specs=specs,
        out_specs=[here] * len(outs),
        scratch_shapes=flat(scratch_list(fast)),
        compiler_params=pltpu.CompilerParams(
            collective_id=0, has_side_effects=True, vmem_limit_bytes=63 * 2**20
        ),
    )(*flat(operands))


def finish_outputs(*parts):
    sd = jax.ShapeDtypeStruct
    vmem, hbm = pl.BlockSpec(memory_space=pltpu.VMEM), pl.BlockSpec(memory_space=pl.ANY)
    own, square = sd((16,), f32), sd((16, D), f32)
    tokens = sd((SHORT, D), bf16)
    outs = [tokens, tokens, own, own, square, square, square, square, own, own, own]
    outs += [sd((16, 4 * D), f32), sd((HEAD,), f32), sd((HEAD, D), f32), own]
    return pl.pallas_call(
        final_kernel,
        out_shape=outs,
        in_specs=[hbm] * 2 + [vmem] * 4,
        out_specs=[hbm] * 2 + [vmem] * 13,
        scratch_shapes=[pltpu.VMEM((2, SHORT, D), bf16), pltpu.SemaphoreType.DMA((2, 2, 2))],
    )(*parts)


def on_device(
    tokens, cotangent, row_length, first_gain, first_shift, query_weight, key_weight, value_weight,
    mixer_weight, mixer_bias, second_gain, second_shift, inner_weight, inner_bias, outer_weight, outer_bias,
):
    n_dp, n_fsdp = lax.axis_size("dp"), lax.axis_size("fsdp")
    fast = (n_dp, n_fsdp) == (8, 4) and query_weight.shape[0] == 16
    vectors = (first_gain, first_shift, mixer_bias, second_gain, second_shift, outer_bias)
    first = dict(tok_h=tokens, cot_h=cotangent, row_length=row_length)
    if fast:
        first.update(
            wq_s=query_weight, wk_s=key_weight, wv_s=value_weight, wm_s=mixer_weight, wi_s=inner_weight, wo_s=outer_weight
        )
        return finish_outputs(*run_layer(True, first, dict(vectors=list(vectors) + [inner_bias])))
    whole = lambda part: lax.all_gather(part, AXES, axis=0, tiled=True)
    wide = whole(jnp.concatenate((query_weight, key_weight, value_weight), axis=1))
    eights = [whole(vector).reshape(4, 8, 16) for vector in vectors]
    small = jnp.zeros((4, 8, 16, SMALL), bf16)
    for row, vector in enumerate(eights):
        for at in range(8):
            small = small.at[:, at, row, 16 * at : 16 * at + 16].set(vector[:, at])
    pairs = whole(inner_bias).reshape(4, 4, 2, 64)
    pairs_at = small.reshape(4, 4, 2, 16, SMALL)
    for at in range(2):
        pairs_at = pairs_at.at[:, :, at, 6, 64 * at : 64 * at + 64].set(pairs[:, :, at])
    wide = jnp.concatenate((wide.reshape(4, 8, 16, WIDTH), pairs_at.reshape(4, 8, 16, SMALL)), axis=-1)
    weights = dict(
        wa=wide.reshape(SLOTS + (16, WIDTH + SMALL)),
        wi=whole(jnp.concatenate((inner_weight, mixer_weight), axis=1)).reshape(SLOTS + (16, 5 * D)),
        wo=whole(outer_weight).reshape(SLOTS + (64, D)),
    )
    out, g_tok, d_a, d_i, d_o, o_v = run_layer(False, first, weights)
    owned = lambda part: lax.psum_scatter(part, AXES, scatter_dimension=0, tiled=True)
    g_a = owned(d_a.astype(f32).reshape(D, WIDTH))
    g_q, g_k, g_v = (g_a[:, k * D : (k + 1) * D] for k in range(3))
    g_i = owned(d_i.astype(f32).reshape(D, 5 * D))
    g_i, g_m = g_i[:, : 4 * D], g_i[:, 4 * D :]
    g_o = owned(d_o.astype(f32).reshape(4 * D, D))
    six = [owned(o_v[k]) for k in range(6)]
    g_bias_in = owned(o_v[8:12].reshape(-1))
    return (
        out, g_tok, six[0], six[1], g_q, g_k, g_v, g_m, six[2], six[3], six[4], g_i, g_bias_in, g_o, six[5],
    )


def solution(mesh):
    rows, flat, both = P(AXES, None), P(AXES), P("dp")
    in_specs = (rows, rows, both, flat, flat, rows, rows, rows, rows, flat, flat, flat, rows, flat, rows, flat)
    out_specs = (rows, rows, flat, flat, rows, rows, rows, rows, flat, flat, flat, rows, flat, rows, flat)
    return jax.shard_map(on_device, mesh=mesh, in_specs=in_specs, out_specs=out_specs, check_vma=False)
```

time: 1600 us -> 145 us (0.09); the launches traced: 1580 us -> 144 us
  waiting for transfers between devices: 694 us -> 0 us
  local copies, waits for them, and re-layouts: 332 us -> 0 us
  blocking collectives: 252 us -> 0 us
  matrix products: 144 us -> 0 us
  Pallas kernels: 0 us -> 143 us
  other arithmetic: 140 us -> 0 us
  between operations: 17.9 us -> 1.47 us
    reduce_scatter x8 -> x0, waiting for transfers between devices: 691 us -> none  [the longest x1 140 us: on_device(): lax.psum_scatter(grad_weight_in, ('dp', 'fsdp'), scatter_dimension=0, til...]
    all_gather x6 -> x0, blocking collectives: 173 us -> none  [the longest x1 42.5 us: gather_mixer(): lax.all_gather(query_weight, ('dp', 'fsdp'), axis=0, tiled=True)]
    dot_general x60 -> x0, matrix products: 144 us -> none  [the longest x1 24.7 us: on_device(): jnp.dot(normal_two, weight_in, preferred_element_type=jnp.float32)]
    pallas_call x0 -> x2, Pallas kernels: none -> 143 us  [the longest x1 139 us: run_layer(): pl.pallas_call(functools.partial(layer_kernel, fast, dict(operands, **out...]
    unnamed x2 -> x0, blocking collectives: 79.5 us -> none
    broadcast_in_dim x44 -> x0, local copies, waits for them, and re-layouts: 48.2 us -> none  [spread(): jnp.broadcast_to(values[:, :, None], extent[:2] + (stride,) + extent[2:])]
    reshape x36 -> x0, local copies, waits for them, and re-layouts: 48 us -> none  [the longest x8 15.4 us: local_return(): partner_part.reshape(paired)[:, ::-1].reshape(blocks, BLOCK, HEADS, HEAD)]
    unnamed x430 -> x0, local copies, waits for them, and re-layouts: 45.5 us -> none
  transfers between devices with their start and end apart: 10 -> 0, of which waited for: 6 -> 0; matrix products, arithmetic and copies ran while one was open for 26% -> 0% of each run, Pallas kernels for 0% -> 0%
where the time goes in v1:
time: 145 us; the launch traced here: 144 us
  Pallas kernels  143 us (99%)
  between operations  1.47 us (1%)
    pallas_call x1, Pallas kernels, run_layer(): pl.pallas_call(functools.partial(layer_kernel, fast, dict(operands, **out...  139 us
    pallas_call x1, Pallas kernels, finish_outputs(): pl.pallas_call(final_kernel, out_shape=outs, in_specs=[hbm] * 2 + [vmem]...  4.24 us

profile of v1, /device:TPU:0, one launch (start us, length us, event | category | flops | bytes accessed | tf_op | source)
XLA Modules:
  0.0 144.5 jit_solution(14837698042550552343)
XLA Ops:
  1.3 138.8 %shard_map.316 = (bf16[1024,512]{1,0:T(8,128)(2,1)}, bf16[1024,512]{1,0:T(8,128)(2,1)}, f32[16,1536]{1,0:T(8,128)}, f32[16,2560]{1,0:T(8,128)}, f32[64,512]{1,0:T(8,128)}, /*index=5*/f32[16,128]{1,0:T(8,128)}) custom-call(bf16[1024,512]{1,0:T(8,128)(2,1)} %refs_0_.1, bf16[1024,512]{1,0:T(8,128)(2,1)} %refs_1_.1, bf16[16,512]{1,0:T(8,128)(2,1)} %refs_2_.1, ...), custom_call_target="tpu_custom_call" | custom-call | tf_op jit(solution)/shard_map/pallas_call | solution.py:1011
  140.1 4.2 %shard_map.317 = (bf16[1024,512]{1,0:T(8,128)(2,1)}, bf16[1024,512]{1,0:T(8,128)(2,1)}, f32[16]{0:T(128)}, f32[16]{0:T(128)}, f32[16,512]{1,0:T(8,128)}, /*index...) custom-call(bf16[1024,512]{1,0:T(8,128)(2,1)} %get-tuple-element.21., ...), custom_call_target="tpu_custom_call" | custom-call | tf_op jit(solution)/shard_map/pallas_call | solution.py:1030

commit v2 on v1

v2 whole, which is shorter than its diff:
```python
import functools
import math
import types

import jax
import jax.numpy as jnp
import numpy as np
from jax import lax
from jax.experimental import pallas as pl
from jax.experimental.pallas import tpu as pltpu
from jax.sharding import PartitionSpec as P

D = 512
HEADS = 8
HEAD = 64
BLOCK = 16
SHORT = 1024
LEVELS = 8
TILE = 128
TOGETHER = 5
CHUNK = 256
STACK = 2 * SHORT
WIDTH = 3 * D
SMALL = 128
GROUP = 3 * TILE
PAIRS = HEADS // 2
FEED_STEPS = 2
AXES = ("dp", "fsdp")
MESH = pl.DeviceIdType.MESH
SLOTS = (4, 2, 2, 2)

norm_eps = 1e-05
far_off = -1e30
f32 = jnp.float32
bf16 = jnp.bfloat16

FIRST = [STACK - (STACK >> level) for level in range(LEVELS + 1)]
LOW_TOP = 4


def member_matrix():
    token = np.arange(SHORT)
    rows = []
    for level, span in ((1, 256), (2, 512), (3, 1024)):
        rows.append((token[None] % span) >> level == np.arange(TILE)[:, None])
    for level in range(LOW_TOP, LEVELS):
        rows.append(token[None] >> level == np.arange(SHORT >> level)[:, None])
    rows.append(np.zeros((8, SHORT), bool))
    return np.concatenate(rows).astype(np.float32)


def block_bias():
    key = np.arange(32)[:, None]
    query = np.arange(2 * TILE)[None]
    across = (key < BLOCK) != (query % 32 < BLOCK)
    last = np.where(query % TILE >= 96, ~across, across)
    kinds = [np.ones_like(across), across, last]
    return np.stack([np.where(kind, 0.0, far_off) for kind in kinds]).astype(np.float32)


def head_mask():
    lane = np.arange(TILE)[None]
    side = np.arange(2 * TILE)[:, None] // TILE
    return (lane // HEAD == side).astype(np.float32)


def group_mask():
    key = np.arange(TILE)[:, None]
    query = np.arange(2 * TILE)[None]
    return (key // 32 == query % TILE // 32).astype(np.float32)


def top_level_of():
    index = np.arange(TILE)
    return np.minimum(LOW_TOP + (index >= 64) * 1 + (index >= 96) * 1 + (index >= 112) * 1, 7)


def nn(a, b):
    return lax.dot_general(a, b, (((1,), (0,)), ((), ())), preferred_element_type=f32)


def nt(a, b):
    return lax.dot_general(a, b, (((1,), (1,)), ((), ())), preferred_element_type=f32)


def tn(a, b):
    return lax.dot_general(a, b, (((0,), (0,)), ((), ())), preferred_element_type=f32)


def normalize(values):
    center = values - jnp.mean(values, axis=-1, keepdims=True)
    inverse = lax.rsqrt(jnp.mean(center * center, axis=-1, keepdims=True) + norm_eps)
    return center * inverse, inverse


def normalize_back(grad_normed, normed, inverse):
    return inverse * (
        grad_normed
        - jnp.mean(grad_normed, axis=-1, keepdims=True)
        - normed * jnp.mean(grad_normed * normed, axis=-1, keepdims=True)
    )


def gelu_both(v):
    mag = jnp.abs(v) * (0.5**0.5)
    t = 1.0 / (1.0 + 0.3275911 * mag)
    gauss = jnp.exp(-0.5 * v * v)
    poly = t * (
        0.254829592
        + t * (-0.284496736 + t * (1.421413741 + t * (-1.453152027 + t * 1.061405429)))
    )
    tail = 0.5 * poly * gauss
    cdf = jnp.where(v < 0, tail, 1.0 - tail)
    return v * cdf, cdf + v * gauss * ((2 * math.pi) ** -0.5)


def split3(values):
    one = values.astype(bf16)
    rest = values - one.astype(f32)
    two = rest.astype(bf16)
    return one, two, (rest - two.astype(f32)).astype(bf16)


def split2(values):
    one = values.astype(bf16)
    return one, (values - one.astype(f32)).astype(bf16)


class Place:
    def __init__(self):
        self.dp = lax.axis_index("dp")
        self.fs = lax.axis_index("fsdp")
        self.z, self.y = self.dp // 2, self.dp % 2
        self.x, self.c = self.fs // 2, self.fs % 2
        self.oy, self.ox, self.oc = 1 - self.y, 1 - self.x, 1 - self.c
        self.zs = [lax.rem(self.z + step, 4) for step in (1, 2, 3)]
        self.by_core = (self.dp, self.x * 2 + self.oc)
        self.by_x = (self.dp, self.ox * 2 + self.c)
        self.by_y = (self.z * 2 + self.oy, self.fs)
        self.by_z = [(z * 2 + self.y, self.fs) for z in self.zs]
        ys, xs, cs = (self.y, self.oy), (self.x, self.ox), (self.c, self.oc)
        self.plane = [(self.z * 2 + ys[k // 4], xs[k // 2 % 2] * 2 + cs[k % 2]) for k in range(1, 8)]


def remote(src, dst, send, recv, device):
    return pltpu.make_async_remote_copy(
        src_ref=src, dst_ref=dst, send_sem=send, recv_sem=recv, device_id=device, device_id_type=MESH
    )


def arrived(ref, sem, device):
    remote(ref, ref, sem, sem, device).wait_recv()


def gone(ref, sem, device):
    remote(ref, ref, sem, sem, device).wait_send()


class Gather:
    def __init__(self, ref, lanes, p, sems):
        self.at = lambda z, y, x: ref.at[z, y, x, p.c, :, lanes]
        self.p, self.sems = p, sems

    def advance(self, step):
        p, at, sems = self.p, self.at, self.sems
        low, high, both, full = pl.ds(0, 2), pl.ds(2, 2), pl.ds(0, 2), pl.ds(0, 4)
        if step:
            ref = (at(pl.ds(0, 3), p.y, p.x), at(full, p.y, p.x), at(full, both, p.x), at(full, both, both))[step - 1]
            arrived(ref, sems.at[step - 1], p.by_core)
        if step == 4:
            gone(at(pl.ds(0, 3), p.y, p.x), sems.at[4], p.by_core)
            gone(at(pl.ds(0, 3), both, both), sems.at[5], p.by_core)
            gone(at(full, both, both), sems.at[6], p.by_core)
            return
        if step == 0:
            parts = [(at(p.z, p.y, p.x), device) for device in p.by_z]
        elif step == 1:
            parts = [(at(low, p.y, p.x), p.by_x), (at(high, p.y, p.x), p.by_y)]
        elif step == 2:
            parts = [(at(low, p.y, both), p.by_y), (at(high, both, p.x), p.by_x)]
        else:
            parts = [(at(full, both, both), p.by_core)]
        for part, device in parts:
            remote(part, part, sems.at[(4, 5, 5, 6)[step]], sems.at[step], device).start()


class Total:
    def __init__(self, ref, lanes, part, p, sems, bufs):
        self.ref, self.lanes, self.part, self.p, self.sems, self.bufs = ref, lanes, part, p, sems.at[part], bufs

    def add(self, index, buf):
        at = index + (self.p.c, slice(None), self.lanes)
        self.ref[at] = self.ref[at] + buf

    def advance(self, step):
        p, part, sems = self.p, self.part, self.sems
        from_core, one_a, one_b, two_a, two_b, far = self.bufs
        at = lambda z, y, x, c: self.ref.at[z, y, x, c, :, self.lanes]
        low, high, both, full, every = pl.ds(0, 2), pl.ds(2, 2), pl.ds(0, 2), pl.ds(0, 4), slice(None)
        if step:
            ref = (from_core.at[part], from_core.at[part, both], from_core.at[part, 0])[step - 1]
            arrived(ref, sems.at[step - 1], p.by_core)
        if step == 0:
            sends = [(at(full, both, both, p.oc), from_core, p.by_core)]
        elif step == 1:
            for z in range(4):
                self.add((z, every, every), from_core[part, z])
            sends = [(at(low, p.oy, both, p.c), one_a, p.by_y), (at(high, both, p.ox, p.c), one_b, p.by_x)]
        elif step == 2:
            for z in range(2):
                self.add((z, p.y, every), one_a[part, z])
                self.add((2 + z, every, p.x), one_b[part, z])
            sends = [(at(low, p.y, p.ox, p.c), two_a, p.by_x), (at(high, p.oy, p.x, p.c), two_b, p.by_y)]
        else:
            for z in range(2):
                self.add((z, p.y, p.x), two_a[part, z])
                self.add((2 + z, p.y, p.x), two_b[part, z])
            for k, z in enumerate(p.zs):
                remote(at(z, p.y, p.x, p.c), far.at[part, k], sems.at[6], sems.at[3], p.by_z[k]).start()
            return
        for src, buf, device in sends:
            remote(src, buf.at[part], sems.at[(4, 5, 5)[step]], sems.at[step], device).start()

    def finish(self, out):
        p, sems, far, part = self.p, self.sems, self.bufs[5], self.part
        arrived(far.at[part], sems.at[3], p.by_core)
        total = self.ref[p.z, p.y, p.x, p.c, :, self.lanes].astype(f32)
        out[:, self.lanes] = functools.reduce(jnp.add, [far[part, k].astype(f32) for k in range(3)], total)
        gone(self.bufs[0].at[part], sems.at[4], p.by_core)
        gone(self.bufs[0].at[part, pl.ds(0, 3)], sems.at[5], p.by_core)
        gone(far.at[part], sems.at[6], p.by_core)


class TotalRows:
    def __init__(self, ref, part, p, sems, bufs):
        self.ref, self.part, self.p, self.sems, self.bufs = ref, part, p, sems.at[part], bufs

    def add(self, index, buf):
        at = (self.part,) + index
        self.ref[at] = self.ref[at] + buf

    def advance(self, step):
        p, part, sems = self.p, self.part, self.sems
        from_core, one_a, one_b, two_a, two_b, _ = self.bufs
        both, every, low, high = pl.ds(0, 2), slice(None), pl.ds(0, 32), pl.ds(32, 32)
        at = lambda y, x, c, *rows: self.ref.at[(part, y, x, c) + rows]
        if step:
            ref = (from_core.at[part], from_core.at[part, 0], from_core.at[part, 0, 0])[step - 1]
            arrived(ref, sems.at[step - 1], p.by_core)
        if step == 0:
            sends = [(at(both, both, p.oc), from_core, p.by_core)]
        elif step == 1:
            self.add((every, every, p.c), from_core[part])
            sends = [(at(p.oy, both, p.c, low), one_a, p.by_y), (at(both, p.ox, p.c, high), one_b, p.by_x)]
        elif step == 2:
            self.add((p.y, every, p.c, low), one_a[part])
            self.add((every, p.x, p.c, high), one_b[part])
            sends = [(at(p.y, p.ox, p.c, low), two_a, p.by_x), (at(p.oy, p.x, p.c, high), two_b, p.by_y)]
        else:
            self.add((p.y, p.x, p.c, low), two_a[part])
            self.add((p.y, p.x, p.c, high), two_b[part])
            return
        for src, buf, device in sends:
            remote(src, buf.at[part], sems.at[(3, 4, 4)[step]], sems.at[step], device).start()

    def settle(self):
        gone(self.bufs[0].at[self.part], self.sems.at[3], self.p.by_core)
        gone(self.bufs[5], self.sems.at[4], self.p.by_core)


class TotalVectors:
    def __init__(self, ref, p, sems, got, mid, far):
        self.ref, self.p, self.sems, self.got, self.mid, self.far = ref, p, sems, got, mid, far

    def begin(self):
        for k, device in enumerate(self.p.plane):
            remote(self.ref, self.got.at[k], self.sems.at[1], self.sems.at[0], device).start()

    def second(self):
        arrived(self.got, self.sems.at[0], self.p.by_core)
        self.mid[...] = functools.reduce(jnp.add, [self.got[k] for k in range(7)], self.ref[...])
        for k, device in enumerate(self.p.by_z):
            remote(self.mid, self.far.at[k], self.sems.at[3], self.sems.at[2], device).start()

    def finish(self):
        arrived(self.far, self.sems.at[2], self.p.by_core)
        gone(self.got, self.sems.at[1], self.p.by_core)
        gone(self.far, self.sems.at[3], self.p.by_core)
        return functools.reduce(jnp.add, [self.far[k] for k in range(3)], self.mid[...])


def layer_kernel(fast, kinds, *refs):
    shapes = dict(kinds, **scratch_list(fast))
    r, left = types.SimpleNamespace(), list(refs)
    for name, kind in shapes.items():
        amount = len(kind) if isinstance(kind, list) else 1
        taken, left = left[:amount], left[amount:]
        setattr(r, name, taken if isinstance(kind, list) else taken[0])
    assert not left
    p = Place()
    tok, cot = r.tok, r.cot
    member, spread = r.member, r.spread
    stack, probs, out_t, mix_t = r.stack, r.probs, r.out_t, r.mix_t
    lse_s, share, inner_s, total_h = r.lse_s, r.share, r.inner_s, r.total_h
    resid, n_one, n_two = r.resid, r.n_one, r.n_two
    acc_out, acc_two = r.acc_out, r.acc_two
    g_att, g_num = r.g_att, r.g_num
    g_mix, weight = g_num.at[0:SHORT], r.weight
    grad_kv = r.grad_kv
    vec_a, vec_b = r.vec_a, r.vec_b
    wa, wi, wo = r.wa, r.wi, r.wo
    da, di, do = (r.da, r.di, r.do) if fast else (r.o_a, r.o_i, r.o_o)
    grad_qt = out_t

    def fetch(src, dst, slot):
        copy = pltpu.make_async_copy(src, dst, r.in_sem.at[slot])
        copy.start()
        return copy

    def taken(ref, slot):
        pltpu.make_async_copy(ref, ref, r.in_sem.at[slot]).wait()

    if fast:
        small_in = [fetch(ref, kept, k) for k, (ref, kept) in enumerate(zip(r.vectors, r.vec_in))]
        own_a, own_i, own_o = (ref.at[p.z, p.y, p.x, p.c] for ref in (wa, wi, wo))
        for pair in range(PAIRS):
            for slot, ref in enumerate((r.wq_s, r.wk_s, r.wv_s)):
                there = pl.ds(SMALL + pair * GROUP + slot * TILE, TILE)
                fetch(ref.at[:, pl.ds(pair * TILE, TILE)], own_a.at[:, there], 7)
        fetch(r.wi_s, own_i.at[:, pl.ds(0, 4 * D)], 8)
        fetch(r.wm_s, own_i.at[:, pl.ds(4 * D, D)], 8)
        fetch(r.wo_s, own_o, 9)
    tok_in = fetch(r.tok_h, tok, 10)
    rest_in = [
        fetch(src, dst, 11 + k)
        for k, (src, dst) in enumerate(
            ((r.member_h, member), (r.head_h, r.head_m), (r.group_h, r.group_m), (r.bias_h, r.bias), (r.cot_h, cot), (r.spread_h, spread))
        )
    ]

    other = p.fs // 2 * 2 + 1 - p.fs % 2
    pairs_at = (1 - p.fs // 2) * 2
    side = p.fs % 2
    barrier = pltpu.get_barrier_semaphore()
    reach = [(p.dp, other), (p.dp, pairs_at), (p.dp, pairs_at + 1)]
    if fast:
        reach += p.plane[3:] + p.by_z
    for device in reach:
        pl.semaphore_signal(barrier, inc=1, device_id=device, device_id_type=MESH)
    if fast:
        whose = p.dp * 4 + p.fs
        for copy in small_in:
            copy.wait()
        at = lax.broadcasted_iota(jnp.int32, (HEAD, SMALL), 0)
        lane = lax.broadcasted_iota(jnp.int32, (HEAD, SMALL), 1)
        rows = [ref[...].astype(f32).reshape(1, 16) for ref in r.vec_in[:6]]
        rows = jnp.concatenate(rows + [jnp.zeros((10, 16), f32)], axis=0).astype(bf16)
        spot = (lane[0:16] == at[0:16] + 16 * (whose % 8)).astype(f32).astype(bf16)
        own = nn(rows, spot)
        bias = jnp.concatenate([r.vec_in[6][...].astype(f32).reshape(1, HEAD), jnp.zeros((15, HEAD), f32)], axis=0)
        spot = (lane == at + HEAD * (whose % 2)).astype(f32).astype(bf16)
        own_bias = nn(bias.astype(bf16), spot)
        own = jnp.concatenate([own[0:6], own_bias[0:1], jnp.zeros((9, SMALL), f32)], axis=0)
        own_a[:, 0:SMALL] = own.astype(bf16)
    if fast:
        taken(own_a.at[:, pl.ds(SMALL, WIDTH)], 7)
    pl.semaphore_wait(barrier, len(reach))


    def first_norm(step, carry):
        at = pl.ds(pl.multiple_of(step * CHUNK, CHUNK), CHUNK)
        acc_two[at, :] = normalize(tok[at, :].astype(f32))[0]
        return carry

    if fast:
        spans = [(wa, 0, SMALL + GROUP)] + [(wa, SMALL + k * GROUP, GROUP) for k in range(1, PAIRS)]
        spans += [(wi, 0, 1280), (wi, 1280, 1280), (wo, 0, 256), (wo, 256, 256)]
        gathers = [
            Gather(ref, pl.ds(lo, wide), p, r.g_sem.at[k]) for k, (ref, lo, wide) in enumerate(spans)
        ]

    def pump(*events):
        if fast:
            for k, step in events:
                gathers[k].advance(step)

    pump((0, 0), (1, 0), (2, 0), (3, 0))
    tok_in.wait()
    lax.fori_loop(0, SHORT // CHUNK, first_norm, 0)
    if fast:
        taken(own_i, 8)
        taken(own_o, 9)
    pump((0, 1), (1, 1), (0, 2), (2, 1), (1, 2), (0, 3), (3, 1), (4, 0), (2, 2), (0, 4))
    for copy in rest_in:
        copy.wait()

    def rows_of(ref, lo, width):
        return ref[:, :, :, :, :, lo : lo + width].reshape(512, width)

    small = wa[:, :, :, :, :, 0:SMALL].astype(f32)
    by_z = jnp.sum(small, axis=(1, 2, 3))
    param = jnp.concatenate([by_z[z] for z in range(4)], axis=1)
    r.param[...] = param
    by_pair = jnp.sum(small, axis=3)
    r.bias_in[...] = jnp.concatenate(
        [by_pair[z, y, x, 6:7, :] for z in range(4) for y in range(2) for x in range(2)], axis=1
    )
    vec_a[...] = jnp.zeros_like(vec_a)
    vec_b[...] = jnp.zeros_like(vec_b)
    r.lanes_in[...] = jnp.zeros_like(r.lanes_in)

    gain_one, shift_one = r.param[0:1, :], r.param[1:2, :]

    def scale_shift(step, carry):
        at = pl.ds(pl.multiple_of(step * CHUNK, CHUNK), CHUNK)
        n_one[at, :] = (acc_two[at, :] * gain_one + shift_one).astype(bf16)
        return carry

    lax.fori_loop(0, SHORT // CHUNK, scale_shift, 0)

    index = lax.broadcasted_iota(jnp.int32, (TILE, 1), 0)
    steps_down = jnp.where(
        index < 64, 1 / 16, jnp.where(index < 96, 1 / 32, jnp.where(index < 112, 1 / 64, 1 / 128))
    ).astype(f32)

    def chunk_rows(step):
        one = pl.ds(pl.multiple_of(FIRST[1] + step * 128, 128), 128)
        two = pl.ds(pl.multiple_of(FIRST[2] + step * 64, 64), 64)
        return one, two, pl.ds(pl.multiple_of(FIRST[3] + step * 32, 32), 32)

    def chunk_members(chunk):
        near = [member[lo:hi, 0:CHUNK] for lo, hi in ((0, 128), (128, 192), (256, 288))]
        return near + [member[lo:hi, chunk] for lo, hi in ((384, 448), (448, 480), (480, 496), (496, 512))]

    lane_group = lax.broadcasted_iota(jnp.int32, (32, 2 * TILE), 1) % TILE // 32

    def squeeze(tall):
        parts = [tall[32 * part : 32 * part + 32, :] for part in range(4)]
        return jnp.where(
            lane_group < 2,
            jnp.where(lane_group == 0, parts[0], parts[1]),
            jnp.where(lane_group == 2, parts[2], parts[3]),
        )

    def widen(low):
        return jnp.concatenate([low, low, low, low], axis=0) * r.group_m[...]

    def two_heads(low):
        return jnp.concatenate([low, low], axis=0) * r.head_m[...]

    top_lane = lax.broadcasted_iota(jnp.int32, (HEADS, TILE), 1)
    top_scale_t = jnp.where(
        top_lane < 64, 1 / 16, jnp.where(top_lane < 96, 1 / 32, jnp.where(top_lane < 112, 1 / 64, 1 / 128))
    ).astype(f32)

    def tile_scale(tile):
        return jnp.where(
            tile < 8, 1.0, jnp.where(tile < 12, 0.5, jnp.where(tile < 14, 0.25, 0.125))
        ).astype(f32)

    def lanes_at(start, wide):
        return pl.ds(pl.multiple_of(start, TILE), wide)

    def tile_forward(tile, pair, kind, scale_t):
        rows = lanes_at(tile * TILE, TILE)
        at = lambda slot: (rows, lanes_at(pair * GROUP + slot * TILE, TILE))
        score = squeeze(nt(stack[at(1)], two_heads(stack[at(0)]))) + r.bias[kind]
        peak = jnp.max(score, axis=0, keepdims=True)
        prob = jnp.exp(score - peak)
        total = jnp.sum(prob, axis=0, keepdims=True)
        low = (prob * (1.0 / total)).astype(bf16)
        probs[tile, :, lanes_at(pair * 2 * TILE, 2 * TILE)] = low
        log_total = peak + jnp.log(total)
        lse_s[pair, 0:1, rows] = log_total[:, :TILE]
        lse_s[pair, 1:2, rows] = log_total[:, TILE:]
        made = nn(stack[at(2)].T, widen(low))
        head = pl.multiple_of(pair * TILE, TILE)
        out_t[pl.ds(head, HEAD), rows] = (made[:HEAD, :TILE] * scale_t).astype(bf16)
        out_t[pl.ds(head + HEAD, HEAD), rows] = (made[HEAD:, TILE:] * scale_t).astype(bf16)

    far_s, far_r = r.far_s, r.far_r
    far_out = [
        remote(far_s.at[0], far_r.at[0], r.far_sem.at[1], r.far_sem.at[0], (p.dp, other)),
        remote(far_s.at[1], far_r.at[1 + side], r.far_sem.at[1], r.far_sem.at[0], (p.dp, pairs_at)),
        remote(far_s.at[1], far_r.at[1 + side], r.far_sem.at[1], r.far_sem.at[0], (p.dp, pairs_at + 1)),
    ]
    tops_acc = acc_out

    def pair_forward(pair, carry):
        def pump_here(*plan):
            for number, events in enumerate(plan):
                if events:
                    pl.when(pair == number)(functools.partial(pump, *events))

        pump_here([], [(1, 4), (5, 1)], [(2, 4)], [(3, 4)])
        lanes = lanes_at(pair * GROUP, GROUP)
        made = nn(n_one[...], wa[:, :, :, :, :, lanes_at(SMALL + pair * GROUP, GROUP)].reshape(D, GROUP))
        first = lax.broadcasted_iota(jnp.int32, (1, GROUP), 1)
        stack[0:SHORT, lanes] = (made * jnp.where(first < TILE, 0.125, 1.0)).astype(bf16)
        key_like = first < 2 * TILE
        pump_here([(1, 3), (3, 2), (5, 0)])
        tops_acc[0:TILE, 0:GROUP] = jnp.zeros((TILE, GROUP), f32)

        def pool(step, carry):
            chunk = pl.ds(pl.multiple_of(step * CHUNK, CHUNK), CHUNK)
            made = nn(jnp.concatenate(chunk_members(chunk), axis=0), stack[chunk, lanes])
            to = chunk_rows(step)
            for level, (lo, hi) in enumerate(((0, 128), (128, 192), (192, 224))):
                scale = jnp.where(key_like, 0.5 ** (level + 1), 1.0)
                stack[to[level], lanes] = (made[lo:hi] * scale).astype(bf16)
            tops_acc[0:TILE, 0:GROUP] += made[224:352]
            return carry

        lax.fori_loop(0, SHORT // CHUNK, pool, 0)
        stack[FIRST[4] : STACK, lanes] = (
            tops_acc[0:TILE, 0:GROUP] * jnp.where(key_like, steps_down, 1.0)
        ).astype(bf16)
        theirs = lanes_at(pair * GROUP + TILE, 2 * TILE)
        mine = lanes_at(pair * 2 * TILE, 2 * TILE)
        far_s[0, :, mine] = stack[2016:2032, theirs]
        far_s[1, :, mine] = stack[2032:2048, theirs]

        @pl.when(pair == PAIRS - 1)
        def _():
            for copy in far_out:
                copy.start()

        def near_tiles(group, carry):
            for one in range(TOGETHER):
                tile = group * TOGETHER + one
                tile_forward(tile, pair, jnp.where(tile < 8, 0, 1), tile_scale(tile))
            return carry

        pump_here([(2, 3), (4, 1)], [(4, 3), (6, 1)], [(5, 3), (7, 1)], [(6, 3)])
        lax.fori_loop(0, 15 // TOGETHER, near_tiles, 0)
        pump_here([(3, 3), (4, 2), (6, 0)], [(5, 2), (7, 0)], [(4, 4), (6, 2)], [(7, 2)])
        return carry

    lax.fori_loop(0, PAIRS, pair_forward, 0)
    arrived(far_r, r.far_sem.at[0], p.by_core)
    gone(far_r, r.far_sem.at[1], p.by_core)
    last_rows = jnp.concatenate([far_r[1].astype(f32)[:8], far_r[2].astype(f32)[:8]], axis=0).astype(bf16)
    for pair in range(PAIRS):
        theirs = slice(pair * GROUP + TILE, (pair + 1) * GROUP)
        mine = slice(pair * 2 * TILE, (pair + 1) * 2 * TILE)
        stack[2016:2032, theirs] = far_r[0, :, mine]
        stack[2032:2048, theirs] = last_rows[:, mine]
    for pair in range(PAIRS):
        tile_forward(15, pair, 2, top_scale_t[0:1, :])
    idle = jnp.where(r.row_length[0] > SHORT, 0.0, far_off)
    lse_s[:, :, 1920:2048] = lse_s[:, :, 1920:2048] + jnp.where(top_lane[0:2] >= 96, idle, 0.0)

    edges = (0, 64, 96, 112, 128)

    def windows(step):
        one = pl.ds(pl.multiple_of(FIRST[1] + step * TILE, TILE), TILE)
        two = pl.ds(pl.multiple_of(FIRST[2] + step // 2 * TILE, TILE), TILE)
        return one, two, pl.ds(FIRST[3], TILE), pl.ds(FIRST[4], TILE)

    def per_level(step, chunk):
        one = member[0:512, chunk]

        def for_head(head):
            rows = []
            spans = [(0, 128), (128, 256), (256, 384), (384, 448), (448, 480), (480, 496), (496, 512)]
            for level, (lo, hi) in enumerate(spans, 1):
                rows.append(one[lo:hi] * share[level, head : head + 1, chunk].astype(bf16))
            return jnp.concatenate(rows, axis=0)

        return for_head

    def lse_of(lanes):
        return jnp.concatenate([lse_s[pair, :, lanes] for pair in range(PAIRS)], axis=0)

    def combine(step, carry):
        chunk = pl.ds(pl.multiple_of(step * CHUNK, CHUNK), CHUNK)
        wins = windows(step)
        logs = [lse_of(chunk)]
        for slot in range(3):
            parts = jnp.concatenate(split3(lse_of(wins[slot])), axis=0)
            made = nn(parts, member[slot * TILE : (slot + 1) * TILE, chunk])
            logs.append(made[0:8] + made[8:16] + made[16:24] + (slot + 1) * math.log(2.0))
        top = lse_of(wins[3])
        parts = []
        for slot in range(4):
            inside = (top_lane >= edges[slot]) & (top_lane < edges[slot + 1])
            parts += list(split3(jnp.where(inside, top, 0.0)))
        made = nn(jnp.concatenate(parts, axis=0), member[384:512, chunk])
        for slot in range(4):
            b = slot * 24
            logs.append(made[b : b + 8] + made[b + 8 : b + 16] + made[b + 16 : b + 24] + (slot + 4) * math.log(2.0))
        peak = functools.reduce(jnp.maximum, logs)
        den = functools.reduce(jnp.add, [jnp.exp(one - peak) for one in logs])
        lse = peak + jnp.log(den)
        for level in range(LEVELS):
            share[level, :, chunk] = jnp.exp(logs[level] - lse)
        for_head = per_level(step, chunk)
        for head in range(HEADS):
            at = slice(head * HEAD, (head + 1) * HEAD)
            coarse = jnp.concatenate([out_t[at, win] for win in wins], axis=1)
            made = nn(coarse, for_head(head))
            made = made + share[0, head : head + 1, chunk] * out_t[at, chunk].astype(f32)
            mix_t[at, chunk] = made.astype(bf16)
        return carry

    lax.fori_loop(0, SHORT // CHUNK, combine, 0)
    pump((7, 3), (5, 4), (6, 4))

    bias_mix, gain_two = r.param[2:3, :], r.param[3:4, :]
    shift_two, bias_out = r.param[4:5, :], r.param[5:6, :]
    w_mix = rows_of(wi, 4 * D, D)
    resid[...] = tn(mix_t[...], w_mix)

    def second_norm(step, carry):
        at = pl.ds(pl.multiple_of(step * CHUNK, CHUNK), CHUNK)
        mid = tok[at, :].astype(f32) + resid[at, :] + bias_mix
        resid[at, :] = mid
        normed, _ = normalize(mid)
        n_two[at, :] = (normed * gain_two + shift_two).astype(bf16)
        return carry

    lax.fori_loop(0, SHORT // CHUNK, second_norm, 0)
    pump((7, 4))

    hid, g_pre = grad_kv.at[0:SHORT, 0:D], grad_kv.at[0:SHORT, D : 2 * D]
    acc_out[...] = jnp.zeros_like(acc_out)
    acc_two[...] = jnp.zeros_like(acc_two)

    def total_i(part):
        return Total(di, lanes_at(part * 512, 512), part, p, r.si[0], r.si[1:])

    def total_o(part):
        return TotalRows(do, part, p, r.so[0], r.so[1:7])

    def onward(total, *steps):
        if fast:
            for part, step in steps:
                if isinstance(part, int):
                    total(part).advance(step)
                else:
                    pl.when(part >= 0)(lambda: total(part).advance(step))

    def feed(part, carry):
        lanes = pl.ds(pl.multiple_of(part * 512, 512), 512)
        w_in = wi[:, :, :, :, :, lanes].reshape(512, 512)
        w_out = wo[part].reshape(512, 512)
        b_in = r.bias_in[:, lanes]
        sums = jnp.zeros((1, 512), f32)
        for step in range(FEED_STEPS):
            at = pl.ds(step * (SHORT // FEED_STEPS), SHORT // FEED_STEPS)
            act, slope = gelu_both(nn(n_two[at, :], w_in) + b_in)
            act = act.astype(bf16)
            hid[at, :] = act
            back = (nt(cot[at, :], w_out) * slope).astype(bf16)
            g_pre[at, :] = back
            acc_out[at, :] += nn(act, w_out)
            acc_two[at, :] += nt(back, w_in)
            sums = sums + jnp.sum(back.astype(f32), axis=0, keepdims=True)
            if step == 0:
                onward(total_i, (part - 2, 2), (part - 1, 1))
                onward(total_o, (part - 2, 2), (part - 1, 1))
        r.lanes_in[0:1, lanes] = sums
        di[:, :, :, :, :, lanes] = tn(n_two[...], g_pre[...]).astype(bf16).reshape(4, 2, 2, 2, 16, 512)
        do[part] = tn(hid[...], cot[...]).astype(bf16).reshape(2, 2, 2, 64, 512)
        if fast:
            onward(total_i, (part - 2, 3), (part, 0))
            onward(total_o, (part - 2, 3), (part, 0))
        return carry

    lax.fori_loop(0, 4, feed, 0)

    def middle(step, carry):
        at = pl.ds(pl.multiple_of(step * CHUNK, CHUNK), CHUNK)
        mid = resid[at, :]
        n_two[at, :] = (mid + acc_out[at, :] + bias_out).astype(bf16)
        normed, inverse = normalize(mid)
        g_two = acc_two[at, :]
        c = cot[at, :].astype(f32)
        g_mid = c + normalize_back(g_two * gain_two, normed, inverse)
        resid[at, :] = g_mid
        low = g_mid.astype(bf16)
        g_att[at, :] = low
        vec_b[0:1, :] += jnp.sum(low.astype(f32), axis=0, keepdims=True)
        vec_b[1:2, :] += jnp.sum(g_two * normed, axis=0, keepdims=True)
        vec_b[2:3, :] += jnp.sum(g_two, axis=0, keepdims=True)
        vec_b[3:4, :] += jnp.sum(c, axis=0, keepdims=True)
        return carry

    lax.fori_loop(0, SHORT // CHUNK, middle, 0)
    out_copy = pltpu.make_async_copy(n_two, r.out, r.out_sem.at[0])
    out_copy.start()
    onward(total_i, (2, 2), (3, 1))
    onward(total_o, (2, 2), (3, 1))
    g_mix[...] = nt(g_att[...], w_mix).astype(bf16)

    def inner_sums(step, carry):
        at = pl.ds(pl.multiple_of(step * 512, 512), 512)
        turned = nt(w_mix, g_att[at, :]).astype(bf16).astype(f32) * mix_t[:, at].astype(f32)
        inner_s[:, at] = jnp.concatenate(
            [jnp.sum(turned[h * HEAD : (h + 1) * HEAD], axis=0, keepdims=True) for h in range(HEADS)], axis=0
        )
        return carry

    lax.fori_loop(0, SHORT // 512, inner_sums, 0)

    made = nn(mix_t[...], g_att[...])
    di[:, :, :, :, :, 4 * D :] = made.astype(bf16).reshape(4, 2, 2, 2, 16, D)
    onward(total_i, (4, 0), (2, 3), (3, 2))
    onward(total_o, (2, 3), (3, 2))


    def keep_h(lanes, values):
        for pair in range(PAIRS):
            total_h[pair, :, lanes] = values[2 * pair : 2 * pair + 2]

    def sums_of(level, source, members):
        both = jnp.concatenate(split2(share[level, :, source] * inner_s[:, source]), axis=0)
        made = nt(both, members)
        return made[0:8] + made[8:16]

    tops_acc[0:TILE, :] = jnp.zeros((TILE, D), f32)

    def lift(step, carry):
        pl.when(step == 2)(lambda: onward(total_i, (4, 1)))
        chunk = pl.ds(pl.multiple_of(step * CHUNK, CHUNK), CHUNK)
        to = chunk_rows(step)
        members = chunk_members(chunk)
        for pair_at in range(HEADS // 2):
            lo = pair_at * TILE
            left = [
                jnp.concatenate(
                    [one * share[1 + k, head : head + 1, chunk].astype(bf16) for k, one in enumerate(members)], axis=0
                )
                for head in (2 * pair_at, 2 * pair_at + 1)
            ]
            tokens = g_num[chunk, lo : lo + TILE]
            right = [tokens * r.head_m[0:1, :], tokens * r.head_m[TILE : TILE + 1, :]]
            made = nn(jnp.concatenate(left, axis=1), jnp.concatenate(right, axis=0))
            for level, (low, high) in enumerate(((0, 128), (128, 192), (192, 224))):
                g_num[to[level], lo : lo + TILE] = (made[low:high] * 0.5 ** (level + 1)).astype(bf16)
            tops_acc[0:TILE, lo : lo + TILE] += made[224:352]
        keep_h(chunk, share[0, :, chunk] * inner_s[:, chunk])
        keep_h(to[0], sums_of(1, chunk, member[0:128, chunk]))
        return carry

    lax.fori_loop(0, SHORT // CHUNK, lift, 0)
    g_num[FIRST[4] : STACK, :] = (tops_acc[0:TILE, :] * steps_down).astype(bf16)

    def lift_two(step, carry):
        source = pl.ds(pl.multiple_of(step * 512, 512), 512)
        rows = pl.ds(pl.multiple_of(FIRST[2] + step * TILE, TILE), TILE)
        keep_h(rows, sums_of(2, source, member[128:256, source]))
        return carry

    lax.fori_loop(0, 2, lift_two, 0)
    every = pl.ds(0, SHORT)
    keep_h(pl.ds(FIRST[3], TILE), sums_of(3, every, member[256:384, :]))
    tops = [sums_of(4 + slot, every, member[384:512, :]) for slot in range(4)]
    keep_h(
        pl.ds(FIRST[4], TILE),
        jnp.where(top_lane < 64, tops[0], jnp.where(top_lane < 96, tops[1], jnp.where(top_lane < 112, tops[2], tops[3]))),
    )
    onward(total_i, (3, 3))
    onward(total_o, (3, 3))
    if fast:
        for k, z in enumerate(p.zs):
            remote(do.at[z, p.y, p.x, p.c], r.so[6].at[k], r.so[7].at[1], r.so[7].at[0], p.by_z[k]).start()
    for pair in range(PAIRS):
        weight[pair, :, 0:SHORT] = share[0, 2 * pair : 2 * pair + 2]
    weight[:, :, SHORT:STACK] = jnp.ones((PAIRS, 2, SHORT), f32)

    def tile_backward(tile, pair, scale, scale_t):
        rows = lanes_at(tile * TILE, TILE)
        at = lambda slot: (rows, lanes_at(pair * GROUP + slot * TILE, TILE))
        both = lambda ref: jnp.concatenate([ref[pair, 0:1, rows], ref[pair, 1:2, rows]], axis=1)
        low = probs[tile, :, lanes_at(pair * 2 * TILE, 2 * TILE)].astype(f32)
        times = both(weight)
        num = two_heads(g_num[rows, lanes_at(pair * TILE, TILE)])
        got = squeeze(nt(stack[at(2)], num))
        wide_s = widen((low * (got * times - both(total_h))).astype(bf16))
        wide_p = widen((low * times).astype(bf16))
        query = two_heads(stack[at(0)])
        grad_kv[rows, lanes_at(pair * 2 * TILE, TILE)] = (nn(wide_s, query) * scale).astype(bf16)
        grad_kv[rows, lanes_at(pair * 2 * TILE + TILE, TILE)] = nn(wide_p, num).astype(bf16)
        made = nn(stack[at(1)].T, wide_s)
        head = pl.multiple_of(pair * TILE, TILE)
        grad_qt[pl.ds(head, HEAD), rows] = (made[:HEAD, :TILE] * scale_t).astype(bf16)
        grad_qt[pl.ds(head + HEAD, HEAD), rows] = (made[HEAD:, TILE:] * scale_t).astype(bf16)

    for pair in range(PAIRS):
        tile_backward(15, pair, steps_down, top_scale_t[0:1, :] * 0.125)
    back_s, back_r = r.back_s, r.back_r
    tall = grad_kv[2016:2048, :].astype(f32)
    nothing = jnp.zeros((8, 2 * D), f32)
    back_s[0] = tall[0:16].astype(bf16)
    back_s[1] = jnp.concatenate([tall[16:24], nothing], axis=0).astype(bf16)
    back_s[2] = jnp.concatenate([tall[24:32], nothing], axis=0).astype(bf16)
    back_out = [
        remote(back_s.at[0], back_r.at[0], r.far_sem.at[3], r.far_sem.at[2], (p.dp, other)),
        remote(back_s.at[1], back_r.at[1 + side], r.far_sem.at[3], r.far_sem.at[2], (p.dp, pairs_at)),
        remote(back_s.at[2], back_r.at[1 + side], r.far_sem.at[3], r.far_sem.at[2], (p.dp, pairs_at + 1)),
    ]
    for copy in back_out:
        copy.start()

    def total_a(part):
        return Total(da, lanes_at(part * GROUP, GROUP), part, p, r.sa[0], r.sa[1:])

    def far_grads():
        arrived(back_r, r.far_sem.at[2], p.by_core)
        gone(back_r, r.far_sem.at[3], p.by_core)
        grad_kv[2016:2032, :] = back_r[0]
        grad_kv[2032:2048, :] = (back_r[1].astype(f32) + back_r[2].astype(f32)).astype(bf16)

    def finish_feed():
        for part in range(5):
            total_i(part).finish(r.keep_i)
        arrived(r.so[6], r.so[7].at[0], p.by_core)
        total = do[p.z, p.y, p.x, p.c].astype(f32)
        r.keep_o[...] = functools.reduce(jnp.add, [r.so[6][k].astype(f32) for k in range(3)], total)
        gone(r.so[6], r.so[7].at[1], p.by_core)
        for part in range(4):
            total_o(part).settle()
        for copy in kept[:2]:
            copy.start()

    if fast:
        kept = [
            pltpu.make_async_copy(src, dst, r.keep_sem.at[k])
            for k, (src, dst) in enumerate(
                ((r.keep_i, r.o_i), (r.keep_o, r.o_o), (r.keep_a, r.o_a), (r.keep_v, r.o_v))
            )
        ]

        early = TotalVectors(r.vec_b, p, r.v_sem.at[0], r.got_b, r.mid_b, r.far_b)
        late = TotalVectors(r.vec_a, p, r.v_sem.at[1], r.got_a, r.mid_a, r.far_a)
    vec_b[4:8, :] = jnp.concatenate([r.lanes_in[0:1, k * 512 : (k + 1) * 512] for k in range(4)], axis=0)

    def early_done():
        r.done_b[...] = early.finish()

    def pair_backward(pair, carry):
        def near_back(group, carry):
            for one in range(TOGETHER):
                tile = group * TOGETHER + one
                scale = tile_scale(tile)
                tile_backward(tile, pair, scale, scale * 0.125)
            return carry

        lax.fori_loop(0, 15 // TOGETHER, near_back, 0)
        pl.when(pair == 0)(far_grads)
        if fast:
            pl.when(pair == 0)(lambda: onward(total_i, (4, 2)))
            pl.when(pair == 1)(lambda: onward(total_i, (4, 3)))
            pl.when(pair == 0)(early.begin)
            pl.when(pair == 1)(early.second)
            pl.when(pair == 2)(finish_feed)
            pl.when(pair == 3)(early_done)
        onward(total_a, (pair - 3, 3), (pair - 2, 2), (pair - 1, 1))

        @pl.when(pair == PAIRS - 1)
        def _():
            done = (PAIRS - 1) * GROUP
            acc_two[...] = nt(stack[0:SHORT, 0:done], wa[:, :, :, :, :, SMALL : SMALL + done].reshape(D, done))

        turned_rows = pl.ds(pl.multiple_of(pair * TILE, TILE), TILE)
        kv = lanes_at(pair * 2 * TILE, 2 * TILE)

        def level_sums(step, carry):
            chunk = pl.ds(pl.multiple_of(step * CHUNK, CHUNK), CHUNK)
            wins = windows(step)
            turned = nn(jnp.concatenate([grad_qt[turned_rows, win] for win in wins], axis=1), member[:, chunk])
            turned = (turned + grad_qt[turned_rows, chunk].astype(f32)).astype(bf16)
            stack[chunk, lanes_at(pair * GROUP, TILE)] = turned.T
            made = nn(spread[chunk, :], jnp.concatenate([grad_kv[win, kv] for win in wins], axis=0))
            stack[chunk, lanes_at(pair * GROUP + TILE, 2 * TILE)] = (
                made + grad_kv[chunk, kv].astype(f32)
            ).astype(bf16)
            return carry

        lax.fori_loop(0, SHORT // CHUNK, level_sums, 0)
        lanes = lanes_at(pair * GROUP, GROUP)
        da[:, :, :, :, :, lanes] = tn(n_one[...], stack[0:SHORT, lanes]).astype(bf16).reshape(4, 2, 2, 2, 16, GROUP)
        onward(total_a, (pair, 0))
        return carry

    lax.fori_loop(0, PAIRS, pair_backward, 0)

    done = (PAIRS - 1) * GROUP
    acc_two[...] += nt(stack[0:SHORT, done:], wa[:, :, :, :, :, SMALL + done :].reshape(D, GROUP))
    onward(total_a, (1, 3), (2, 2))

    def first_back(step, carry):
        chunk = pl.ds(pl.multiple_of(step * CHUNK, CHUNK), CHUNK)
        g_one = acc_two[chunk, :]
        normed, inverse = normalize(tok[chunk, :].astype(f32))
        vec_a[0:1, :] += jnp.sum(g_one * normed, axis=0, keepdims=True)
        vec_a[1:2, :] += jnp.sum(g_one, axis=0, keepdims=True)
        g_att[chunk, :] = (resid[chunk, :] + normalize_back(g_one * gain_one, normed, inverse)).astype(bf16)
        return carry

    lax.fori_loop(0, SHORT // CHUNK, first_back, 0)
    tok_copy = pltpu.make_async_copy(g_att, r.g_tok, r.out_sem.at[1])
    tok_copy.start()
    if fast:
        late.begin()
        onward(total_a, (3, 1), (2, 3))
        total_a(0).finish(r.keep_a)
        total_a(1).finish(r.keep_a)
        onward(total_a, (3, 2))
        late.second()
        total_a(2).finish(r.keep_a)
        onward(total_a, (3, 3))
        short = jnp.concatenate([late.finish()[0:2], r.done_b[0:4], jnp.zeros((2, D), f32)], axis=0)
        short = pltpu.roll(short, 512 - 16 * whose, axis=1)[:, 0:SMALL]
        long = jnp.concatenate([r.done_b[4 + k : 5 + k] for k in range(4)], axis=1)
        long = pltpu.roll(jnp.concatenate([long] * 8, axis=0), 2048 - HEAD * whose, axis=1)[:, 0:SMALL]
        r.keep_v[0:8] = short
        r.keep_v[8:16] = long
        kept[3].start()
        total_a(3).finish(r.keep_a)
        kept[2].start()
        for copy in kept:
            copy.wait()
    else:
        r.o_v[0:8] = vec_a[...]
        r.o_v[8:16] = vec_b[...]
    out_copy.wait()
    tok_copy.wait()


def final_kernel(*refs):
    big, small, outs, (kept, vmem_a, vmem_i, vmem_o, vmem_v, sem) = refs[:2], refs[2:6], refs[6:21], refs[21:]
    parts = [pl.ds(k * CHUNK, CHUNK) for k in range(SHORT // CHUNK)]
    count = iter(range(24))
    copy = lambda src, dst: pltpu.make_async_copy(src, dst, sem.at[next(count)])
    into = [copy(ref.at[at], kept.at[slot, at]) for slot, ref in enumerate(big) for at in parts]
    onto = [copy(kept.at[slot, at], outs[slot].at[at]) for slot in range(2) for at in parts]
    rest = [copy(src, dst) for src, dst in zip(small, (vmem_a, vmem_i, vmem_o, vmem_v))]
    for one in into + rest:
        one.start()
    for one, then in zip(into, onto):
        one.wait()
        then.start()
    for one in rest:
        one.wait()
    for slot, at in ((2, 0), (3, 1), (8, 2), (9, 3), (10, 4), (14, 5)):
        outs[slot][...] = vmem_v[at : at + 1, 0:16].reshape(16)
    outs[12][...] = vmem_v[8:9, 0:HEAD].reshape(HEAD)
    for k in range(3):
        for pair in range(PAIRS):
            at = pair * GROUP + k * TILE
            outs[4 + k][:, pair * TILE : (pair + 1) * TILE] = vmem_a[:, at : at + TILE]
    outs[7][...] = vmem_i[:, 4 * D :]
    outs[11][...] = vmem_i[:, : 4 * D]
    outs[13][...] = vmem_o[...]
    for one in onto:
        one.wait()


def scratch_list(fast):
    V, S = pltpu.VMEM, pltpu.SemaphoreType.DMA
    made = dict(
        tok=V((SHORT, D), bf16),
        cot=V((SHORT, D), bf16),
        member=V((D, SHORT), bf16),
        spread=V((SHORT, D), bf16),
        head_m=V((2 * TILE, TILE), bf16),
        group_m=V((TILE, 2 * TILE), bf16),
        bias=V((3, 32, 2 * TILE), f32),
        in_sem=S((17,)),
        out_sem=S((2,)),
        stack=V((STACK, WIDTH), bf16),
        probs=V((16, 32, HEADS * TILE), bf16),
        out_t=V((D, STACK), bf16),
        mix_t=V((D, SHORT), bf16),
        lse_s=V((PAIRS, 2, STACK), f32),
        share=V((LEVELS, HEADS, SHORT), f32),
        inner_s=V((HEADS, SHORT), f32),
        total_h=V((PAIRS, 2, STACK), f32),
        resid=V((SHORT, D), f32),
        n_one=V((SHORT, D), bf16),
        n_two=V((SHORT, D), bf16),
        acc_out=V((SHORT, D), f32),
        acc_two=V((SHORT, D), f32),
        grad_kv=V((STACK, 2 * D), bf16),
        g_att=V((SHORT, D), bf16),
        weight=V((PAIRS, 2, STACK), f32),
        g_num=V((STACK, D), bf16),
        vec_a=V((8, D), f32),
        vec_b=V((8, D), f32),
        param=V((16, D), f32),
        bias_in=V((1, 4 * D), f32),
        lanes_in=V((8, 4 * D), f32),
        far_s=V((2, 16, 2 * D), bf16),
        far_r=V((3, 16, 2 * D), bf16),
        far_sem=S((4,)),
        back_s=V((3, 16, 2 * D), bf16),
        back_r=V((3, 16, 2 * D), bf16),
    )
    if fast:

        def sums(parts, wide):
            shape = lambda *dims: V((parts,) + dims + (16, wide), bf16)
            return [S((parts, 7)), shape(4, 2, 2), shape(2, 2), shape(2, 2), shape(2), shape(2), shape(3)]

        rows = lambda *dims: V((4,) + dims + (D,), bf16)
        made.update(
            wa=V(SLOTS + (16, WIDTH + SMALL), bf16),
            wi=V(SLOTS + (16, 5 * D), bf16),
            wo=V(SLOTS + (64, D), bf16),
            da=V(SLOTS + (16, WIDTH), bf16),
            di=V(SLOTS + (16, 5 * D), bf16),
            do=V(SLOTS + (64, D), bf16),
            g_sem=S((8, 7)),
            si=sums(5, D),
            so=[S((4, 5)), rows(2, 2, 64), rows(2, 32), rows(2, 32), rows(32), rows(32), V((3, 64, D), bf16), S((2,))],
            sa=sums(4, GROUP),
            v_sem=S((2, 4)),
            got_a=V((7, 8, D), f32),
            mid_a=V((8, D), f32),
            far_a=V((3, 8, D), f32),
            got_b=V((7, 8, D), f32),
            mid_b=V((8, D), f32),
            far_b=V((3, 8, D), f32),
            done_b=V((8, D), f32),
            vec_in=[V((16,), bf16)] * 6 + [V((HEAD,), bf16)],
            keep_a=V((16, WIDTH), f32),
            keep_i=V((16, 5 * D), f32),
            keep_o=V((HEAD, D), f32),
            keep_v=V((16, SMALL), f32),
            keep_sem=S((4,)),
        )
    return made


def constants():
    member = member_matrix()
    as_low = lambda values: jnp.asarray(values.astype(np.float32), bf16)
    return dict(
        member_h=as_low(member),
        spread_h=as_low(np.ascontiguousarray(member.T)),
        head_h=as_low(head_mask()),
        group_h=as_low(group_mask()),
        bias_h=jnp.asarray(block_bias()),
    )


def run_layer(fast, hbm, vmem):
    sd = jax.ShapeDtypeStruct
    const = constants()
    hbm = dict(hbm, **const)
    here, there = pl.BlockSpec(memory_space=pltpu.VMEM), pl.BlockSpec(memory_space=pl.ANY)
    slots = () if fast else SLOTS
    kind = f32 if fast else bf16
    outs = dict(
        out=sd((SHORT, D), bf16),
        g_tok=sd((SHORT, D), bf16),
        o_a=sd(slots + (16, WIDTH), kind),
        o_i=sd(slots + (16, 5 * D), kind),
        o_o=sd(slots + (64, D), kind),
        o_v=sd((16, SMALL if fast else D), f32),
    )
    row_length = hbm.pop("row_length")
    operands = dict(hbm, row_length=row_length, **vmem)
    flat = lambda parts: [one for part in parts.values() for one in (part if isinstance(part, list) else [part])]
    specs = [there] * len(flat(hbm)) + [pl.BlockSpec(memory_space=pltpu.SMEM)] + [here] * len(vmem)
    hbm_outs = len(outs) if fast else 2
    return pl.pallas_call(
        functools.partial(layer_kernel, fast, dict(operands, **outs)),
        out_shape=list(outs.values()),
        in_specs=specs,
        out_specs=[there] * hbm_outs + [here] * (len(outs) - hbm_outs),
        scratch_shapes=flat(scratch_list(fast)),
        compiler_params=pltpu.CompilerParams(
            collective_id=0, has_side_effects=True, vmem_limit_bytes=63 * 2**20
        ),
    )(*flat(operands))


def finish_outputs(*parts):
    sd = jax.ShapeDtypeStruct
    vmem, hbm = pl.BlockSpec(memory_space=pltpu.VMEM), pl.BlockSpec(memory_space=pl.ANY)
    own, square = sd((16,), f32), sd((16, D), f32)
    tokens = sd((SHORT, D), bf16)
    outs = [tokens, tokens, own, own, square, square, square, square, own, own, own]
    outs += [sd((16, 4 * D), f32), sd((HEAD,), f32), sd((HEAD, D), f32), own]
    return pl.pallas_call(
        final_kernel,
        out_shape=outs,
        in_specs=[hbm] * 6,
        out_specs=[hbm] * 2 + [vmem] * 13,
        scratch_shapes=[
            pltpu.VMEM((2, SHORT, D), bf16),
            pltpu.VMEM((16, WIDTH), f32),
            pltpu.VMEM((16, 5 * D), f32),
            pltpu.VMEM((HEAD, D), f32),
            pltpu.VMEM((16, SMALL), f32),
            pltpu.SemaphoreType.DMA((20,)),
        ],
    )(*parts)


def on_device(
    tokens, cotangent, row_length, first_gain, first_shift, query_weight, key_weight, value_weight,
    mixer_weight, mixer_bias, second_gain, second_shift, inner_weight, inner_bias, outer_weight, outer_bias,
):
    n_dp, n_fsdp = lax.axis_size("dp"), lax.axis_size("fsdp")
    fast = (n_dp, n_fsdp) == (8, 4) and query_weight.shape[0] == 16
    vectors = (first_gain, first_shift, mixer_bias, second_gain, second_shift, outer_bias)
    first = dict(tok_h=tokens, cot_h=cotangent, row_length=row_length)
    if fast:
        first.update(
            wq_s=query_weight, wk_s=key_weight, wv_s=value_weight, wm_s=mixer_weight, wi_s=inner_weight, wo_s=outer_weight,
            vectors=list(vectors) + [inner_bias],
        )
        return finish_outputs(*run_layer(True, first, dict()))
    whole = lambda part: lax.all_gather(part, AXES, axis=0, tiled=True)
    three = jnp.stack([part.reshape(-1, PAIRS, TILE) for part in (query_weight, key_weight, value_weight)], axis=2)
    wide = whole(three.reshape(-1, WIDTH))
    eights = [whole(vector).reshape(4, 8, 16) for vector in vectors]
    small = jnp.zeros((4, 8, 16, SMALL), bf16)
    for row, vector in enumerate(eights):
        for at in range(8):
            small = small.at[:, at, row, 16 * at : 16 * at + 16].set(vector[:, at])
    pairs = whole(inner_bias).reshape(4, 4, 2, 64)
    pairs_at = small.reshape(4, 4, 2, 16, SMALL)
    for at in range(2):
        pairs_at = pairs_at.at[:, :, at, 6, 64 * at : 64 * at + 64].set(pairs[:, :, at])
    wide = jnp.concatenate((pairs_at.reshape(4, 8, 16, SMALL), wide.reshape(4, 8, 16, WIDTH)), axis=-1)
    weights = dict(
        wa=wide.reshape(SLOTS + (16, WIDTH + SMALL)),
        wi=whole(jnp.concatenate((inner_weight, mixer_weight), axis=1)).reshape(SLOTS + (16, 5 * D)),
        wo=whole(outer_weight).reshape(SLOTS + (64, D)),
    )
    out, g_tok, d_a, d_i, d_o, o_v = run_layer(False, first, weights)
    owned = lambda part: lax.psum_scatter(part, AXES, scatter_dimension=0, tiled=True)
    g_a = owned(d_a.astype(f32).reshape(D, WIDTH))
    g_q, g_k, g_v = (g_a.reshape(-1, PAIRS, 3, TILE)[:, :, k].reshape(-1, D) for k in range(3))
    g_i = owned(d_i.astype(f32).reshape(D, 5 * D))
    g_i, g_m = g_i[:, : 4 * D], g_i[:, 4 * D :]
    g_o = owned(d_o.astype(f32).reshape(4 * D, D))
    six = [owned(o_v[k]) for k in (0, 1, 8, 9, 10, 11)]
    g_bias_in = owned(o_v[12:16].reshape(-1))
    return (
        out, g_tok, six[0], six[1], g_q, g_k, g_v, g_m, six[2], six[3], six[4], g_i, g_bias_in, g_o, six[5],
    )


def solution(mesh):
    rows, flat, both = P(AXES, None), P(AXES), P("dp")
    in_specs = (rows, rows, both, flat, flat, rows, rows, rows, rows, flat, flat, flat, rows, flat, rows, flat)
    out_specs = (rows, rows, flat, flat, rows, rows, rows, rows, flat, flat, flat, rows, flat, rows, flat)
    return jax.shard_map(on_device, mesh=mesh, in_specs=in_specs, out_specs=out_specs, check_vma=False)
```

time: 145 us -> 132 us (0.910)
  Pallas kernels: 143 us -> 131 us
    pallas_call x1, Pallas kernels: 139 us -> 127 us  [run_layer(): pl.pallas_call(functools.partial(layer_kernel, fast, dict(operands, **out...]
where the time goes in v2:
time: 132 us
  Pallas kernels  131 us (99%)
  between operations  1.47 us (1%)
    pallas_call x1, Pallas kernels, run_layer(): pl.pallas_call(functools.partial(layer_kernel, fast, dict(operands, **out...  127 us
    pallas_call x1, Pallas kernels, finish_outputs(): pl.pallas_call(final_kernel, out_shape=outs, in_specs=[hbm] * 6, out_spec...  3.2 us

profile of v2, /device:TPU:0, one launch (start us, length us, event | category | flops | bytes accessed | tf_op | source)
XLA Modules:
  0.0 132.1 jit_solution(8011638521254401167)
XLA Ops:
  1.3 127.4 %shard_map.316 = (bf16[1024,512]{1,0:T(8,128)(2,1)}, bf16[1024,512]{1,0:T(8,128)(2,1)}, f32[16,1536]{1,0:T(8,128)}, f32[16,2560]{1,0:T(8,128)}, f32[64,512]{1,0:T(8,128)}, /*index=5*/f32[16,128]{1,0:T(8,128)}) custom-call(bf16[1024,512]{1,0:T(8,128)(2,1)} %refs_0_.1, bf16[1024,512]{1,0:T(8,128)(2,1)} %refs_1_.1, bf16[16,512]{1,0:T(8,128)(2,1)} %refs_2_.1, ...), custom_call_target="tpu_custom_call" | custom-call | tf_op jit(solution)/shard_map/pallas_call | solution.py:1069
  128.7 3.2 %shard_map.317 = (bf16[1024,512]{1,0:T(8,128)(2,1)}, bf16[1024,512]{1,0:T(8,128)(2,1)}, f32[16]{0:T(128)}, f32[16]{0:T(128)}, f32[16,512]{1,0:T(8,128)}, /*index...) custom-call(bf16[1024,512]{1,0:T(8,128)(2,1)} %get-tuple-element.21., ...), custom_call_target="tpu_custom_call" | custom-call | tf_op jit(solution)/shard_map/pallas_call | solution.py:1088

commit v3 on v2

--- a/solution.py
+++ b/solution.py
@@ -47,6 +47,12 @@
         rows.append(token[None] >> level == np.arange(SHORT >> level)[:, None])
     rows.append(np.zeros((8, SHORT), bool))
     return np.concatenate(rows).astype(np.float32)
+
+
+def spread_matrix():
+    member = member_matrix()
+    near = np.concatenate([member[0:128, :CHUNK], member[128:192, :CHUNK], member[256:288, :CHUNK], np.zeros((32, CHUNK))])
+    return np.concatenate([np.tile(near, (1, SHORT // CHUNK)), member[384:]]).T.astype(np.float32)
 
 
 def block_bias():
@@ -306,11 +312,10 @@
     acc_out, acc_two = r.acc_out, r.acc_two
     g_att, g_num = r.g_att, r.g_num
     g_mix, weight = g_num.at[0:SHORT], r.weight
-    grad_kv = r.grad_kv
+    grads = r.grads
     vec_a, vec_b = r.vec_a, r.vec_b
     wa, wi, wo = r.wa, r.wi, r.wo
     da, di, do = (r.da, r.di, r.do) if fast else (r.o_a, r.o_i, r.o_o)
-    grad_qt = out_t
 
     def fetch(src, dst, slot):
         copy = pltpu.make_async_copy(src, dst, r.in_sem.at[slot])
@@ -373,8 +378,7 @@
         return carry
 
     if fast:
-        spans = [(wa, 0, SMALL + GROUP)] + [(wa, SMALL + k * GROUP, GROUP) for k in range(1, PAIRS)]
-        spans += [(wi, 0, 1280), (wi, 1280, 1280), (wo, 0, 256), (wo, 256, 256)]
+        spans = [(wa, 0, SMALL + GROUP), (wa, SMALL + GROUP, 3 * GROUP), (wi, 0, 1280), (wi, 1280, 1280), (wo, 0, D)]
         gathers = [
             Gather(ref, pl.ds(lo, wide), p, r.g_sem.at[k]) for k, (ref, lo, wide) in enumerate(spans)
         ]
@@ -384,13 +388,14 @@
             for k, step in events:
                 gathers[k].advance(step)
 
-    pump((0, 0), (1, 0), (2, 0), (3, 0))
-    tok_in.wait()
-    lax.fori_loop(0, SHORT // CHUNK, first_norm, 0)
+    pump((0, 0), (1, 0))
     if fast:
         taken(own_i, 8)
         taken(own_o, 9)
-    pump((0, 1), (1, 1), (0, 2), (2, 1), (1, 2), (0, 3), (3, 1), (4, 0), (2, 2), (0, 4))
+    pump((2, 0))
+    tok_in.wait()
+    lax.fori_loop(0, SHORT // CHUNK, first_norm, 0)
+    pump((0, 1), (3, 0), (0, 2), (1, 1), (0, 3), (1, 2), (0, 4))
     for copy in rest_in:
         copy.wait()
 
@@ -432,7 +437,7 @@
         near = [member[lo:hi, 0:CHUNK] for lo, hi in ((0, 128), (128, 192), (256, 288))]
         return near + [member[lo:hi, chunk] for lo, hi in ((384, 448), (448, 480), (480, 496), (496, 512))]
 
-    lane_group = lax.broadcasted_iota(jnp.int32, (32, 2 * TILE), 1) % TILE // 32
+    lane_group = lax.broadcasted_iota(jnp.int32, (32, TILE), 1) // 32
 
     def squeeze(tall):
         parts = [tall[32 * part : 32 * part + 32, :] for part in range(4)]
@@ -443,7 +448,12 @@
         )
 
     def widen(low):
-        return jnp.concatenate([low, low, low, low], axis=0) * r.group_m[...]
+        return jnp.concatenate([low, low, low, low], axis=0) * r.group_m[:, 0 : low.shape[1]]
+
+    def by_head(both):
+        half = both.shape[0] // 2
+        lane = lax.broadcasted_iota(jnp.int32, (half, TILE), 1)
+        return jnp.where(lane < HEAD, both[:half], both[half:])
 
     def two_heads(low):
         return jnp.concatenate([low, low], axis=0) * r.head_m[...]
@@ -464,7 +474,8 @@
     def tile_forward(tile, pair, kind, scale_t):
         rows = lanes_at(tile * TILE, TILE)
         at = lambda slot: (rows, lanes_at(pair * GROUP + slot * TILE, TILE))
-        score = squeeze(nt(stack[at(1)], two_heads(stack[at(0)]))) + r.bias[kind]
+        score = nt(two_heads(stack[at(1)]), stack[at(0)])
+        score = jnp.concatenate([squeeze(score[:TILE]), squeeze(score[TILE:])], axis=1) + r.bias[kind]
         peak = jnp.max(score, axis=0, keepdims=True)
         prob = jnp.exp(score - peak)
         total = jnp.sum(prob, axis=0, keepdims=True)
@@ -492,13 +503,13 @@
                 if events:
                     pl.when(pair == number)(functools.partial(pump, *events))
 
-        pump_here([], [(1, 4), (5, 1)], [(2, 4)], [(3, 4)])
+        pump_here([], [(1, 4)])
         lanes = lanes_at(pair * GROUP, GROUP)
         made = nn(n_one[...], wa[:, :, :, :, :, lanes_at(SMALL + pair * GROUP, GROUP)].reshape(D, GROUP))
         first = lax.broadcasted_iota(jnp.int32, (1, GROUP), 1)
         stack[0:SHORT, lanes] = (made * jnp.where(first < TILE, 0.125, 1.0)).astype(bf16)
         key_like = first < 2 * TILE
-        pump_here([(1, 3), (3, 2), (5, 0)])
+        pump_here([(2, 1), (4, 0)])
         tops_acc[0:TILE, 0:GROUP] = jnp.zeros((TILE, GROUP), f32)
 
         def pool(step, carry):
@@ -529,11 +540,17 @@
             for one in range(TOGETHER):
                 tile = group * TOGETHER + one
                 tile_forward(tile, pair, jnp.where(tile < 8, 0, 1), tile_scale(tile))
+            for when, what, events in (
+                (0, 1, [(1, 3)]),
+                (0, 2, [(2, 2), (3, 1)]),
+                (1, 2, [(2, 3), (3, 2), (4, 1)]),
+                (2, 2, [(2, 4)]),
+                (3, 1, [(3, 3), (4, 2)]),
+            ):
+                pl.when((pair == when) & (group == what))(functools.partial(pump, *events))
             return carry
 
-        pump_here([(2, 3), (4, 1)], [(4, 3), (6, 1)], [(5, 3), (7, 1)], [(6, 3)])
         lax.fori_loop(0, 15 // TOGETHER, near_tiles, 0)
-        pump_here([(3, 3), (4, 2), (6, 0)], [(5, 2), (7, 0)], [(4, 4), (6, 2)], [(7, 2)])
         return carry
 
     lax.fori_loop(0, PAIRS, pair_forward, 0)
@@ -604,7 +621,7 @@
         return carry
 
     lax.fori_loop(0, SHORT // CHUNK, combine, 0)
-    pump((7, 3), (5, 4), (6, 4))
+    pump((3, 4), (4, 3))
 
     bias_mix, gain_two = r.param[2:3, :], r.param[3:4, :]
     shift_two, bias_out = r.param[4:5, :], r.param[5:6, :]
@@ -620,9 +637,9 @@
         return carry
 
     lax.fori_loop(0, SHORT // CHUNK, second_norm, 0)
-    pump((7, 4))
-
-    hid, g_pre = grad_kv.at[0:SHORT, 0:D], grad_kv.at[0:SHORT, D : 2 * D]
+    pump((4, 4))
+
+    hid, g_pre = grads.at[0:SHORT, 0:D], grads.at[0:SHORT, D : 2 * D]
     acc_out[...] = jnp.zeros_like(acc_out)
     acc_two[...] = jnp.zeros_like(acc_two)
 
@@ -657,14 +674,14 @@
             acc_two[at, :] += nt(back, w_in)
             sums = sums + jnp.sum(back.astype(f32), axis=0, keepdims=True)
             if step == 0:
-                onward(total_i, (part - 2, 2), (part - 1, 1))
-                onward(total_o, (part - 2, 2), (part - 1, 1))
+                onward(total_i, (part - 3, 3), (part - 2, 2), (part - 1, 1))
+                onward(total_o, (part - 3, 3), (part - 2, 2), (part - 1, 1))
         r.lanes_in[0:1, lanes] = sums
         di[:, :, :, :, :, lanes] = tn(n_two[...], g_pre[...]).astype(bf16).reshape(4, 2, 2, 2, 16, 512)
         do[part] = tn(hid[...], cot[...]).astype(bf16).reshape(2, 2, 2, 64, 512)
         if fast:
-            onward(total_i, (part - 2, 3), (part, 0))
-            onward(total_o, (part - 2, 3), (part, 0))
+            onward(total_i, (part, 0))
+            onward(total_o, (part, 0))
         return carry
 
     lax.fori_loop(0, 4, feed, 0)
@@ -689,8 +706,8 @@
     lax.fori_loop(0, SHORT // CHUNK, middle, 0)
     out_copy = pltpu.make_async_copy(n_two, r.out, r.out_sem.at[0])
     out_copy.start()
-    onward(total_i, (2, 2), (3, 1))
-    onward(total_o, (2, 2), (3, 1))
+    onward(total_i, (1, 3), (2, 2), (3, 1))
+    onward(total_o, (1, 3), (2, 2), (3, 1))
     g_mix[...] = nt(g_att[...], w_mix).astype(bf16)
 
     def inner_sums(step, carry):
@@ -705,8 +722,7 @@
 
     made = nn(mix_t[...], g_att[...])
     di[:, :, :, :, :, 4 * D :] = made.astype(bf16).reshape(4, 2, 2, 2, 16, D)
-    onward(total_i, (4, 0), (2, 3), (3, 2))
-    onward(total_o, (2, 3), (3, 2))
+    onward(total_i, (4, 0))
 
 
     def keep_h(lanes, values):
@@ -721,24 +737,24 @@
     tops_acc[0:TILE, :] = jnp.zeros((TILE, D), f32)
 
     def lift(step, carry):
-        pl.when(step == 2)(lambda: onward(total_i, (4, 1)))
+        pl.when(step == 2)(lambda: onward(total_i, (2, 3)))
+        pl.when(step == 3)(lambda: onward(total_o, (2, 3)))
         chunk = pl.ds(pl.multiple_of(step * CHUNK, CHUNK), CHUNK)
         to = chunk_rows(step)
         members = chunk_members(chunk)
-        for pair_at in range(HEADS // 2):
-            lo = pair_at * TILE
-            left = [
-                jnp.concatenate(
-                    [one * share[1 + k, head : head + 1, chunk].astype(bf16) for k, one in enumerate(members)], axis=0
-                )
-                for head in (2 * pair_at, 2 * pair_at + 1)
+        made = []
+        for pair in range(PAIRS):
+            weighted = [
+                one * share[1 + k, head : head + 1, chunk].astype(bf16)
+                for head in (2 * pair, 2 * pair + 1)
+                for k, one in enumerate(members)
             ]
-            tokens = g_num[chunk, lo : lo + TILE]
-            right = [tokens * r.head_m[0:1, :], tokens * r.head_m[TILE : TILE + 1, :]]
-            made = nn(jnp.concatenate(left, axis=1), jnp.concatenate(right, axis=0))
-            for level, (low, high) in enumerate(((0, 128), (128, 192), (192, 224))):
-                g_num[to[level], lo : lo + TILE] = (made[low:high] * 0.5 ** (level + 1)).astype(bf16)
-            tops_acc[0:TILE, lo : lo + TILE] += made[224:352]
+            tokens = g_num[chunk, pair * TILE : (pair + 1) * TILE]
+            made.append(by_head(nn(jnp.concatenate(weighted, axis=0), tokens)))
+        made = jnp.concatenate(made, axis=1)
+        for level, (low, high) in enumerate(((0, 128), (128, 192), (192, 224))):
+            g_num[to[level], :] = (made[low:high] * 0.5 ** (level + 1)).astype(bf16)
+        tops_acc[0:TILE, :] += made[224:352]
         keep_h(chunk, share[0, :, chunk] * inner_s[:, chunk])
         keep_h(to[0], sums_of(1, chunk, member[0:128, chunk]))
         return carry
@@ -760,37 +776,36 @@
         pl.ds(FIRST[4], TILE),
         jnp.where(top_lane < 64, tops[0], jnp.where(top_lane < 96, tops[1], jnp.where(top_lane < 112, tops[2], tops[3]))),
     )
-    onward(total_i, (3, 3))
-    onward(total_o, (3, 3))
-    if fast:
-        for k, z in enumerate(p.zs):
-            remote(do.at[z, p.y, p.x, p.c], r.so[6].at[k], r.so[7].at[1], r.so[7].at[0], p.by_z[k]).start()
+    onward(total_i, (3, 2))
+    onward(total_o, (3, 2))
     for pair in range(PAIRS):
         weight[pair, :, 0:SHORT] = share[0, 2 * pair : 2 * pair + 2]
     weight[:, :, SHORT:STACK] = jnp.ones((PAIRS, 2, SHORT), f32)
 
-    def tile_backward(tile, pair, scale, scale_t):
+    def tile_backward(tile, pair, scale):
         rows = lanes_at(tile * TILE, TILE)
         at = lambda slot: (rows, lanes_at(pair * GROUP + slot * TILE, TILE))
+        num = g_num[rows, lanes_at(pair * TILE, TILE)]
+        got = nt(two_heads(stack[at(2)]), num)
+        got = jnp.concatenate([squeeze(got[:TILE]), squeeze(got[TILE:])], axis=1)
         both = lambda ref: jnp.concatenate([ref[pair, 0:1, rows], ref[pair, 1:2, rows]], axis=1)
         low = probs[tile, :, lanes_at(pair * 2 * TILE, 2 * TILE)].astype(f32)
         times = both(weight)
-        num = two_heads(g_num[rows, lanes_at(pair * TILE, TILE)])
-        got = squeeze(nt(stack[at(2)], num))
         wide_s = widen((low * (got * times - both(total_h))).astype(bf16))
         wide_p = widen((low * times).astype(bf16))
-        query = two_heads(stack[at(0)])
-        grad_kv[rows, lanes_at(pair * 2 * TILE, TILE)] = (nn(wide_s, query) * scale).astype(bf16)
-        grad_kv[rows, lanes_at(pair * 2 * TILE + TILE, TILE)] = nn(wide_p, num).astype(bf16)
+        tall = lambda wide: jnp.concatenate([wide[:, :TILE], wide[:, TILE:]], axis=0)
+        grads[at(1)] = (by_head(nn(tall(wide_s), stack[at(0)])) * scale).astype(bf16)
+        grads[at(2)] = by_head(nn(tall(wide_p), num)).astype(bf16)
         made = nn(stack[at(1)].T, wide_s)
-        head = pl.multiple_of(pair * TILE, TILE)
-        grad_qt[pl.ds(head, HEAD), rows] = (made[:HEAD, :TILE] * scale_t).astype(bf16)
-        grad_qt[pl.ds(head + HEAD, HEAD), rows] = (made[HEAD:, TILE:] * scale_t).astype(bf16)
+        made = jnp.concatenate([made[:HEAD, :TILE], made[HEAD:, TILE:]], axis=0).astype(bf16).T
+        grads[at(0)] = (made.astype(f32) * (scale * 0.125)).astype(bf16)
 
     for pair in range(PAIRS):
-        tile_backward(15, pair, steps_down, top_scale_t[0:1, :] * 0.125)
+        tile_backward(15, pair, steps_down)
+    onward(total_i, (4, 1))
     back_s, back_r = r.back_s, r.back_r
-    tall = grad_kv[2016:2048, :].astype(f32)
+    spans = [(slice(k * GROUP + TILE, (k + 1) * GROUP), slice(k * 2 * TILE, (k + 1) * 2 * TILE)) for k in range(PAIRS)]
+    tall = jnp.concatenate([grads[2016:2048, theirs] for theirs, _ in spans], axis=1).astype(f32)
     nothing = jnp.zeros((8, 2 * D), f32)
     back_s[0] = tall[0:16].astype(bf16)
     back_s[1] = jnp.concatenate([tall[16:24], nothing], axis=0).astype(bf16)
@@ -809,8 +824,15 @@
     def far_grads():
         arrived(back_r, r.far_sem.at[2], p.by_core)
         gone(back_r, r.far_sem.at[3], p.by_core)
-        grad_kv[2016:2032, :] = back_r[0]
-        grad_kv[2032:2048, :] = (back_r[1].astype(f32) + back_r[2].astype(f32)).astype(bf16)
+        two = (back_r[1].astype(f32) + back_r[2].astype(f32)).astype(bf16)
+        for theirs, mine in spans:
+            grads[2016:2032, theirs] = back_r[0, :, mine]
+            grads[2032:2048, theirs] = two[:, mine]
+
+    def send_rows():
+        onward(total_o, (3, 3))
+        for k, z in enumerate(p.zs):
+            remote(do.at[z, p.y, p.x, p.c], r.so[6].at[k], r.so[7].at[1], r.so[7].at[0], p.by_z[k]).start()
 
     def finish_feed():
         for part in range(5):
@@ -833,64 +855,56 @@
         ]
 
         early = TotalVectors(r.vec_b, p, r.v_sem.at[0], r.got_b, r.mid_b, r.far_b)
-        late = TotalVectors(r.vec_a, p, r.v_sem.at[1], r.got_a, r.mid_a, r.far_a)
+        late = TotalVectors(r.vec_s, p, r.v_sem.at[1], r.got_a, r.mid_a, r.far_a)
     vec_b[4:8, :] = jnp.concatenate([r.lanes_in[0:1, k * 512 : (k + 1) * 512] for k in range(4)], axis=0)
 
     def early_done():
         r.done_b[...] = early.finish()
+        long = jnp.concatenate([r.done_b[4 + k : 5 + k] for k in range(4)], axis=1)
+        long = pltpu.roll(jnp.concatenate([long] * 8, axis=0), 2048 - HEAD * whose, axis=1)[:, 0:SMALL]
+        r.keep_v[8:16] = long
 
     def pair_backward(pair, carry):
         def near_back(group, carry):
             for one in range(TOGETHER):
                 tile = group * TOGETHER + one
-                scale = tile_scale(tile)
-                tile_backward(tile, pair, scale, scale * 0.125)
+                tile_backward(tile, pair, tile_scale(tile))
             return carry
 
         lax.fori_loop(0, 15 // TOGETHER, near_back, 0)
         pl.when(pair == 0)(far_grads)
         if fast:
-            pl.when(pair == 0)(lambda: onward(total_i, (4, 2)))
+            pl.when(pair == 0)(lambda: onward(total_i, (3, 3), (4, 2)))
+            pl.when(pair == 0)(send_rows)
             pl.when(pair == 1)(lambda: onward(total_i, (4, 3)))
             pl.when(pair == 0)(early.begin)
             pl.when(pair == 1)(early.second)
-            pl.when(pair == 2)(finish_feed)
+            pl.when(pair == 3)(finish_feed)
             pl.when(pair == 3)(early_done)
         onward(total_a, (pair - 3, 3), (pair - 2, 2), (pair - 1, 1))
 
-        @pl.when(pair == PAIRS - 1)
-        def _():
-            done = (PAIRS - 1) * GROUP
-            acc_two[...] = nt(stack[0:SHORT, 0:done], wa[:, :, :, :, :, SMALL : SMALL + done].reshape(D, done))
-
-        turned_rows = pl.ds(pl.multiple_of(pair * TILE, TILE), TILE)
-        kv = lanes_at(pair * 2 * TILE, 2 * TILE)
+        lanes = lanes_at(pair * GROUP, GROUP)
 
         def level_sums(step, carry):
             chunk = pl.ds(pl.multiple_of(step * CHUNK, CHUNK), CHUNK)
-            wins = windows(step)
-            turned = nn(jnp.concatenate([grad_qt[turned_rows, win] for win in wins], axis=1), member[:, chunk])
-            turned = (turned + grad_qt[turned_rows, chunk].astype(f32)).astype(bf16)
-            stack[chunk, lanes_at(pair * GROUP, TILE)] = turned.T
-            made = nn(spread[chunk, :], jnp.concatenate([grad_kv[win, kv] for win in wins], axis=0))
-            stack[chunk, lanes_at(pair * GROUP + TILE, 2 * TILE)] = (
-                made + grad_kv[chunk, kv].astype(f32)
-            ).astype(bf16)
+            top = grads[FIRST[4] : STACK, lanes]
+            coarse = [grads[rows, lanes] for rows in chunk_rows(step)] + [top[0:32], top]
+            made = nn(spread[chunk, :], jnp.concatenate(coarse, axis=0))
+            stack[chunk, lanes] = (made + grads[chunk, lanes].astype(f32)).astype(bf16)
             return carry
 
         lax.fori_loop(0, SHORT // CHUNK, level_sums, 0)
-        lanes = lanes_at(pair * GROUP, GROUP)
         da[:, :, :, :, :, lanes] = tn(n_one[...], stack[0:SHORT, lanes]).astype(bf16).reshape(4, 2, 2, 2, 16, GROUP)
         onward(total_a, (pair, 0))
         return carry
 
     lax.fori_loop(0, PAIRS, pair_backward, 0)
 
-    done = (PAIRS - 1) * GROUP
-    acc_two[...] += nt(stack[0:SHORT, done:], wa[:, :, :, :, :, SMALL + done :].reshape(D, GROUP))
-    onward(total_a, (1, 3), (2, 2))
+    acc_two[...] = nt(stack[0:SHORT, :], wa[:, :, :, :, :, SMALL : SMALL + WIDTH].reshape(D, WIDTH))
+    onward(total_a, (3, 1), (1, 3), (2, 2))
 
     def first_back(step, carry):
+        pl.when(step == 2)(lambda: onward(total_a, (3, 2), (2, 3)))
         chunk = pl.ds(pl.multiple_of(step * CHUNK, CHUNK), CHUNK)
         g_one = acc_two[chunk, :]
         normed, inverse = normalize(tok[chunk, :].astype(f32))
@@ -903,20 +917,20 @@
     tok_copy = pltpu.make_async_copy(g_att, r.g_tok, r.out_sem.at[1])
     tok_copy.start()
     if fast:
+        for row in range(2):
+            for part in range(4):
+                at = row * 4 + part
+                r.vec_s[at : at + 1, :] = vec_a[row : row + 1, part * TILE : (part + 1) * TILE]
         late.begin()
-        onward(total_a, (3, 1), (2, 3))
-        total_a(0).finish(r.keep_a)
-        total_a(1).finish(r.keep_a)
-        onward(total_a, (3, 2))
+        onward(total_a, (3, 3))
         late.second()
-        total_a(2).finish(r.keep_a)
-        onward(total_a, (3, 3))
-        short = jnp.concatenate([late.finish()[0:2], r.done_b[0:4], jnp.zeros((2, D), f32)], axis=0)
+        for part in range(3):
+            total_a(part).finish(r.keep_a)
+        last = late.finish()
+        rows = [jnp.concatenate([last[at + part : at + part + 1] for part in range(4)], axis=1) for at in (0, 4)]
+        short = jnp.concatenate(rows + [r.done_b[0:4], jnp.zeros((2, D), f32)], axis=0)
         short = pltpu.roll(short, 512 - 16 * whose, axis=1)[:, 0:SMALL]
-        long = jnp.concatenate([r.done_b[4 + k : 5 + k] for k in range(4)], axis=1)
-        long = pltpu.roll(jnp.concatenate([long] * 8, axis=0), 2048 - HEAD * whose, axis=1)[:, 0:SMALL]
         r.keep_v[0:8] = short
-        r.keep_v[8:16] = long
         kept[3].start()
         total_a(3).finish(r.keep_a)
         kept[2].start()
@@ -964,7 +978,7 @@
         tok=V((SHORT, D), bf16),
         cot=V((SHORT, D), bf16),
         member=V((D, SHORT), bf16),
-        spread=V((SHORT, D), bf16),
+        spread=V((SHORT, GROUP), bf16),
         head_m=V((2 * TILE, TILE), bf16),
         group_m=V((TILE, 2 * TILE), bf16),
         bias=V((3, 32, 2 * TILE), f32),
@@ -983,7 +997,7 @@
         n_two=V((SHORT, D), bf16),
         acc_out=V((SHORT, D), f32),
         acc_two=V((SHORT, D), f32),
-        grad_kv=V((STACK, 2 * D), bf16),
+        grads=V((STACK, WIDTH), bf16),
         g_att=V((SHORT, D), bf16),
         weight=V((PAIRS, 2, STACK), f32),
         g_num=V((STACK, D), bf16),
@@ -1012,14 +1026,15 @@
             da=V(SLOTS + (16, WIDTH), bf16),
             di=V(SLOTS + (16, 5 * D), bf16),
             do=V(SLOTS + (64, D), bf16),
-            g_sem=S((8, 7)),
+            g_sem=S((5, 7)),
             si=sums(5, D),
             so=[S((4, 5)), rows(2, 2, 64), rows(2, 32), rows(2, 32), rows(32), rows(32), V((3, 64, D), bf16), S((2,))],
             sa=sums(4, GROUP),
             v_sem=S((2, 4)),
-            got_a=V((7, 8, D), f32),
-            mid_a=V((8, D), f32),
-            far_a=V((3, 8, D), f32),
+            vec_s=V((8, TILE), f32),
+            got_a=V((7, 8, TILE), f32),
+            mid_a=V((8, TILE), f32),
+            far_a=V((3, 8, TILE), f32),
             got_b=V((7, 8, D), f32),
             mid_b=V((8, D), f32),
             far_b=V((3, 8, D), f32),
@@ -1039,7 +1054,7 @@
     as_low = lambda values: jnp.asarray(values.astype(np.float32), bf16)
     return dict(
         member_h=as_low(member),
-        spread_h=as_low(np.ascontiguousarray(member.T)),
+        spread_h=as_low(np.ascontiguousarray(spread_matrix())),
         head_h=as_low(head_mask()),
         group_h=as_low(group_mask()),
         bias_h=jnp.asarray(block_bias()),

time: 132 us -> 119 us (0.902)
  Pallas kernels: 131 us -> 118 us
    pallas_call x1, Pallas kernels: 127 us -> 115 us  [run_layer(): pl.pallas_call(functools.partial(layer_kernel, fast, dict(operands, **out...]
where the time goes in v3:
time: 119 us
  Pallas kernels  118 us (99%)
  between operations  1.47 us (1%)
    pallas_call x1, Pallas kernels, run_layer(): pl.pallas_call(functools.partial(layer_kernel, fast, dict(operands, **out...  115 us
    pallas_call x1, Pallas kernels, finish_outputs(): pl.pallas_call(final_kernel, out_shape=outs, in_specs=[hbm] * 6, out_spec...  3.2 us

profile of v3, /device:TPU:0, one launch (start us, length us, event | category | flops | bytes accessed | tf_op | source)
XLA Modules:
  0.0 119.2 jit_solution(8713950727164363162)
XLA Ops:
  1.3 114.6 %shard_map.316 = (bf16[1024,512]{1,0:T(8,128)(2,1)}, bf16[1024,512]{1,0:T(8,128)(2,1)}, f32[16,1536]{1,0:T(8,128)}, f32[16,2560]{1,0:T(8,128)}, f32[64,512]{1,0:T(8,128)}, /*index=5*/f32[16,128]{1,0:T(8,128)}) custom-call(bf16[1024,512]{1,0:T(8,128)(2,1)} %refs_0_.1, bf16[1024,512]{1,0:T(8,128)(2,1)} %refs_1_.1, bf16[16,512]{1,0:T(8,128)(2,1)} %refs_2_.1, ...), custom_call_target="tpu_custom_call" | custom-call | tf_op jit(solution)/shard_map/pallas_call | solution.py:1084
  115.9 3.2 %shard_map.317 = (bf16[1024,512]{1,0:T(8,128)(2,1)}, bf16[1024,512]{1,0:T(8,128)(2,1)}, f32[16]{0:T(128)}, f32[16]{0:T(128)}, f32[16,512]{1,0:T(8,128)}, /*index...) custom-call(bf16[1024,512]{1,0:T(8,128)(2,1)} %get-tuple-element.21., ...), custom_call_target="tpu_custom_call" | custom-call | tf_op jit(solution)/shard_map/pallas_call | solution.py:1103

commit v4 on v3

--- a/solution.py
+++ b/solution.py
@@ -192,7 +192,8 @@
 
 class Total:
     def __init__(self, ref, lanes, part, p, sems, bufs):
-        self.ref, self.lanes, self.part, self.p, self.sems, self.bufs = ref, lanes, part, p, sems.at[part], bufs
+        self.ref, self.lanes, self.part, self.p, self.bufs = ref, lanes, part, p, bufs
+        self.sems, self.sent = sems[0].at[part], sems[1]
 
     def add(self, index, buf):
         at = index + (self.p.c, slice(None), self.lanes)
@@ -222,24 +223,28 @@
                 self.add((z, p.y, p.x), two_a[part, z])
                 self.add((2 + z, p.y, p.x), two_b[part, z])
             for k, z in enumerate(p.zs):
-                remote(at(z, p.y, p.x, p.c), far.at[part, k], sems.at[6], sems.at[3], p.by_z[k]).start()
+                remote(at(z, p.y, p.x, p.c), far.at[part, k], self.sent.at[2], sems.at[3], p.by_z[k]).start()
             return
         for src, buf, device in sends:
-            remote(src, buf.at[part], sems.at[(4, 5, 5)[step]], sems.at[step], device).start()
+            remote(src, buf.at[part], self.sent.at[(0, 1, 1)[step]], sems.at[step], device).start()
 
     def finish(self, out):
         p, sems, far, part = self.p, self.sems, self.bufs[5], self.part
         arrived(far.at[part], sems.at[3], p.by_core)
         total = self.ref[p.z, p.y, p.x, p.c, :, self.lanes].astype(f32)
         out[:, self.lanes] = functools.reduce(jnp.add, [far[part, k].astype(f32) for k in range(3)], total)
-        gone(self.bufs[0].at[part], sems.at[4], p.by_core)
-        gone(self.bufs[0].at[part, pl.ds(0, 3)], sems.at[5], p.by_core)
-        gone(far.at[part], sems.at[6], p.by_core)
+
+    def settle(self):
+        everything, far = self.bufs[0], self.bufs[5]
+        gone(everything, self.sent.at[0], self.p.by_core)
+        gone(everything.at[:, pl.ds(0, 3)], self.sent.at[1], self.p.by_core)
+        gone(far, self.sent.at[2], self.p.by_core)
 
 
 class TotalRows:
     def __init__(self, ref, part, p, sems, bufs):
-        self.ref, self.part, self.p, self.sems, self.bufs = ref, part, p, sems.at[part], bufs
+        self.ref, self.part, self.p, self.bufs = ref, part, p, bufs
+        self.sems, self.sent = sems[0].at[part], sems[1]
 
     def add(self, index, buf):
         at = (self.part,) + index
@@ -267,11 +272,11 @@
             self.add((p.y, p.x, p.c, high), two_b[part])
             return
         for src, buf, device in sends:
-            remote(src, buf.at[part], sems.at[(3, 4, 4)[step]], sems.at[step], device).start()
+            remote(src, buf.at[part], self.sent.at[(0, 1, 1)[step]], sems.at[step], device).start()
 
     def settle(self):
-        gone(self.bufs[0].at[self.part], self.sems.at[3], self.p.by_core)
-        gone(self.bufs[5], self.sems.at[4], self.p.by_core)
+        gone(self.bufs[0], self.sent.at[0], self.p.by_core)
+        gone(self.bufs[0].at[pl.ds(0, 3)], self.sent.at[1], self.p.by_core)
 
 
 class TotalVectors:
@@ -392,10 +397,9 @@
     if fast:
         taken(own_i, 8)
         taken(own_o, 9)
-    pump((2, 0))
     tok_in.wait()
     lax.fori_loop(0, SHORT // CHUNK, first_norm, 0)
-    pump((0, 1), (3, 0), (0, 2), (1, 1), (0, 3), (1, 2), (0, 4))
+    pump((0, 1), (0, 2), (1, 1), (2, 0), (0, 3), (1, 2), (3, 0), (0, 4), (2, 1))
     for copy in rest_in:
         copy.wait()
 
@@ -509,7 +513,7 @@
         first = lax.broadcasted_iota(jnp.int32, (1, GROUP), 1)
         stack[0:SHORT, lanes] = (made * jnp.where(first < TILE, 0.125, 1.0)).astype(bf16)
         key_like = first < 2 * TILE
-        pump_here([(2, 1), (4, 0)])
+        pump_here([(4, 0)])
         tops_acc[0:TILE, 0:GROUP] = jnp.zeros((TILE, GROUP), f32)
 
         def pool(step, carry):
@@ -541,11 +545,11 @@
                 tile = group * TOGETHER + one
                 tile_forward(tile, pair, jnp.where(tile < 8, 0, 1), tile_scale(tile))
             for when, what, events in (
-                (0, 1, [(1, 3)]),
-                (0, 2, [(2, 2), (3, 1)]),
+                (0, 1, [(1, 3), (2, 2)]),
+                (0, 2, [(3, 1)]),
                 (1, 2, [(2, 3), (3, 2), (4, 1)]),
                 (2, 2, [(2, 4)]),
-                (3, 1, [(3, 3), (4, 2)]),
+                (3, 0, [(3, 3), (4, 2)]),
             ):
                 pl.when((pair == when) & (group == what))(functools.partial(pump, *events))
             return carry
@@ -626,28 +630,23 @@
     bias_mix, gain_two = r.param[2:3, :], r.param[3:4, :]
     shift_two, bias_out = r.param[4:5, :], r.param[5:6, :]
     w_mix = rows_of(wi, 4 * D, D)
-    resid[...] = tn(mix_t[...], w_mix)
-
-    def second_norm(step, carry):
-        at = pl.ds(pl.multiple_of(step * CHUNK, CHUNK), CHUNK)
-        mid = tok[at, :].astype(f32) + resid[at, :] + bias_mix
+    halves = [slice(half * 512, (half + 1) * 512) for half in range(2)]
+    for at in halves:
+        mid = tok[at, :].astype(f32) + tn(mix_t[:, at], w_mix) + bias_mix
         resid[at, :] = mid
+        acc_out[at, :] = mid + bias_out
         normed, _ = normalize(mid)
         n_two[at, :] = (normed * gain_two + shift_two).astype(bf16)
-        return carry
-
-    lax.fori_loop(0, SHORT // CHUNK, second_norm, 0)
     pump((4, 4))
 
     hid, g_pre = grads.at[0:SHORT, 0:D], grads.at[0:SHORT, D : 2 * D]
-    acc_out[...] = jnp.zeros_like(acc_out)
     acc_two[...] = jnp.zeros_like(acc_two)
 
     def total_i(part):
-        return Total(di, lanes_at(part * 512, 512), part, p, r.si[0], r.si[1:])
+        return Total(di, lanes_at(part * 512, 512), part, p, r.si[0:2], r.si[2:])
 
     def total_o(part):
-        return TotalRows(do, part, p, r.so[0], r.so[1:7])
+        return TotalRows(do, part, p, r.so[0:2], r.so[2:8])
 
     def onward(total, *steps):
         if fast:
@@ -686,40 +685,26 @@
 
     lax.fori_loop(0, 4, feed, 0)
 
-    def middle(step, carry):
-        at = pl.ds(pl.multiple_of(step * CHUNK, CHUNK), CHUNK)
-        mid = resid[at, :]
-        n_two[at, :] = (mid + acc_out[at, :] + bias_out).astype(bf16)
-        normed, inverse = normalize(mid)
+    for at in halves:
+        n_two[at, :] = acc_out[at, :].astype(bf16)
+        normed, inverse = normalize(resid[at, :])
         g_two = acc_two[at, :]
         c = cot[at, :].astype(f32)
         g_mid = c + normalize_back(g_two * gain_two, normed, inverse)
         resid[at, :] = g_mid
         low = g_mid.astype(bf16)
         g_att[at, :] = low
-        vec_b[0:1, :] += jnp.sum(low.astype(f32), axis=0, keepdims=True)
-        vec_b[1:2, :] += jnp.sum(g_two * normed, axis=0, keepdims=True)
-        vec_b[2:3, :] += jnp.sum(g_two, axis=0, keepdims=True)
-        vec_b[3:4, :] += jnp.sum(c, axis=0, keepdims=True)
-        return carry
-
-    lax.fori_loop(0, SHORT // CHUNK, middle, 0)
+        for row, values in enumerate((low.astype(f32), g_two * normed, g_two, c)):
+            vec_b[row : row + 1, :] += jnp.sum(values, axis=0, keepdims=True)
+        g_mix[at, :] = nt(low, w_mix).astype(bf16)
+        turned = nt(w_mix, low).astype(bf16).astype(f32) * mix_t[:, at].astype(f32)
+        inner_s[:, at] = jnp.concatenate(
+            [jnp.sum(turned[h * HEAD : (h + 1) * HEAD], axis=0, keepdims=True) for h in range(HEADS)], axis=0
+        )
     out_copy = pltpu.make_async_copy(n_two, r.out, r.out_sem.at[0])
     out_copy.start()
     onward(total_i, (1, 3), (2, 2), (3, 1))
     onward(total_o, (1, 3), (2, 2), (3, 1))
-    g_mix[...] = nt(g_att[...], w_mix).astype(bf16)
-
-    def inner_sums(step, carry):
-        at = pl.ds(pl.multiple_of(step * 512, 512), 512)
-        turned = nt(w_mix, g_att[at, :]).astype(bf16).astype(f32) * mix_t[:, at].astype(f32)
-        inner_s[:, at] = jnp.concatenate(
-            [jnp.sum(turned[h * HEAD : (h + 1) * HEAD], axis=0, keepdims=True) for h in range(HEADS)], axis=0
-        )
-        return carry
-
-    lax.fori_loop(0, SHORT // 512, inner_sums, 0)
-
     made = nn(mix_t[...], g_att[...])
     di[:, :, :, :, :, 4 * D :] = made.astype(bf16).reshape(4, 2, 2, 2, 16, D)
     onward(total_i, (4, 0))
@@ -737,8 +722,6 @@
     tops_acc[0:TILE, :] = jnp.zeros((TILE, D), f32)
 
     def lift(step, carry):
-        pl.when(step == 2)(lambda: onward(total_i, (2, 3)))
-        pl.when(step == 3)(lambda: onward(total_o, (2, 3)))
         chunk = pl.ds(pl.multiple_of(step * CHUNK, CHUNK), CHUNK)
         to = chunk_rows(step)
         members = chunk_members(chunk)
@@ -769,6 +752,8 @@
         return carry
 
     lax.fori_loop(0, 2, lift_two, 0)
+    onward(total_i, (2, 3))
+    onward(total_o, (2, 3))
     every = pl.ds(0, SHORT)
     keep_h(pl.ds(FIRST[3], TILE), sums_of(3, every, member[256:384, :]))
     tops = [sums_of(4 + slot, every, member[384:512, :]) for slot in range(4)]
@@ -776,8 +761,6 @@
         pl.ds(FIRST[4], TILE),
         jnp.where(top_lane < 64, tops[0], jnp.where(top_lane < 96, tops[1], jnp.where(top_lane < 112, tops[2], tops[3]))),
     )
-    onward(total_i, (3, 2))
-    onward(total_o, (3, 2))
     for pair in range(PAIRS):
         weight[pair, :, 0:SHORT] = share[0, 2 * pair : 2 * pair + 2]
     weight[:, :, SHORT:STACK] = jnp.ones((PAIRS, 2, SHORT), f32)
@@ -802,7 +785,6 @@
 
     for pair in range(PAIRS):
         tile_backward(15, pair, steps_down)
-    onward(total_i, (4, 1))
     back_s, back_r = r.back_s, r.back_r
     spans = [(slice(k * GROUP + TILE, (k + 1) * GROUP), slice(k * 2 * TILE, (k + 1) * 2 * TILE)) for k in range(PAIRS)]
     tall = jnp.concatenate([grads[2016:2048, theirs] for theirs, _ in spans], axis=1).astype(f32)
@@ -817,9 +799,11 @@
     ]
     for copy in back_out:
         copy.start()
+    onward(total_i, (3, 2), (4, 1))
+    onward(total_o, (3, 2))
 
     def total_a(part):
-        return Total(da, lanes_at(part * GROUP, GROUP), part, p, r.sa[0], r.sa[1:])
+        return Total(da, lanes_at(part * GROUP, GROUP), part, p, r.sa[0:2], r.sa[2:])
 
     def far_grads():
         arrived(back_r, r.far_sem.at[2], p.by_core)
@@ -832,17 +816,17 @@
     def send_rows():
         onward(total_o, (3, 3))
         for k, z in enumerate(p.zs):
-            remote(do.at[z, p.y, p.x, p.c], r.so[6].at[k], r.so[7].at[1], r.so[7].at[0], p.by_z[k]).start()
+            remote(do.at[z, p.y, p.x, p.c], r.so[7].at[k], r.so[8].at[1], r.so[8].at[0], p.by_z[k]).start()
 
     def finish_feed():
         for part in range(5):
             total_i(part).finish(r.keep_i)
-        arrived(r.so[6], r.so[7].at[0], p.by_core)
+        arrived(r.so[7], r.so[8].at[0], p.by_core)
         total = do[p.z, p.y, p.x, p.c].astype(f32)
-        r.keep_o[...] = functools.reduce(jnp.add, [r.so[6][k].astype(f32) for k in range(3)], total)
-        gone(r.so[6], r.so[7].at[1], p.by_core)
-        for part in range(4):
-            total_o(part).settle()
+        r.keep_o[...] = functools.reduce(jnp.add, [r.so[7][k].astype(f32) for k in range(3)], total)
+        gone(r.so[7], r.so[8].at[1], p.by_core)
+        total_o(0).settle()
+        total_i(0).settle()
         for copy in kept[:2]:
             copy.start()
 
@@ -900,20 +884,19 @@
 
     lax.fori_loop(0, PAIRS, pair_backward, 0)
 
-    acc_two[...] = nt(stack[0:SHORT, :], wa[:, :, :, :, :, SMALL : SMALL + WIDTH].reshape(D, WIDTH))
-    onward(total_a, (3, 1), (1, 3), (2, 2))
-
-    def first_back(step, carry):
-        pl.when(step == 2)(lambda: onward(total_a, (3, 2), (2, 3)))
-        chunk = pl.ds(pl.multiple_of(step * CHUNK, CHUNK), CHUNK)
-        g_one = acc_two[chunk, :]
-        normed, inverse = normalize(tok[chunk, :].astype(f32))
+    w_qkv = lambda: wa[:, :, :, :, :, SMALL : SMALL + WIDTH].reshape(D, WIDTH)
+
+    def first_back(at, g_one):
+        normed, inverse = normalize(tok[at, :].astype(f32))
         vec_a[0:1, :] += jnp.sum(g_one * normed, axis=0, keepdims=True)
         vec_a[1:2, :] += jnp.sum(g_one, axis=0, keepdims=True)
-        g_att[chunk, :] = (resid[chunk, :] + normalize_back(g_one * gain_one, normed, inverse)).astype(bf16)
-        return carry
-
-    lax.fori_loop(0, SHORT // CHUNK, first_back, 0)
+        g_att[at, :] = (resid[at, :] + normalize_back(g_one * gain_one, normed, inverse)).astype(bf16)
+
+    acc_two[halves[0], :] = nt(stack[halves[0], :], w_qkv())
+    acc_two[halves[1], :] = nt(stack[halves[1], :], w_qkv())
+    first_back(halves[0], acc_two[halves[0], :])
+    onward(total_a, (3, 1), (2, 2))
+    first_back(halves[1], acc_two[halves[1], :])
     tok_copy = pltpu.make_async_copy(g_att, r.g_tok, r.out_sem.at[1])
     tok_copy.start()
     if fast:
@@ -922,8 +905,9 @@
                 at = row * 4 + part
                 r.vec_s[at : at + 1, :] = vec_a[row : row + 1, part * TILE : (part + 1) * TILE]
         late.begin()
+        onward(total_a, (1, 3), (3, 2), (2, 3))
+        late.second()
         onward(total_a, (3, 3))
-        late.second()
         for part in range(3):
             total_a(part).finish(r.keep_a)
         last = late.finish()
@@ -933,6 +917,7 @@
         r.keep_v[0:8] = short
         kept[3].start()
         total_a(3).finish(r.keep_a)
+        total_a(0).settle()
         kept[2].start()
         for copy in kept:
             copy.wait()
@@ -1016,7 +1001,7 @@
 
         def sums(parts, wide):
             shape = lambda *dims: V((parts,) + dims + (16, wide), bf16)
-            return [S((parts, 7)), shape(4, 2, 2), shape(2, 2), shape(2, 2), shape(2), shape(2), shape(3)]
+            return [S((parts, 4)), S((3,)), shape(4, 2, 2), shape(2, 2), shape(2, 2), shape(2), shape(2), shape(3)]
 
         rows = lambda *dims: V((4,) + dims + (D,), bf16)
         made.update(
@@ -1028,7 +1013,7 @@
             do=V(SLOTS + (64, D), bf16),
             g_sem=S((5, 7)),
             si=sums(5, D),
-            so=[S((4, 5)), rows(2, 2, 64), rows(2, 32), rows(2, 32), rows(32), rows(32), V((3, 64, D), bf16), S((2,))],
+            so=[S((4, 3)), S((2,)), rows(2, 2, 64), rows(2, 32), rows(2, 32), rows(32), rows(32), V((3, 64, D), bf16), S((2,))],
             sa=sums(4, GROUP),
             v_sem=S((2, 4)),
             vec_s=V((8, TILE), f32),

time: 119 us -> 117 us (0.983)
  Pallas kernels: 118 us -> 115 us
    pallas_call x1, Pallas kernels: 115 us -> 112 us  [run_layer(): pl.pallas_call(functools.partial(layer_kernel, fast, dict(operands, **out...]
where the time goes in v4:
time: 117 us; the launch traced here: 116 us
  Pallas kernels  115 us (98%)
  between operations  1.47 us (1%)
    pallas_call x1, Pallas kernels, run_layer(): pl.pallas_call(functools.partial(layer_kernel, fast, dict(operands, **out...  112 us
    pallas_call x1, Pallas kernels, finish_outputs(): pl.pallas_call(final_kernel, out_shape=outs, in_specs=[hbm] * 6, out_spec...  3.2 us

profile of v4, /device:TPU:0, one launch (start us, length us, event | category | flops | bytes accessed | tf_op | source)
XLA Modules:
  0.0 116.5 jit_solution(15150451902185241558)
XLA Ops:
  1.3 111.8 %shard_map.316 = (bf16[1024,512]{1,0:T(8,128)(2,1)}, bf16[1024,512]{1,0:T(8,128)(2,1)}, f32[16,1536]{1,0:T(8,128)}, f32[16,2560]{1,0:T(8,128)}, f32[64,512]{1,0:T(8,128)}, /*index=5*/f32[16,128]{1,0:T(8,128)}) custom-call(bf16[1024,512]{1,0:T(8,128)(2,1)} %refs_0_.1, bf16[1024,512]{1,0:T(8,128)(2,1)} %refs_1_.1, bf16[16,512]{1,0:T(8,128)(2,1)} %refs_2_.1, ...), custom_call_target="tpu_custom_call" | custom-call | tf_op jit(solution)/shard_map/pallas_call | solution.py:1069
  113.1 3.2 %shard_map.317 = (bf16[1024,512]{1,0:T(8,128)(2,1)}, bf16[1024,512]{1,0:T(8,128)(2,1)}, f32[16]{0:T(128)}, f32[16]{0:T(128)}, f32[16,512]{1,0:T(8,128)}, /*index...) custom-call(bf16[1024,512]{1,0:T(8,128)(2,1)} %get-tuple-element.21., ...), custom_call_target="tpu_custom_call" | custom-call | tf_op jit(solution)/shard_map/pallas_call | solution.py:1088

commit v5 on v4

--- a/solution.py
+++ b/solution.py
@@ -24,7 +24,6 @@
 SMALL = 128
 GROUP = 3 * TILE
 PAIRS = HEADS // 2
-FEED_STEPS = 2
 AXES = ("dp", "fsdp")
 MESH = pl.DeviceIdType.MESH
 SLOTS = (4, 2, 2, 2)
@@ -639,7 +638,8 @@
         n_two[at, :] = (normed * gain_two + shift_two).astype(bf16)
     pump((4, 4))
 
-    hid, g_pre = grads.at[0:SHORT, 0:D], grads.at[0:SHORT, D : 2 * D]
+    rows = (pl.ds(0, SHORT), pl.ds(SHORT, SHORT))
+    hid, g_pre = ([grads.at[at, pl.ds(lane, D)] for at in rows] for lane in (0, D))
     acc_two[...] = jnp.zeros_like(acc_two)
 
     def total_i(part):
@@ -656,34 +656,32 @@
                 else:
                     pl.when(part >= 0)(lambda: total(part).advance(step))
 
-    def feed(part, carry):
-        lanes = pl.ds(pl.multiple_of(part * 512, 512), 512)
+    def feed_grads(part):
+        lanes = pl.ds(part * 512, 512)
+        di[:, :, :, :, :, lanes] = tn(n_two[...], g_pre[part % 2][...]).astype(bf16).reshape(4, 2, 2, 2, 16, 512)
+        do[part] = tn(hid[part % 2][...], cot[...]).astype(bf16).reshape(2, 2, 2, 64, 512)
+        onward(total_i, (part, 0))
+        onward(total_o, (part, 0))
+
+    for part in range(4):
+        lanes = pl.ds(part * 512, 512)
         w_in = wi[:, :, :, :, :, lanes].reshape(512, 512)
         w_out = wo[part].reshape(512, 512)
-        b_in = r.bias_in[:, lanes]
-        sums = jnp.zeros((1, 512), f32)
-        for step in range(FEED_STEPS):
-            at = pl.ds(step * (SHORT // FEED_STEPS), SHORT // FEED_STEPS)
-            act, slope = gelu_both(nn(n_two[at, :], w_in) + b_in)
-            act = act.astype(bf16)
-            hid[at, :] = act
-            back = (nt(cot[at, :], w_out) * slope).astype(bf16)
-            g_pre[at, :] = back
-            acc_out[at, :] += nn(act, w_out)
-            acc_two[at, :] += nt(back, w_in)
-            sums = sums + jnp.sum(back.astype(f32), axis=0, keepdims=True)
-            if step == 0:
-                onward(total_i, (part - 3, 3), (part - 2, 2), (part - 1, 1))
-                onward(total_o, (part - 3, 3), (part - 2, 2), (part - 1, 1))
-        r.lanes_in[0:1, lanes] = sums
-        di[:, :, :, :, :, lanes] = tn(n_two[...], g_pre[...]).astype(bf16).reshape(4, 2, 2, 2, 16, 512)
-        do[part] = tn(hid[...], cot[...]).astype(bf16).reshape(2, 2, 2, 64, 512)
-        if fast:
-            onward(total_i, (part, 0))
-            onward(total_o, (part, 0))
-        return carry
-
-    lax.fori_loop(0, 4, feed, 0)
+        pre = nn(n_two[...], w_in) + r.bias_in[:, lanes]
+        back = nt(cot[...], w_out)
+        if part:
+            feed_grads(part - 1)
+        act, slope = gelu_both(pre)
+        act = act.astype(bf16)
+        back = (back * slope).astype(bf16)
+        hid[part % 2][...] = act
+        g_pre[part % 2][...] = back
+        r.lanes_in[0:1, lanes] = jnp.sum(back.astype(f32), axis=0, keepdims=True)
+        acc_out[...] += nn(act, w_out)
+        acc_two[...] += nt(back, w_in)
+        for total in (total_i, total_o):
+            onward(total, *[(part - k, k) for k in (3, 2, 1) if part >= k])
+    feed_grads(3)
 
     for at in halves:
         n_two[at, :] = acc_out[at, :].astype(bf16)
@@ -704,10 +702,10 @@
     out_copy = pltpu.make_async_copy(n_two, r.out, r.out_sem.at[0])
     out_copy.start()
     onward(total_i, (1, 3), (2, 2), (3, 1))
-    onward(total_o, (1, 3), (2, 2), (3, 1))
     made = nn(mix_t[...], g_att[...])
     di[:, :, :, :, :, 4 * D :] = made.astype(bf16).reshape(4, 2, 2, 2, 16, D)
     onward(total_i, (4, 0))
+    onward(total_o, (1, 3), (2, 2), (3, 1))
 
 
     def keep_h(lanes, values):

time: 117 us -> 115 us (0.983)
  Pallas kernels: 115 us -> 113 us
    pallas_call x1, Pallas kernels: 112 us -> 110 us  [run_layer(): pl.pallas_call(functools.partial(layer_kernel, fast, dict(operands, **out...]
where the time goes in v5:
time: 115 us
  Pallas kernels  113 us (98%)
  between operations  1.51 us (1%)
    pallas_call x1, Pallas kernels, run_layer(): pl.pallas_call(functools.partial(layer_kernel, fast, dict(operands, **out...  110 us
    pallas_call x1, Pallas kernels, finish_outputs(): pl.pallas_call(final_kernel, out_shape=outs, in_specs=[hbm] * 6, out_spec...  3.2 us

profile of v5, /device:TPU:0, one launch (start us, length us, event | category | flops | bytes accessed | tf_op | source)
XLA Modules:
  0.0 114.8 jit_solution(6529730133215440793)
XLA Ops:
  1.3 110.0 %shard_map.316 = (bf16[1024,512]{1,0:T(8,128)(2,1)}, bf16[1024,512]{1,0:T(8,128)(2,1)}, f32[16,1536]{1,0:T(8,128)}, f32[16,2560]{1,0:T(8,128)}, f32[64,512]{1,0:T(8,128)}, /*index=5*/f32[16,128]{1,0:T(8,128)}) custom-call(bf16[1024,512]{1,0:T(8,128)(2,1)} %refs_0_.1, bf16[1024,512]{1,0:T(8,128)(2,1)} %refs_1_.1, bf16[16,512]{1,0:T(8,128)(2,1)} %refs_2_.1, ...), custom_call_target="tpu_custom_call" | custom-call | tf_op jit(solution)/shard_map/pallas_call | solution.py:1067
  111.4 3.2 %shard_map.317 = (bf16[1024,512]{1,0:T(8,128)(2,1)}, bf16[1024,512]{1,0:T(8,128)(2,1)}, f32[16]{0:T(128)}, f32[16]{0:T(128)}, f32[16,512]{1,0:T(8,128)}, /*index...) custom-call(bf16[1024,512]{1,0:T(8,128)(2,1)} %get-tuple-element.21., ...), custom_call_target="tpu_custom_call" | custom-call | tf_op jit(solution)/shard_map/pallas_call | solution.py:1086

commit v6 on v5

--- a/solution.py
+++ b/solution.py
@@ -640,7 +640,6 @@
 
     rows = (pl.ds(0, SHORT), pl.ds(SHORT, SHORT))
     hid, g_pre = ([grads.at[at, pl.ds(lane, D)] for at in rows] for lane in (0, D))
-    acc_two[...] = jnp.zeros_like(acc_two)
 
     def total_i(part):
         return Total(di, lanes_at(part * 512, 512), part, p, r.si[0:2], r.si[2:])
@@ -678,7 +677,8 @@
         g_pre[part % 2][...] = back
         r.lanes_in[0:1, lanes] = jnp.sum(back.astype(f32), axis=0, keepdims=True)
         acc_out[...] += nn(act, w_out)
-        acc_two[...] += nt(back, w_in)
+        shares = nt(back, w_in)
+        acc_two[...] = acc_two[...] + shares if part else shares
         for total in (total_i, total_o):
             onward(total, *[(part - k, k) for k in (3, 2, 1) if part >= k])
     feed_grads(3)

time: 115 us -> 115 us (level)
  no operation moved by 1% of the time
where the time goes in v6:
time: 115 us
  Pallas kernels  113 us (98%)
  between operations  1.51 us (1%)
    pallas_call x1, Pallas kernels, run_layer(): pl.pallas_call(functools.partial(layer_kernel, fast, dict(operands, **out...  110 us
    pallas_call x1, Pallas kernels, finish_outputs(): pl.pallas_call(final_kernel, out_shape=outs, in_specs=[hbm] * 6, out_spec...  3.2 us

profile of v6, /device:TPU:0, one launch (start us, length us, event | category | flops | bytes accessed | tf_op | source)
XLA Modules:
  0.0 114.7 jit_solution(11273706119245884885)
XLA Ops:
  1.3 110.0 %shard_map.316 = (bf16[1024,512]{1,0:T(8,128)(2,1)}, bf16[1024,512]{1,0:T(8,128)(2,1)}, f32[16,1536]{1,0:T(8,128)}, f32[16,2560]{1,0:T(8,128)}, f32[64,512]{1,0:T(8,128)}, /*index=5*/f32[16,128]{1,0:T(8,128)}) custom-call(bf16[1024,512]{1,0:T(8,128)(2,1)} %refs_0_.1, bf16[1024,512]{1,0:T(8,128)(2,1)} %refs_1_.1, bf16[16,512]{1,0:T(8,128)(2,1)} %refs_2_.1, ...), custom_call_target="tpu_custom_call" | custom-call | tf_op jit(solution)/shard_map/pallas_call | solution.py:1067
  111.4 3.2 %shard_map.317 = (bf16[1024,512]{1,0:T(8,128)(2,1)}, bf16[1024,512]{1,0:T(8,128)(2,1)}, f32[16]{0:T(128)}, f32[16]{0:T(128)}, f32[16,512]{1,0:T(8,128)}, /*index...) custom-call(bf16[1024,512]{1,0:T(8,128)(2,1)} %get-tuple-element.21., ...), custom_call_target="tpu_custom_call" | custom-call | tf_op jit(solution)/shard_map/pallas_call | solution.py:1086
